TPU v7x, 32 devices: a whole 2x2x4 slice. The times are simulated.
32 devices in a mesh: rt: 4 (over x, core), ct: 8 (over z, y).
Axes of the slice: x: 2, y: 2, z: 4, core: 2. Of those that a mesh axis runs over, the one named last changes fastest.
Arguments:
- children: float32 [2048, 12288], P(('rt', 'ct')), may hold values from -6 to 6
- row_map: int32 [2048], replicated, may hold values from 0 to 2047, as said below
- column_map: int32 [2, 12288], replicated, may hold values from 0 to 16383, as said below
- staircase: int32 [2, 48], replicated, may hold values from 640 to 1024, as said below
Outputs:
- factor_rows: float32 [512, 16384], P(None, 'ct')
- basis: float32 [512, 2048], P(None, 'rt')
- remainder: float32 [2048, 16384], P('rt', 'ct')
Inputs may be any that keep to these rules, and one draw needn't show every extreme that they name: `row_map`: A permutation of the front rows. Of the 64 stacked child rows in each aligned block of 64 (the rows of one device), at most 32 have front rows in any one aligned block of 512 front rows, and every such block of child rows reaches 32 for some block of front rows. `column_map`: each row is strictly increasing, begins with 0, 1, ..., 511 and ends with 16383. `staircase`: each row is nondecreasing and ends with 1024.
All inputs are finite; a program needn't handle non-finite values.
Results may differ from a plain program's by a relative error of at most 0.0003.
Values sent between devices are 32-bit elements; how exact they have to be, the bound alone decides.
No kernel may reach another device: no remote copies, remote signals or barrier semaphores. Data moves between devices by JAX's collectives and lax.ppermute only.
A program may use at most 128 MiB of HBM per device.

v0:
```python
import jax
import jax.numpy as jnp
from jax import lax
from jax.sharding import PartitionSpec as P

FRONT_COLS = 16384
TILE = 256
ROWS_DEV = 512
PANEL = 512


highest = lax.Precision.HIGHEST


def from_root(value, axis, source):
    kept = jnp.where(lax.axis_index(axis) == source, value, 0).astype(value.dtype)
    return lax.psum(kept, axis)


def factor_panel(front_block, first_col, panel_width):
    panel_cols = lax.slice_in_dim(front_block, first_col, first_col + panel_width, axis=1)
    gram_matrix = lax.dot_general(
        panel_cols,
        panel_cols,
        (((0,), (0,)), ((), ())),
        precision=highest,
        preferred_element_type=jnp.float32,
    )
    gram_matrix = lax.psum(gram_matrix, "rt")
    lower_factor = jnp.linalg.cholesky(gram_matrix)
    basis_rows = jax.scipy.linalg.solve_triangular(lower_factor, panel_cols.T, lower=True)
    basis_rows = from_root(basis_rows, "ct", 0)
    partial_rows = jnp.dot(
        basis_rows, front_block, precision=highest, preferred_element_type=jnp.float32
    )
    factor = lax.psum(partial_rows, "rt")
    update = lax.dot_general(
        basis_rows,
        factor,
        (((0,), (0,)), ((), ())),
        precision=highest,
        preferred_element_type=jnp.float32,
    )
    return (front_block - update, basis_rows, factor)


def shards(children, row_map, column_map, staircase):
    tiles_down = lax.axis_size("rt")
    tiles_across = lax.axis_size("ct")
    source_rows = children.shape[0]
    child_cols = children.shape[1]
    total_rows = row_map.shape[0]
    child_rows = total_rows // 2
    sources = tiles_down * tiles_across
    capacity = 2 * source_rows // tiles_down
    block_cols = FRONT_COLS // tiles_across
    device_id = lax.axis_index("rt") * tiles_across + lax.axis_index("ct")
    first_row = device_id * source_rows
    which_child = first_row // child_rows
    within_child = first_row - which_child * child_rows + jnp.arange(source_rows, dtype=jnp.int32)
    target_tile = row_map // ROWS_DEV
    tile_ids = jnp.arange(tiles_down, dtype=jnp.int32)
    tile_hits = (
        target_tile.reshape(sources, source_rows)[:, :, None] == tile_ids[None, None, :]
    ).astype(jnp.int32)
    earlier = jnp.cumsum(tile_hits, axis=1) - tile_hits
    slot_of_row = jnp.sum(earlier * tile_hits, axis=2).reshape(-1)
    my_tiles = lax.dynamic_slice_in_dim(target_tile, first_row, source_rows)
    my_slots = lax.dynamic_slice_in_dim(slot_of_row, first_row, source_rows)
    slot_ids_all = jnp.arange(capacity, dtype=jnp.int32)
    matches = (my_tiles[None, None, :] == tile_ids[:, None, None]) & (
        my_slots[None, None, :] == slot_ids_all[None, :, None]
    )
    selection = matches.astype(jnp.float32)
    child_map = lax.dynamic_index_in_dim(column_map, which_child, 0, keepdims=False)
    child_stair = lax.dynamic_index_in_dim(staircase, which_child, 0, keepdims=False)
    limits = jnp.repeat(child_stair, TILE, total_repeat_length=child_cols)
    masked_rows = jnp.where(within_child[:, None] < limits[None, :], children, 0.0)
    column_slot = (
        jnp.zeros((FRONT_COLS,), jnp.int32)
        .at[child_map]
        .set(jnp.arange(child_cols, dtype=jnp.int32))
    )
    present = jnp.zeros((FRONT_COLS,), jnp.bool_).at[child_map].set(True)
    placed_cols = jnp.where(present[:, None], masked_rows.T[column_slot], 0.0)
    outgoing = lax.dot_general(
        selection,
        placed_cols,
        (((2,), (1,)), ((), ())),
        precision=highest,
        preferred_element_type=jnp.float32,
    )
    outgoing = outgoing.reshape(tiles_down, capacity, tiles_across, block_cols).transpose(
        0, 2, 1, 3
    )
    arrived = lax.all_to_all(
        outgoing.reshape(sources, capacity, block_cols),
        ("rt", "ct"),
        split_axis=0,
        concat_axis=0,
        tiled=True,
    )
    arrived = arrived.reshape(sources * capacity, block_cols)
    inverse = (
        jnp.zeros((total_rows,), jnp.int32).at[row_map].set(jnp.arange(total_rows, dtype=jnp.int32))
    )
    my_sources = lax.dynamic_slice_in_dim(inverse, lax.axis_index("rt") * ROWS_DEV, ROWS_DEV)
    slot_index = my_sources // source_rows * capacity + slot_of_row[my_sources]
    front_block = arrived[slot_index]
    front_block, basis_rows, factor_rows = factor_panel(front_block, 0, PANEL)
    return (factor_rows, basis_rows, front_block)


def solution(mesh):
    placed = (P(("rt", "ct"), None), P(), P(), P())
    return jax.shard_map(
        shards,
        mesh=mesh,
        in_specs=placed,
        out_specs=(P(None, "ct"), P(None, "rt"), P("rt", "ct")),
        check_vma=False,
    )
```

profile of v0, /device:TPU:0, one launch (start us, length us, event | category | flops | bytes accessed | tf_op | source)
XLA Modules:
  0.0 808.1 jit_solution(910246412102446716)
XLA Ops:
  16.4 45.4 %scatter_custom_fusion.1 = s32[16384]{0:T(1024)S(1)} fusion(s32[12288]{0:T(1024)S(1)} %bitcast.123, s32[12288]{0:T(1024)S(1)} %iota.103, s32[]{:T(128)} %copy.55), kind=kCustom, calls=%fused_computation.80 | custom fusion | bytes 65540 | tf_op jit(solution)/shard_map/scatter | solution.py:82
  65.1 31.2 %select_select_fusion.1 = s32[12288]{0:T(1024)S(1)} fusion(pred[12288]{0:T(1024)(128)(4,1)S(1)} %copy-done.5, pred[12288]{0:T(1024)(128)(4,1)S(1)} %copy-done.6, pred[12288]{0:T(1024)(128)(4,1)S(1)} %copy-done.7, pred[12288]{0:T(1024)(128)(4,1)S(1)} %copy-done.8, pred[12288]{0:T(1024)(128)(4,1)S(1)} %copy-done.9, pred[12288]{0:T(1024)(128)(4,1)S(1)} %copy-done.10, ...), kind=kLoop, calls=%fused_computation.79 | loop fusion | flops 577536 | bytes 626880 | tf_op jit(solution)/shard_map/jit(_take)/gather | solution.py:77
  96.3 9.8 %select_bitcast_fusion = f32[12288,64]{1,0:T(8,128)} fusion(f32[64,12288]{0,1:T(8,128)} %copy.26, s32[64]{0:T(128)S(1)} %iota_add_fusion, s32[12288]{0:T(1024)S(1)} %select_select_fusion.1), kind=kLoop, calls=%fused_computation.12 | loop fusion | flops 1572864 | bytes 6340864 | tf_op jit(solution)/shard_map/transpose | solution.py:85
  106.2 57.5 %gather_fusion = f32[16384,64]{1,0:T(8,128)} fusion(f32[12288,64]{1,0:T(8,128)} %select_bitcast_fusion, s32[16384]{0:T(1024)S(1)} %fusion.29), kind=kCustom, calls=%fused_computation | custom fusion | bytes 8454144 | tf_op jit(solution)/shard_map/gather | solution.py:85
  163.7 51.6 %scatter_custom_fusion = pred[16384]{0:T(1024)(128)(4,1)S(1)} fusion(s32[12288]{0:T(1024)S(1)} %bitcast.124, pred[12288]{0:T(1024)(128)(4,1)S(1)} %broadcast.466, pred[]{:T(512)} %constant.313.clone.1), kind=kCustom, calls=%fused_computation.82 | custom fusion | bytes 16385 | tf_op jit(solution)/shard_map/scatter | solution.py:84
  215.3 9.5 %fusion = f32[4,32,16384]{2,1,0:T(8,128)S(1)} fusion(f32[16384,64]{1,0:T(8,128)} %gather_fusion, pred[16384]{0:T(1024)(128)(4,1)S(1)} %scatter_custom_fusion, pred[32,64]{1,0:T(8,128)(4,1)S(1)} %iota_compare_fusion.5, pred[4,64]{1,0:T(4,128)(4,1)S(1)} %iota_compare_fusion.6), kind=kOutput, calls=%fused_computation.9 | convolution fusion | flops 1611669504 | bytes 12601600 | tf_op jit(solution)/shard_map/dot_general | solution.py:86
  236.0 12.2 %all-reduce.5.cloned.1.call-start = ((), (), s32[]{:S(2)}) async-start(), calls=%async_computation.1 | async-start | bytes 2097152 | tf_op jit(solution)/shard_map/psum | solution.py:29
  248.3 8.0 scatter_custom_fusion.2
  259.7 165.9 %all-to-all-done = f32[32,32,2048]{2,1,0:T(8,128)} async-done(((f32[32,32,2048]{2,1,0:T(8,128)}), f32[32,32,2048]{2,1,0:T(8,128)}, u32[]{:S(2)}, u32[]{:S(2)}) %all-to-all-start) | async-done | bytes 8388640 | tf_op jit(solution)/shard_map/all_to_all | solution.py:96
  425.6 8.8 %gather_fusion.2 = f32[512,2048]{1,0:T(8,128)} fusion(f32[1024,2048]{1,0:T(8,128)} %bitcast.54, s32[1024]{0:T(1024)S(1)} %pad_clamp_fusion), kind=kCustom, calls=%fused_computation.2 | custom fusion | bytes 8390656 | tf_op jit(solution)/shard_map/gather | solution.py:109
  439.5 32.4 %all-reduce.5.cloned.1.call-done = f32[512,512]{0,1:T(8,128)} async-done(((f32[512,512]{0,1:T(8,128)}), f32[512,512]{0,1:T(8,128)}) %all-reduce.5.cloned.1.call-update) | async-done | bytes 1048592 | tf_op jit(solution)/shard_map/psum | solution.py:29
  474.9 11.7 %cholesky.104 = f32[128,128]{1,0:T(8,128)S(1)} custom-call(f32[128,128]{1,0:T(8,128)S(1)} %cholesky.266), custom_call_target="Cholesky" | custom-call | tf_op jit(solution)/shard_map/jit(cholesky)/cholesky | solution.py:30
  486.8 9.8 %custom-call.31 = f32[1,128,128]{1,2,0:T(8,128)S(1)} custom-call(f32[1,128,128]{2,1,0:T(8,128)S(1)} %get-tuple-element.42), custom_call_target="InvertDiagBlocksLowerTriangular" | custom-call | tf_op jit(solution)/shard_map/jit(cholesky)/cholesky | solution.py:30
  497.3 11.7 %cholesky.217 = f32[128,128]{1,0:T(8,128)S(1)} custom-call(f32[128,128]{1,0:T(8,128)S(1)} %cholesky.270), custom_call_target="Cholesky" | custom-call | tf_op jit(solution)/shard_map/jit(cholesky)/cholesky | solution.py:30
  509.0 10.2 %custom-call.32 = f32[1,128,128]{1,2,0:T(8,128)S(1)} custom-call(f32[1,128,128]{2,1,0:T(8,128)S(1)} %get-tuple-element.39), custom_call_target="InvertDiagBlocksLowerTriangular" | custom-call | tf_op jit(solution)/shard_map/jit(cholesky)/cholesky | solution.py:30
  519.9 11.7 %cholesky.238 = f32[128,128]{1,0:T(8,128)S(1)} custom-call(f32[128,128]{1,0:T(8,128)S(1)} %cholesky.275), custom_call_target="Cholesky" | custom-call | tf_op jit(solution)/shard_map/jit(cholesky)/cholesky | solution.py:30
  532.3 9.8 %custom-call.33 = f32[1,128,128]{1,2,0:T(8,128)S(1)} custom-call(f32[1,128,128]{2,1,0:T(8,128)S(1)} %get-tuple-element.36), custom_call_target="InvertDiagBlocksLowerTriangular" | custom-call | tf_op jit(solution)/shard_map/jit(cholesky)/cholesky | solution.py:30
  542.7 11.7 %cholesky.255 = f32[128,128]{1,0:T(8,128)S(1)} custom-call(f32[128,128]{1,0:T(8,128)S(1)} %convolution_subtract_fusion.6), custom_call_target="Cholesky" | custom-call | tf_op jit(solution)/shard_map/jit(cholesky)/cholesky | solution.py:30
  558.7 10.4 %while.2 = (s32[]{:T(128)}, f32[512,512]{1,0:T(8,128)S(1)}, s32[4,2]{0,1:T(2,128)S(1)}, f32[4,128,128]{2,1,0:T(8,128)}, s32[]{:T(128)}) while((s32[]{:T(128)}, f32[512,512]{1,0:T(8,128)S(1)}, s32[4,2]{0,1:T(2,128)S(1)}, f32[4,128,128]{2,1,0:T(8,128)}, s32[]{:T(128)}) %tuple.81), condition=%wide.while_cond.1, body=%wide.while_body.1.sunk | while | flops 2 | bytes 132705 | solution.py:31
  569.1 40.1 %custom-call.34 = f32[4,128,128]{1,2,0:T(8,128)S(1)} custom-call(f32[4,128,128]{2,1,0:T(8,128)} %get-tuple-element.22), custom_call_target="InvertDiagBlocksLowerTriangular" | custom-call | tf_op jit(solution)/shard_map/jit(_solve_triangular)/triangular_solve | solution.py:31
  613.5 78.5 %all-reduce.7.cloned.1.call-done = f32[512,512]{1,0:T(8,128)} async-done(((f32[512,512]{1,0:T(8,128)}), f32[512,512]{1,0:T(8,128)}) %all-reduce.7.cloned.1.call-update) | async-done | bytes 1048592 | tf_op jit(solution)/shard_map/psum | solution.py:17
  692.0 10.3 %fusion.63 = f32[512,2048]{1,0:T(8,128)} fusion(f32[512,512]{1,0:T(8,128)} %all-reduce.7.cloned.1.call-done, f32[512,2048]{1,0:T(8,128)} %gather_fusion.2), kind=kOutput, calls=%fused_computation.131 | convolution fusion | flops 6442450944 | bytes 9437184 | tf_op jit(solution)/shard_map/dot_general | solution.py:33
  702.4 85.2 %all-reduce.9.cloned.1.call-done = f32[512,2048]{1,0:T(8,128)} async-done(((f32[512,2048]{1,0:T(8,128)}), f32[512,2048]{1,0:T(8,128)}) %all-reduce.9.cloned.1.call-update) | async-done | bytes 4194320 | tf_op jit(solution)/shard_map/psum | solution.py:36
  787.6 10.8 %convolution_subtract_fusion = f32[512,2048]{1,0:T(8,128)} fusion(f32[512,2048]{1,0:T(8,128)} %gather_fusion.2, f32[512,512]{1,0:T(8,128)S(1)} %copy-done.3, f32[512,2048]{1,0:T(8,128)} %all-reduce.9.cloned.1.call-done), kind=kOutput, calls=%fused_computation.15 | convolution fusion | flops 6443499520 | bytes 13631488 | tf_op jit(solution)/shard_map/dot_general | solution.py:37
  (170 shorter events, 56.6 us)
Async XLA Ops:
  10.0 54.7 %copy-start.5 = (pred[12288]{0:T(1024)(128)(4,1)S(1)}, pred[12288]{0:T(1024)(128)(4,1)}, u32[]{:S(2)}) copy-start(pred[12288]{0:T(1024)(128)(4,1)} %constant.397) | copy-start | bytes 36868
  10.0 54.7 %copy-start.6 = (pred[12288]{0:T(1024)(128)(4,1)S(1)}, pred[12288]{0:T(1024)(128)(4,1)}, u32[]{:S(2)}) copy-start(pred[12288]{0:T(1024)(128)(4,1)} %constant.398) | copy-start | bytes 36868
  10.0 54.7 %copy-start.7 = (pred[12288]{0:T(1024)(128)(4,1)S(1)}, pred[12288]{0:T(1024)(128)(4,1)}, u32[]{:S(2)}) copy-start(pred[12288]{0:T(1024)(128)(4,1)} %constant.399) | copy-start | bytes 36868
  10.0 54.7 %copy-start.8 = (pred[12288]{0:T(1024)(128)(4,1)S(1)}, pred[12288]{0:T(1024)(128)(4,1)}, u32[]{:S(2)}) copy-start(pred[12288]{0:T(1024)(128)(4,1)} %constant.400) | copy-start | bytes 36868
  10.1 54.7 %copy-start.9 = (pred[12288]{0:T(1024)(128)(4,1)S(1)}, pred[12288]{0:T(1024)(128)(4,1)}, u32[]{:S(2)}) copy-start(pred[12288]{0:T(1024)(128)(4,1)} %constant.401) | copy-start | bytes 36868
  10.1 54.7 %copy-start.10 = (pred[12288]{0:T(1024)(128)(4,1)S(1)}, pred[12288]{0:T(1024)(128)(4,1)}, u32[]{:S(2)}) copy-start(pred[12288]{0:T(1024)(128)(4,1)} %constant.402) | copy-start | bytes 36868
  10.1 54.7 %copy-start.11 = (pred[12288]{0:T(1024)(128)(4,1)S(1)}, pred[12288]{0:T(1024)(128)(4,1)}, u32[]{:S(2)}) copy-start(pred[12288]{0:T(1024)(128)(4,1)} %constant.403) | copy-start | bytes 36868
  10.1 54.7 %copy-start.12 = (pred[12288]{0:T(1024)(128)(4,1)S(1)}, pred[12288]{0:T(1024)(128)(4,1)}, u32[]{:S(2)}) copy-start(pred[12288]{0:T(1024)(128)(4,1)} %constant.404) | copy-start | bytes 36868
  10.1 54.7 %copy-start.13 = (pred[12288]{0:T(1024)(128)(4,1)S(1)}, pred[12288]{0:T(1024)(128)(4,1)}, u32[]{:S(2)}) copy-start(pred[12288]{0:T(1024)(128)(4,1)} %constant.405) | copy-start | bytes 36868
  10.1 54.7 %copy-start.14 = (pred[12288]{0:T(1024)(128)(4,1)S(1)}, pred[12288]{0:T(1024)(128)(4,1)}, u32[]{:S(2)}) copy-start(pred[12288]{0:T(1024)(128)(4,1)} %constant.406) | copy-start | bytes 36868
  10.1 54.7 %copy-start.15 = (pred[12288]{0:T(1024)(128)(4,1)S(1)}, pred[12288]{0:T(1024)(128)(4,1)}, u32[]{:S(2)}) copy-start(pred[12288]{0:T(1024)(128)(4,1)} %constant.407) | copy-start | bytes 36868
  10.2 54.7 %copy-start.16 = (pred[12288]{0:T(1024)(128)(4,1)S(1)}, pred[12288]{0:T(1024)(128)(4,1)}, u32[]{:S(2)}) copy-start(pred[12288]{0:T(1024)(128)(4,1)} %constant.408) | copy-start | bytes 36868
  10.2 54.7 %copy-start.17 = (pred[12288]{0:T(1024)(128)(4,1)S(1)}, pred[12288]{0:T(1024)(128)(4,1)}, u32[]{:S(2)}) copy-start(pred[12288]{0:T(1024)(128)(4,1)} %constant.409) | copy-start | bytes 36868
  10.2 54.7 %copy-start.18 = (pred[12288]{0:T(1024)(128)(4,1)S(1)}, pred[12288]{0:T(1024)(128)(4,1)}, u32[]{:S(2)}) copy-start(pred[12288]{0:T(1024)(128)(4,1)} %constant.410) | copy-start | bytes 36868
  10.2 54.7 %copy-start.19 = (pred[12288]{0:T(1024)(128)(4,1)S(1)}, pred[12288]{0:T(1024)(128)(4,1)}, u32[]{:S(2)}) copy-start(pred[12288]{0:T(1024)(128)(4,1)} %constant.411) | copy-start | bytes 36868
  10.2 54.7 %copy-start.20 = (pred[12288]{0:T(1024)(128)(4,1)S(1)}, pred[12288]{0:T(1024)(128)(4,1)}, u32[]{:S(2)}) copy-start(pred[12288]{0:T(1024)(128)(4,1)} %constant.412) | copy-start | bytes 36868
  10.2 54.7 %copy-start.21 = (pred[12288]{0:T(1024)(128)(4,1)S(1)}, pred[12288]{0:T(1024)(128)(4,1)}, u32[]{:S(2)}) copy-start(pred[12288]{0:T(1024)(128)(4,1)} %constant.413) | copy-start | bytes 36868
  10.2 54.7 %copy-start.22 = (pred[12288]{0:T(1024)(128)(4,1)S(1)}, pred[12288]{0:T(1024)(128)(4,1)}, u32[]{:S(2)}) copy-start(pred[12288]{0:T(1024)(128)(4,1)} %constant.414) | copy-start | bytes 36868
  10.2 54.7 %copy-start.23 = (pred[12288]{0:T(1024)(128)(4,1)S(1)}, pred[12288]{0:T(1024)(128)(4,1)}, u32[]{:S(2)}) copy-start(pred[12288]{0:T(1024)(128)(4,1)} %constant.415) | copy-start | bytes 36868
  228.6 197.0 %all-to-all-start = ((f32[32,32,2048]{2,1,0:T(8,128)}), f32[32,32,2048]{2,1,0:T(8,128)}, u32[]{:S(2)}, u32[]{:S(2)}) async-start(f32[32,32,2048]{2,1,0:T(8,128)} %bitcast.118), calls=%async_computation | async-start | bytes 16777216 | tf_op jit(solution)/shard_map/all_to_all | solution.py:96
  236.0 235.8 %all-reduce.5.cloned.1.call-start = ((), (), s32[]{:S(2)}) async-start(), calls=%async_computation.1 | async-start | bytes 2097152 | tf_op jit(solution)/shard_map/psum | solution.py:29
  439.1 252.9 %all-reduce.7.cloned.1.call-start = ((), (), s32[]{:S(2)}) async-start(), calls=%async_computation.2 | async-start | bytes 2097152 | tf_op jit(solution)/shard_map/psum | solution.py:17
  613.5 174.1 %all-reduce.9.cloned.1.call-start = ((), (), s32[]{:S(2)}) async-start(), calls=%async_computation.3 | async-start | bytes 8388608 | tf_op jit(solution)/shard_map/psum | solution.py:36
  702.3 85.3 %copy-start.3 = (f32[512,512]{1,0:T(8,128)S(1)}, f32[512,512]{1,0:T(8,128)}, u32[]{:S(2)}) copy-start(f32[512,512]{1,0:T(8,128)} %all-reduce.7.cloned.1.call-done) | copy-start | bytes 3145732
  (25 other events, 1129.5 us)
Sparse Core Ops, SparseCore 0:
  439.2 32.6 all-reduce.4
  613.6 78.3 all-reduce.6
  702.5 85.0 all-reduce.8
where the time goes:
time: 818 us; the launch traced here: 808 us
  waiting for transfers between devices  362 us (44%)
  local copies, waits for them, and re-layouts  203 us (25%)
  other arithmetic  166 us (20%)
  matrix products  40.3 us (5%)
  starting transfers between devices  19.7 us (2%)
  between operations  17.5 us (2%)
    all_to_all x1, waiting for transfers between devices, shards(): lax.all_to_all(outgoing.reshape(sources, capacity, block_cols), ('rt', 'c...  166 us
    psum x1, waiting for transfers between devices, factor_panel(): factor = lax.psum(partial_rows, 'rt')  85.2 us
    another operation x14, other arithmetic, factor_panel(): lower_factor = jnp.linalg.cholesky(gram_matrix)  79 us
    psum x1, waiting for transfers between devices, from_root(): return lax.psum(kept, axis)  78.5 us
    gather x1, local copies, waits for them, and re-layouts, shards(): placed_cols = jnp.where(present[:, None], masked_rows.T[column_slot], 0.0)  57.5 us
    scatter x1, local copies, waits for them, and re-layouts, shards(): present = jnp.zeros((FRONT_COLS,), jnp.bool_).at[child_map].set(True)  51.6 us
    scatter x1, local copies, waits for them, and re-layouts, shards(): column_slot = jnp.zeros((FRONT_COLS,), jnp.int32).at[child_map].set(jnp.a...  45.4 us
    another operation x3, other arithmetic, factor_panel(): jax.scipy.linalg.solve_triangular(lower_factor, panel_cols.T, lower=True)  40.3 us
  transfers between devices with their start and end apart: 4, of which 4 were waited for; matrix products, arithmetic and copies ran while one was open for 1% of the time, Pallas kernels for 0%

commit v1 on v0

v1 whole, which is shorter than its diff:
```python
import functools

import jax
import jax.numpy as jnp
import numpy as np
from jax import lax
from jax.experimental import pallas as pl
from jax.experimental.pallas import tpu as pltpu
from jax.sharding import PartitionSpec as P

FRONT_COLS = 16384
PANEL = 512
STEP = 256
LANES = 128
NB = 128
SUB = 8

HI = lax.Precision.HIGHEST
F32 = jnp.float32
BF16 = jnp.bfloat16
MIB = 2**20


def swap(x, rt_bit, ct_bit):
    n_rt, n_ct = lax.axis_size("rt"), lax.axis_size("ct")
    if not rt_bit:
        return lax.ppermute(x, "ct", [(c, c ^ ct_bit) for c in range(n_ct)])
    if not ct_bit:
        return lax.ppermute(x, "rt", [(r, r ^ rt_bit) for r in range(n_rt)])
    pairs = [
        (r * n_ct + c, (r ^ rt_bit) * n_ct + (c ^ ct_bit)) for r in range(n_rt) for c in range(n_ct)
    ]
    return lax.ppermute(x, ("rt", "ct"), pairs)


def bits_down(size, last):
    bit, bits = size // 2, []
    while bit >= last:
        bits.append(bit)
        bit //= 2
    return bits


def combos(bits):
    order = [0]
    for bit in bits:
        order = order + [value ^ bit for value in order]
    return order


def halves(x):
    high = x.astype(BF16)
    return high, (x - high.astype(F32)).astype(BF16)


def dot(a, b):
    return jnp.dot(a, b, preferred_element_type=F32)


def dot_nt(a, b, precision=None):
    return lax.dot_general(
        a, b, (((1,), (1,)), ((), ())), precision=precision, preferred_element_type=F32
    )


def dot_tn(a, b, precision=None):
    return lax.dot_general(
        a, b, (((0,), (0,)), ((), ())), precision=precision, preferred_element_type=F32
    )


def params(mib):
    return pltpu.CompilerParams(vmem_limit_bytes=mib * MIB)


def widen_kernel(tiles, window, info, child, cmap, limits, *outs):
    rows = child.shape[0]
    my_block = info[info.shape[0] - 2]
    first_row = info[info.shape[0] - 1]
    row_ids = first_row + lax.broadcasted_iota(jnp.int32, (rows, window), 0)
    col_ids = lax.broadcasted_iota(jnp.int32, (STEP, window), 0)
    for place, out in enumerate(outs):
        block = my_block ^ place

        def tile(i, carry, block=block, out=out):
            t = block * tiles + i
            cols = pl.ds(pl.multiple_of(info[t] * LANES, LANES), window)
            live = jnp.where(row_ids < limits[:, cols], child[:, cols], 0.0)
            hot = jnp.where(col_ids + t * STEP == cmap[:, cols], 1.0, 0.0).astype(BF16)
            high = live.astype(BF16)
            rest = live - high.astype(F32)
            mid = rest.astype(BF16)
            low = (rest - mid.astype(F32)).astype(BF16)
            spread = dot_nt(jnp.concatenate([high, mid, low], axis=0), hot)
            out[:, pl.ds(pl.multiple_of(i * STEP, STEP), STEP)] = (
                spread[:rows] + spread[rows : 2 * rows] + spread[2 * rows :]
            )
            return carry

        lax.fori_loop(0, tiles, tile, 0)


def widen(info, child, cmap, limits, n_ct):
    rows, width = child.shape
    block_cols = FRONT_COLS // n_ct
    window = STEP + LANES
    whole = pl.BlockSpec(memory_space=pltpu.VMEM)
    return pl.pallas_call(
        functools.partial(widen_kernel, block_cols // STEP, window),
        out_shape=[jax.ShapeDtypeStruct((rows, block_cols), F32)] * n_ct,
        in_specs=[pl.BlockSpec(memory_space=pltpu.SMEM), whole, whole, whole],
        out_specs=[whole] * n_ct,
        compiler_params=params(24),
        cost_estimate=pl.CostEstimate(
            flops=6 * rows * window * FRONT_COLS,
            bytes_accessed=4 * rows * (width + FRONT_COLS),
            transcendentals=0,
        ),
    )(info, child, cmap, limits)


def small_inverse(tile):
    a = [
        [jnp.broadcast_to(tile[i : i + 1, k : k + 1], (SUB, NB)) for k in range(i + 1)]
        for i in range(SUB)
    ]
    scale = [None] * SUB
    lower = [[None] * SUB for _ in range(SUB)]
    inverse = [[None] * SUB for _ in range(SUB)]
    for j in range(SUB):
        scale[j] = lax.rsqrt(a[j][j])
        for i in range(j + 1, SUB):
            lower[i][j] = a[i][j] * scale[j]
        for i in range(j + 1, SUB):
            for k in range(j + 1, i + 1):
                a[i][k] = a[i][k] - lower[i][j] * lower[k][j]
    for j in range(SUB):
        inverse[j][j] = scale[j]
        for i in range(j + 1, SUB):
            total = lower[i][j] * inverse[j][j]
            for k in range(j + 1, i):
                total = total + lower[i][k] * inverse[k][j]
            inverse[i][j] = -scale[i] * total
    return inverse


def apply_small(inverse, tiles):
    sub = lax.broadcasted_iota(jnp.int32, (SUB, NB), 0)
    outs = [None] * len(tiles)
    for k in range(SUB):
        column = jnp.zeros((SUB, NB), F32)
        for i in range(k, SUB):
            column = jnp.where(sub == i, inverse[i][k], column)
        for n, tile in enumerate(tiles):
            term = column * jnp.broadcast_to(tile[k : k + 1, :], (SUB, NB))
            outs[n] = term if outs[n] is None else outs[n] + term
    return outs


def identity(n):
    shape = (n, n)
    same = lax.broadcasted_iota(jnp.int32, shape, 0) == lax.broadcasted_iota(jnp.int32, shape, 1)
    return jnp.where(same, 1.0, 0.0)


def diagonal_inverse(block, out):
    lane = lax.broadcasted_iota(jnp.int32, (SUB, NB), 1)

    def body(s, carry):
        work, right = carry
        inverse = small_inverse(work[:SUB])
        top, top_right = apply_small(inverse, [work[:SUB], right[:SUB]])
        out[pl.ds(pl.multiple_of(SUB * s, SUB), SUB), :] = top_right
        top = jnp.where(lane < NB - SUB * s, top, 0.0)
        change = dot_tn(top, jnp.concatenate([top, top_right], axis=1), HI)
        work = work - change[:, :NB]
        right = right - change[:, NB:]
        work = pltpu.roll(jnp.concatenate([work[SUB:], work[:SUB]], axis=0), NB - SUB, 1)
        right = jnp.concatenate([right[SUB:], right[:SUB]], axis=0)
        return work, right

    lax.fori_loop(0, NB // SUB, body, (block, identity(NB)))


def factor_kernel(gram_a, gram_b, out, work, small):
    n = gram_a.shape[0]
    work[:, :n] = gram_a[...] + gram_b[...]
    work[:, n:] = identity(n)
    for lo in range(0, n, NB):
        hi = lo + NB
        diagonal_inverse(work[lo:hi, lo:hi], small)
        rows = jnp.dot(small[...], work[lo:hi, lo : n + hi], precision=HI, preferred_element_type=F32)
        out[lo:hi, :hi] = rows[:, n - lo :]
        if hi < n:
            out[lo:hi, hi:] = jnp.zeros((NB, n - hi), F32)
            work[hi:, hi : n + hi] -= dot_tn(rows[:, NB : n - lo], rows[:, NB:], HI)


def inverse_factor(gram_a, gram_b):
    n = gram_a.shape[0]
    return pl.pallas_call(
        factor_kernel,
        out_shape=jax.ShapeDtypeStruct((n, n), F32),
        scratch_shapes=[pltpu.VMEM((n, 2 * n), F32), pltpu.VMEM((NB, NB), F32)],
        compiler_params=params(24),
        cost_estimate=pl.CostEstimate(
            flops=40 * 10**9, bytes_accessed=12 * n * n, transcendentals=0
        ),
    )(gram_a, gram_b)


def basis_kernel(inverse, own, other, targets, q_high, q_low, basis, turned_high, turned_low):
    d = pl.program_id(0)
    group, panel = targets.shape[-1], inverse.shape[0]
    rows = jnp.concatenate(
        [own[...].reshape(group // 2, panel), other[...].reshape(group // 2, panel)], axis=0
    )
    inv_high, inv_low = halves(inverse[...])
    high, low = halves(rows)
    q = dot_nt(inv_high, high) + (dot_nt(inv_low, high) + dot_nt(inv_high, low))
    q_h, q_l = halves(q)
    q_high[...] = q_h
    q_low[...] = q_l
    front = basis.shape[1]
    ids = lax.broadcasted_iota(jnp.int32, (front, group), 0)
    hot = jnp.where(ids == targets[0], 1.0, 0.0).astype(BF16)
    part = dot_nt(q_h, hot) + dot_nt(q_l, hot)

    @pl.when(d == 0)
    def _():
        basis[...] = part

    @pl.when(d > 0)
    def _():
        basis[...] += part

    @pl.when(d == pl.num_programs(0) - 1)
    def _():
        turned_h, turned_l = halves(basis[...].T)
        turned_high[...] = turned_h
        turned_low[...] = turned_l


def basis_rows(inverse, own, other, targets, front_rows):
    half, n_ct, src, panel = own.shape
    group = 2 * half * src
    depth = n_ct.bit_length() - 1

    def place(d):
        return (0, sum(((d >> k) & 1) << (depth - 1 - k) for k in range(depth)), 0, 0)

    wide = jax.ShapeDtypeStruct((panel, n_ct * group), BF16)
    return pl.pallas_call(
        basis_kernel,
        grid=(n_ct,),
        out_shape=[
            wide,
            wide,
            jax.ShapeDtypeStruct((panel, front_rows), F32),
            jax.ShapeDtypeStruct((front_rows, panel), BF16),
            jax.ShapeDtypeStruct((front_rows, panel), BF16),
        ],
        in_specs=[
            pl.BlockSpec((panel, panel), lambda d: (0, 0)),
            pl.BlockSpec((half, 1, src, panel), place),
            pl.BlockSpec((half, 1, src, panel), place),
            pl.BlockSpec((1, 1, group), lambda d: (d, 0, 0)),
        ],
        out_specs=[
            pl.BlockSpec((panel, group), lambda d: (0, d)),
            pl.BlockSpec((panel, group), lambda d: (0, d)),
            pl.BlockSpec((panel, front_rows), lambda d: (0, 0)),
            pl.BlockSpec((front_rows, panel), lambda d: (0, 0)),
            pl.BlockSpec((front_rows, panel), lambda d: (0, 0)),
        ],
        compiler_params=params(24),
        cost_estimate=pl.CostEstimate(
            flops=10 * panel * panel * n_ct * group, bytes_accessed=12 * MIB, transcendentals=0
        ),
    )(inverse, own, other, targets)


def mix(q_high, q_low, hot, pieces):
    rows = jnp.concatenate([piece[...] for piece in pieces], axis=0)
    high, low = halves(rows)
    factor = dot(q_high[...], high) + (dot(q_low[...], high) + dot(q_high[...], low))
    return factor, dot(hot[...], high) + dot(hot[...], low)


def build_hot(targets, hot):
    @pl.when(pl.program_id(0) == 0)
    def _():
        ids = lax.broadcasted_iota(jnp.int32, hot.shape, 0)
        hot[...] = jnp.where(ids == targets[...], 1.0, 0.0).astype(BF16)


def first_kernel(count, q_high, q_low, targets, *refs):
    pieces, (factor, placed, hot) = refs[:count], refs[count:]
    build_hot(targets, hot)
    factor[...], placed[...] = mix(q_high, q_low, hot, pieces)


def more_kernel(count, q_high, q_low, targets, factor_in, placed_in, *refs):
    pieces, (factor, placed, hot) = refs[:count], refs[count:]
    build_hot(targets, hot)
    add_factor, add_placed = mix(q_high, q_low, hot, pieces)
    factor[...] = factor_in[...] + add_factor
    placed[...] = placed_in[...] + add_placed


def last_kernel(count, q_high, q_low, targets, factor_in, placed_in, turned_high, turned_low, *refs):
    pieces, (factor, remainder, hot) = refs[:count], refs[count:]
    build_hot(targets, hot)
    add_factor, add_placed = mix(q_high, q_low, hot, pieces)
    total = factor_in[...] + add_factor
    factor[...] = total
    high, low = halves(total)
    removed = dot(turned_high[...], high) + (dot(turned_low[...], high) + dot(turned_high[...], low))
    remainder[...] = (placed_in[...] + add_placed) - removed


def mix_call(kernel, q_high, q_low, targets, group, extra, turned, pieces, front_rows):
    panel = q_high.shape[0]
    src, block_cols = pieces[0].shape
    depth = len(pieces) * src
    column = lambda j: (0, j)
    fixed = lambda j: (0, group)
    still = lambda j: (0, 0)
    flops = 2 * depth * block_cols * (3 * panel + 2 * front_rows)
    flops += 6 * panel * front_rows * block_cols if turned else 0
    return pl.pallas_call(
        functools.partial(kernel, len(pieces)),
        grid=(block_cols // STEP,),
        out_shape=[
            jax.ShapeDtypeStruct((panel, block_cols), F32),
            jax.ShapeDtypeStruct((front_rows, block_cols), F32),
        ],
        in_specs=[
            pl.BlockSpec((panel, depth), fixed),
            pl.BlockSpec((panel, depth), fixed),
            pl.BlockSpec((1, depth), fixed),
        ]
        + [pl.BlockSpec((x.shape[0], STEP), column) for x in extra]
        + [pl.BlockSpec(x.shape, still) for x in turned]
        + [pl.BlockSpec((src, STEP), column) for _ in pieces],
        out_specs=[
            pl.BlockSpec((panel, STEP), column),
            pl.BlockSpec((front_rows, STEP), column),
        ],
        scratch_shapes=[pltpu.VMEM((front_rows, depth), BF16)],
        compiler_params=params(32),
        cost_estimate=pl.CostEstimate(
            flops=flops,
            bytes_accessed=4 * block_cols * (depth + (1 + bool(extra)) * (panel + front_rows)),
            transcendentals=0,
        ),
    )(q_high, q_low, targets, *extra, *turned, *pieces)


def shards(children, row_map, column_map, staircase):
    n_rt, n_ct = lax.axis_size("rt"), lax.axis_size("ct")
    my_rt, my_ct = lax.axis_index("rt"), lax.axis_index("ct")
    src, child_cols = children.shape
    total_rows = row_map.shape[0]
    child_rows = total_rows // 2
    front_rows = total_rows // n_rt
    tile_cols = child_cols // staircase.shape[1]
    n_dev = n_rt * n_ct

    first_row = (my_rt * n_ct + my_ct) * src
    which = first_row // child_rows
    first_within = first_row - which * child_rows
    cmap = lax.dynamic_index_in_dim(column_map, which, 0, keepdims=False)
    stairs = lax.dynamic_index_in_dim(staircase, which, 0, keepdims=False)
    limits = jnp.broadcast_to(stairs[:, None], (stairs.shape[0], tile_cols)).reshape(-1)

    within = first_within + jnp.arange(src, dtype=jnp.int32)
    panel = jnp.where(within[:, None] < limits[None, :PANEL], children[:, :PANEL], 0.0)
    ct_bits, rt_bits = bits_down(n_ct, 1), bits_down(n_rt, 2)
    for bit in ct_bits:
        panel = jnp.concatenate([panel, swap(panel, 0, bit)], axis=0)
    for bit in rt_bits:
        panel = jnp.concatenate([panel, swap(panel, bit, 0)], axis=0)
    gram = dot_tn(panel, panel, HI)
    other_gram = swap(gram, 1, 0)
    other_panel = swap(panel, 1, 0)

    rt_order = combos(rt_bits)
    rt_order = rt_order + [r ^ 1 for r in rt_order]
    sources = (my_rt ^ np.array(rt_order, np.int32))[None, :] * n_ct + (
        my_ct ^ np.arange(n_ct, dtype=np.int32)
    )[:, None]
    targets = row_map.reshape(n_dev, src)[sources.reshape(-1)] - my_rt * front_rows
    targets = targets.reshape(n_ct, 1, n_rt * src)
    flat_targets = targets.reshape(1, total_rows)

    edges = STEP * jnp.arange(FRONT_COLS // STEP, dtype=jnp.int32)
    starts = jnp.sum((cmap[None, :] < edges[:, None]).astype(jnp.int32), axis=1)
    starts = jnp.minimum(starts // LANES, (child_cols - STEP - LANES) // LANES)
    info = jnp.concatenate([starts, my_ct[None], first_within[None]]).astype(jnp.int32)
    blocks = widen(info, children, cmap[None, :], limits[None, :], n_ct)

    pieces = [None] * n_ct
    for d in list(range(n_ct // 2, n_ct)) + list(range(n_ct // 2)):
        mine = [swap(blocks[d], 0, d) if d else blocks[0]]
        for bit in rt_bits + [1]:
            mine = mine + [swap(x, bit, 0) for x in mine]
        pieces[d] = mine

    inverse = inverse_factor(gram, other_gram)
    half = n_rt // 2
    q_high, q_low, basis, turned_high, turned_low = basis_rows(
        inverse,
        panel.reshape(half, n_ct, src, PANEL),
        other_panel.reshape(half, n_ct, src, PANEL),
        targets,
        front_rows,
    )
    call = functools.partial(mix_call, front_rows=front_rows)
    two, four = n_ct // 2, n_ct // 4
    gather = lambda lo, hi: [x for d in range(lo, hi) for x in pieces[d]]
    state = call(first_kernel, q_high, q_low, flat_targets, 0, (), (), gather(0, two))
    state = call(more_kernel, q_high, q_low, flat_targets, 2, tuple(state), (), gather(two, two + four))
    factor, remainder = call(
        last_kernel,
        q_high,
        q_low,
        flat_targets,
        3,
        tuple(state),
        (turned_high, turned_low),
        gather(two + four, n_ct),
    )
    return factor, basis, remainder


def solution(mesh):
    placed = (P(("rt", "ct"), None), P(), P(), P())
    return jax.shard_map(
        shards,
        mesh=mesh,
        in_specs=placed,
        out_specs=(P(None, "ct"), P(None, "rt"), P("rt", "ct")),
        check_vma=False,
    )
```

time: 818 us -> 304 us (0.37)
  waiting for transfers between devices: 362 us -> 133 us
  local copies, waits for them, and re-layouts: 203 us -> 16.5 us
  other arithmetic: 166 us -> 1.87 us
  Pallas kernels: 0 us -> 114 us
  matrix products: 40.3 us -> 3.52 us
  between operations: 17.5 us -> 1.18 us
  starting transfers between devices: 19.7 us -> 30.2 us
    psum x3 -> x0, waiting for transfers between devices: 196 us -> none  [the longest x1 85.2 us: factor_panel(): factor = lax.psum(partial_rows, 'rt')]
    all_to_all x1 -> x0, waiting for transfers between devices: 166 us -> none  [shards(): lax.all_to_all(outgoing.reshape(sources, capacity, block_cols), ('rt', 'c...]
    ppermute x0 -> x37, waiting for transfers between devices: none -> 133 us  [the longest x10 80.5 us: swap(): return lax.ppermute(x, 'ct', [(c, c ^ ct_bit) for c in range(n_ct)])]
    another operation x18 -> x0, other arithmetic: 121 us -> none  [the longest x14 79 us: factor_panel(): lower_factor = jnp.linalg.cholesky(gram_matrix)]
    pallas_call x0 -> x6, Pallas kernels: none -> 114 us  [the longest x3 42.5 us: mix_call(): pl.pallas_call(functools.partial(kernel, len(pieces)), grid=(block_cols /...]
    scatter x3 -> x0, local copies, waits for them, and re-layouts: 105 us -> none  [the longest x1 51.6 us: shards(): present = jnp.zeros((FRONT_COLS,), jnp.bool_).at[child_map].set(True)]
    gather x6 -> x1, local copies, waits for them, and re-layouts: 71.6 us -> 0.57 us  [shards(): row_map.reshape(n_dev, src)[sources.reshape(-1)] - my_rt * front_rows]
    dot_general x4 -> x1, matrix products: 35.3 us -> 3.52 us  [dot_tn(): lax.dot_general(a, b, (((0,), (0,)), ((), ())), precision=precision, pref...]
  transfers between devices with their start and end apart: 4 -> 37, of which waited for: 4 -> 14; matrix products, arithmetic and copies ran while one was open for 1% -> 2% of each run, Pallas kernels for 0% -> 32%
where the time goes in v1:
time: 304 us; the launch traced here: 301 us
  waiting for transfers between devices  133 us (44%)
  Pallas kernels  114 us (38%)
  starting transfers between devices  30.2 us (10%)
  local copies, waits for them, and re-layouts  16.5 us (5%)
  matrix products  3.52 us (1%)
    ppermute x10, waiting for transfers between devices, swap(): return lax.ppermute(x, 'ct', [(c, c ^ ct_bit) for c in range(n_ct)])  80.5 us
    ppermute x27, waiting for transfers between devices, swap(): return lax.ppermute(x, 'rt', [(r, r ^ rt_bit) for r in range(n_rt)])  52.8 us
    pallas_call x3, Pallas kernels, mix_call(): pl.pallas_call(functools.partial(kernel, len(pieces)), grid=(block_cols /...  42.5 us
    pallas_call x1, Pallas kernels, inverse_factor(): pl.pallas_call(factor_kernel, out_shape=jax.ShapeDtypeStruct((n, n), F32)...  40.4 us
    ppermute x10, starting transfers between devices, swap(): return lax.ppermute(x, 'ct', [(c, c ^ ct_bit) for c in range(n_ct)])  17.6 us
    pallas_call x1, Pallas kernels, widen(): pl.pallas_call(functools.partial(widen_kernel, block_cols // STEP, window...  16.2 us
    pallas_call x1, Pallas kernels, basis_rows(): pl.pallas_call(basis_kernel, grid=(n_ct,), out_shape=[wide, wide, jax.Sha...  15.4 us
    unnamed x85, local copies, waits for them, and re-layouts  14.1 us
  transfers between devices with their start and end apart: 37, of which 14 were waited for; matrix products, arithmetic and copies ran while one was open for 2% of the time, Pallas kernels for 32%

profile of v1, /device:TPU:0, one launch (start us, length us, event | category | flops | bytes accessed | tf_op | source)
XLA Modules:
  0.0 301.1 jit_solution(8286641463249079070)
XLA Ops:
  2.4 4.1 %collective-permute-start = (f32[64,512]{1,0:T(8,128)S(1)}, f32[64,512]{1,0:T(8,128)S(1)}, u32[]{:S(2)}, u32[]{:S(2)}) collective-permute-start(f32[64,512]{1,0:T(8,128)S(1)} %get-tuple-element.42), channel_id=1, source_target_pairs={{0,4},{1,5},{2,6},{3,7},{4,0},{5,1},{6,2},{7,3},{8,12},{9,13},{10,... | collective-permute-start | bytes 393224 | tf_op jit(solution)/shard_map/ppermute | solution.py:27
  7.4 5.4 %collective-permute-done = f32[64,512]{1,0:T(8,128)S(1)} collective-permute-done((f32[64,512]{1,0:T(8,128)S(1)}, f32[64,512]{1,0:T(8,128)S(1)}, u32[]{:S(2)}, u32[]{:S(2)}) %collective-permute-start) | collective-permute-done | bytes 131104 | tf_op jit(solution)/shard_map/ppermute | solution.py:27
  14.2 6.2 %collective-permute-done.1 = f32[128,512]{1,0:T(8,128)S(1)} collective-permute-done((f32[128,512]{1,0:T(8,128)S(1)}, f32[128,512]{1,0:T(8,128)S(1)}, u32[]{:S(2)}, u32[]{:S(2)}) %collective-permute-start.1) | collective-permute-done | bytes 262176 | tf_op jit(solution)/shard_map/ppermute | solution.py:27
  23.8 16.2 %shard_map.87 = (f32[64,2048]{1,0:T(8,128)S(1)}, f32[64,2048]{1,0:T(8,128)S(1)}, f32[64,2048]{1,0:T(8,128)S(1)}, f32[64,2048]{1,0:T(8,128)S(1)}, f32[64,2048]{1,...) custom-call(s32[66]{0:T(128)S(1)} %pad_add_fusion.info, ...), custom_call_target="tpu_custom_call" | custom-call | flops 2415919104 | bytes 7340032 | tf_op jit(solution)/shard_map/pallas_call | solution.py:108
  45.7 6.8 %collective-permute-done.9.refs_4_ = f32[64,2048]{1,0:T(8,128)S(1)} collective-permute-done((f32[64,2048]{1,0:T(8,128)S(1)}, f32[64,2048]{1,0:T(8,128)S(1)}, u32[]{:S(2)}, u32[]{:S(2)}) %collective-permute-start.9) | collective-permute-done | bytes 524320 | tf_op jit(solution)/shard_map/ppermute | solution.py:27
  52.5 3.1 %collective-permute-done.13.refs_8_ = f32[64,2048]{1,0:T(8,128)S(1)} collective-permute-done((f32[64,2048]{1,0:T(8,128)S(1)}, f32[64,2048]{1,0:T(8,128)S(1)}, u32[]{:S(2)}, u32[]{:S(2)}) %collective-permute-start.13) | collective-permute-done | bytes 524320 | tf_op jit(solution)/shard_map/ppermute | solution.py:27
  55.7 3.1 %collective-permute-start.21 = (f32[64,2048]{1,0:T(8,128)S(1)}, f32[64,2048]{1,0:T(8,128)}, u32[]{:S(2)}, u32[]{:S(2)}) collective-permute-start(f32[64,2048]{1,0:T(8,128)S(1)} %get-tuple-element.30), channel_id=1, source_target_pairs={{0,4},{1,5},{2,6},{3,7},{4,0},{5,1},{6,2},{7,3},{8,12},{9,13},{10,... | collective-permute-start | bytes 1572872 | tf_op jit(solution)/shard_map/ppermute | solution.py:27
  58.8 16.1 %collective-permute-done.17.refs_12_ = f32[64,2048]{1,0:T(8,128)S(1)} collective-permute-done((f32[64,2048]{1,0:T(8,128)S(1)}, f32[64,2048]{1,0:T(8,128)S(1)}, u32[]{:S(2)}, u32[]{:S(2)}) %collective-permute-start.17) | collective-permute-done | bytes 524320 | tf_op jit(solution)/shard_map/ppermute | solution.py:27
  74.9 2.2 collective-permute-done.6.refs_1_
  77.1 3.4 %collective-permute-start.29 = (f32[64,2048]{1,0:T(8,128)S(1)}, f32[64,2048]{1,0:T(8,128)S(1)}, u32[]{:S(2)}, u32[]{:S(2)}) collective-permute-start(f32[64,2048]{1,0:T(8,128)S(1)} %get-tuple-element.36), channel_id=1, source_target_pairs={{0,6},{1,7},{2,4},{3,5},{4,2},{5,3},{6,0},{7,1},{8,14},{9,15},{10,... | collective-permute-start | bytes 1572872 | tf_op jit(solution)/shard_map/ppermute | solution.py:27
  82.7 33.9 %collective-permute-done.21.refs_0_ = f32[64,2048]{1,0:T(8,128)} collective-permute-done((f32[64,2048]{1,0:T(8,128)S(1)}, f32[64,2048]{1,0:T(8,128)}, u32[]{:S(2)}, u32[]{:S(2)}) %collective-permute-start.21) | collective-permute-done | bytes 524320 | tf_op jit(solution)/shard_map/ppermute | solution.py:27
  118.8 8.9 %collective-permute-done.25.refs_4_ = f32[64,2048]{1,0:T(8,128)} collective-permute-done((f32[64,2048]{1,0:T(8,128)S(1)}, f32[64,2048]{1,0:T(8,128)}, u32[]{:S(2)}, u32[]{:S(2)}) %collective-permute-start.25) | collective-permute-done | bytes 524320 | tf_op jit(solution)/shard_map/ppermute | solution.py:27
  131.5 11.2 %collective-permute-done.14.refs_9_ = f32[64,2048]{1,0:T(8,128)S(1)} collective-permute-done((f32[64,2048]{1,0:T(8,128)S(1)}, f32[64,2048]{1,0:T(8,128)S(1)}, u32[]{:S(2)}, u32[]{:S(2)}) %collective-permute-start.14) | collective-permute-done | bytes 524320 | tf_op jit(solution)/shard_map/ppermute | solution.py:29
  142.8 3.5 %fusion.2.gram_a = f32[512,512]{1,0:T(8,128)S(1)} fusion(f32[1024,512]{1,0:T(8,128)S(1)} %constant_dynamic-update-slice_fusion), kind=kOutput, calls=%fused_computation.31 | convolution fusion | flops 3221225472 | bytes 3145728 | tf_op jit(solution)/shard_map/dot_general | solution.py:67
  146.3 3.5 %collective-permute-done.18.refs_13_ = f32[64,2048]{1,0:T(8,128)S(1)} collective-permute-done((f32[64,2048]{1,0:T(8,128)S(1)}, f32[64,2048]{1,0:T(8,128)S(1)}, u32[]{:S(2)}, u32[]{:S(2)}) %collective-permute-start.18) | collective-permute-done | bytes 524320 | tf_op jit(solution)/shard_map/ppermute | solution.py:29
  155.1 10.6 %collective-permute-done.22.refs_1_ = f32[64,2048]{1,0:T(8,128)} collective-permute-done((f32[64,2048]{1,0:T(8,128)}, f32[64,2048]{1,0:T(8,128)}, u32[]{:S(2)}, u32[]{:S(2)}) %collective-permute-start.22) | collective-permute-done | bytes 524320 | tf_op jit(solution)/shard_map/ppermute | solution.py:29
  165.7 10.8 %collective-permute-done.26.refs_5_ = f32[64,2048]{1,0:T(8,128)} collective-permute-done((f32[64,2048]{1,0:T(8,128)}, f32[64,2048]{1,0:T(8,128)}, u32[]{:S(2)}, u32[]{:S(2)}) %collective-permute-start.26) | collective-permute-done | bytes 524320 | tf_op jit(solution)/shard_map/ppermute | solution.py:29
  179.4 12.3 %collective-permute-done.30.refs_1_ = f32[64,2048]{1,0:T(8,128)} collective-permute-done((f32[64,2048]{1,0:T(8,128)}, f32[64,2048]{1,0:T(8,128)}, u32[]{:S(2)}, u32[]{:S(2)}) %collective-permute-start.30) | collective-permute-done | bytes 524320 | tf_op jit(solution)/shard_map/ppermute | solution.py:29
  192.3 40.4 %shard_map.85.inverse = f32[512,512]{1,0:T(8,128)S(1)} custom-call(f32[512,512]{1,0:T(8,128)S(1)} %fusion.2.gram_a, f32[512,512]{1,0:T(8,128)} %collective-permute-done.4.gram_b), custom_call_target="tpu_custom_call" | custom-call | flops 40000000000 | bytes 3145728 | tf_op jit(solution)/shard_map/pallas_call | solution.py:201
  232.8 15.4 %shard_map.86 = (bf16[512,2048]{1,0:T(8,128)(2,1)S(1)}, bf16[512,2048]{1,0:T(8,128)(2,1)S(1)}, f32[512,512]{1,0:T(8,128)}, bf16[512,512]{1,0:T(8,128)(2,1)S(1)}, bf16[512,512]{1,0:T(8,128)(2,1)S(1)}) custom-call(f32[512,512]{1,0:T(8,128)S(1)} %shard_map.85.inverse, f32[2,8,64,512]{3,2,1,0:T(8,128)S(1)} %bitcast.20, f32[2,8,64,512]{3,2,1,0:T(8,128)} %bitcast.2.other, ...), custom_call_target="tpu_custom_call" | custom-call | flops 5368709120 | bytes 12582912 | tf_op jit(solution)/shard_map/pallas_call | solution.py:253
  250.7 15.1 %shard_map.88 = (f32[512,2048]{1,0:T(8,128)S(1)}, f32[512,2048]{1,0:T(8,128)S(1)}) custom-call(bf16[512,2048]{1,0:T(8,128)(2,1)S(1)} %get-tuple-element.22.q_high, bf16[512,2048]{1,0:T(8,128)(2,1)S(1)} %get-tuple-element.23.q_low, s32[1,2048]{1,0:T(1,128)S(1)} %sub.44.targets, f32[64,2048]{1,0:T(8,128)S(1)} %copy-done.3, ...), custom_call_target="tpu_custom_call" | custom-call | flops 10737418240 | bytes 16777216 | tf_op jit(solution)/shard_map/pallas_call | solution.py:331
  269.9 2.2 copy-done.29
  272.1 9.7 %shard_map.89 = (f32[512,2048]{1,0:T(8,128)S(1)}, f32[512,2048]{1,0:T(8,128)S(1)}) custom-call(bf16[512,2048]{1,0:T(8,128)(2,1)S(1)} %get-tuple-element.22.q_high, bf16[512,2048]{1,0:T(8,128)(2,1)S(1)} %get-tuple-element.23.q_low, s32[1,2048]{1,0:T(1,128)S(1)} %sub.44.targets, f32[512,2048]{1,0:T(8,128)S(1)} %copy-done.29, f32[512,2048]{1,0:T(8,128)} %copy-done.30, ...), custom_call_target="tpu_custom_call" | custom-call | flops 5368709120 | bytes 20971520 | tf_op jit(solution)/shard_map/pallas_call | solution.py:331
  283.5 17.6 %shard_map.90 = (f32[512,2048]{1,0:T(8,128)}, f32[512,2048]{1,0:T(8,128)}) custom-call(bf16[512,2048]{1,0:T(8,128)(2,1)S(1)} %get-tuple-element.22.q_high, bf16[512,2048]{1,0:T(8,128)(2,1)S(1)} %copy-done.32, s32[1,2048]{1,0:T(1,128)S(1)} %sub.44.targets, f32[512,2048]{1,0:T(8,128)S(1)} %get-tuple-element.32.factor_in, ...), custom_call_target="tpu_custom_call" | custom-call | flops 8589934592 | bytes 20971520 | tf_op jit(solution)/shard_map/pallas_call | solution.py:331
  (167 shorter events, 37.9 us)
Async XLA Ops:
  20.5 21.8 %collective-permute-start.2 = (f32[256,512]{1,0:T(8,128)S(1)}, f32[256,512]{1,0:T(8,128)S(1)}, u32[]{:S(2)}, u32[]{:S(2)}) collective-permute-start(f32[256,512]{1,0:T(8,128)S(1)} %pad_maximum_fusion.1), channel_id=1, source_target_pairs={{0,1},{1,0},{2,3},{3,2},{4,5},{5,4},{6,7},{7,6},{8,9},{9,8},{10,11... | collective-permute-start | bytes 1572872 | tf_op jit(solution)/shard_map/ppermute | solution.py:27
  42.3 75.8 %collective-permute-start.3 = (f32[512,512]{1,0:T(8,128)S(1)}, f32[512,512]{1,0:T(8,128)S(1)}, u32[]{:S(2)}, u32[]{:S(2)}) collective-permute-start(f32[512,512]{1,0:T(8,128)S(1)} %pad_maximum_fusion), channel_id=1, source_target_pairs={{0,16},{8,24},{16,0},{24,8},{1,17},{9,25},{17,1},{25,9},{2,18},{10... | collective-permute-start | bytes 3145736 | tf_op jit(solution)/shard_map/ppermute | solution.py:29
  43.9 30.9 %collective-permute-start.17 = (f32[64,2048]{1,0:T(8,128)S(1)}, f32[64,2048]{1,0:T(8,128)S(1)}, u32[]{:S(2)}, u32[]{:S(2)}) collective-permute-start(f32[64,2048]{1,0:T(8,128)S(1)} %get-tuple-element.27), channel_id=1, source_target_pairs={{0,3},{1,2},{2,1},{3,0},{4,7},{5,6},{6,5},{7,4},{8,11},{9,10},{10,... | collective-permute-start | bytes 1572872 | tf_op jit(solution)/shard_map/ppermute | solution.py:27
  45.2 32.0 %collective-permute-start.6 = (f32[64,2048]{1,0:T(8,128)S(1)}, f32[64,2048]{1,0:T(8,128)}, u32[]{:S(2)}, u32[]{:S(2)}) collective-permute-start(f32[64,2048]{1,0:T(8,128)S(1)} %get-tuple-element.24.refs_0_), channel_id=1, source_target_pairs={{0,16},{8,24},{16,0},{24,8},{1,17},{9,25},{17,1},{25,9},{2,18},{10... | collective-permute-start | bytes 1572872 | tf_op jit(solution)/shard_map/ppermute | solution.py:29
  52.5 28.0 %collective-permute-start.7 = (f32[64,2048]{1,0:T(8,128)S(1)}, f32[64,2048]{1,0:T(8,128)S(1)}, u32[]{:S(2)}, u32[]{:S(2)}) collective-permute-start(f32[64,2048]{1,0:T(8,128)S(1)} %get-tuple-element.24.refs_0_), channel_id=1, source_target_pairs={{0,8},{8,0},{16,24},{24,16},{1,9},{9,1},{17,25},{25,17},{2,10},{10... | collective-permute-start | bytes 1572872 | tf_op jit(solution)/shard_map/ppermute | solution.py:29
  55.7 61.0 %collective-permute-start.21 = (f32[64,2048]{1,0:T(8,128)S(1)}, f32[64,2048]{1,0:T(8,128)}, u32[]{:S(2)}, u32[]{:S(2)}) collective-permute-start(f32[64,2048]{1,0:T(8,128)S(1)} %get-tuple-element.30), channel_id=1, source_target_pairs={{0,4},{1,5},{2,6},{3,7},{4,0},{5,1},{6,2},{7,3},{8,12},{9,13},{10,... | collective-permute-start | bytes 1572872 | tf_op jit(solution)/shard_map/ppermute | solution.py:27
  74.8 52.9 %collective-permute-start.25 = (f32[64,2048]{1,0:T(8,128)S(1)}, f32[64,2048]{1,0:T(8,128)}, u32[]{:S(2)}, u32[]{:S(2)}) collective-permute-start(f32[64,2048]{1,0:T(8,128)S(1)} %get-tuple-element.31), channel_id=1, source_target_pairs={{0,5},{1,4},{2,7},{3,6},{4,1},{5,0},{6,3},{7,2},{8,13},{9,12},{10,... | collective-permute-start | bytes 1572872 | tf_op jit(solution)/shard_map/ppermute | solution.py:27
  77.1 50.6 %collective-permute-start.29 = (f32[64,2048]{1,0:T(8,128)S(1)}, f32[64,2048]{1,0:T(8,128)S(1)}, u32[]{:S(2)}, u32[]{:S(2)}) collective-permute-start(f32[64,2048]{1,0:T(8,128)S(1)} %get-tuple-element.36), channel_id=1, source_target_pairs={{0,6},{1,7},{2,4},{3,5},{4,2},{5,3},{6,0},{7,1},{8,14},{9,15},{10,... | collective-permute-start | bytes 1572872 | tf_op jit(solution)/shard_map/ppermute | solution.py:27
  81.4 47.9 %collective-permute-start.33 = (f32[64,2048]{1,0:T(8,128)S(1)}, f32[64,2048]{1,0:T(8,128)S(1)}, u32[]{:S(2)}, u32[]{:S(2)}) collective-permute-start(f32[64,2048]{1,0:T(8,128)S(1)} %get-tuple-element.37), channel_id=1, source_target_pairs={{0,7},{1,6},{2,5},{3,4},{4,3},{5,2},{6,1},{7,0},{8,15},{9,14},{10,... | collective-permute-start | bytes 1572872 | tf_op jit(solution)/shard_map/ppermute | solution.py:27
  118.1 24.6 %collective-permute-start.14 = (f32[64,2048]{1,0:T(8,128)S(1)}, f32[64,2048]{1,0:T(8,128)S(1)}, u32[]{:S(2)}, u32[]{:S(2)}) collective-permute-start(f32[64,2048]{1,0:T(8,128)S(1)} %collective-permute-done.13.refs_8_), channel_id=1, source_target_pairs={{0,16},{8,24},{16,0},{24,8},{1,17},{9,25},{17,1},{25,9},{2,18},{10... | collective-permute-start | bytes 1572872 | tf_op jit(solution)/shard_map/ppermute | solution.py:29
  127.7 64.5 %collective-permute-start.5 = (f32[1024,512]{1,0:T(8,128)S(1)}, f32[1024,512]{1,0:T(8,128)}, u32[]{:S(2)}, u32[]{:S(2)}) collective-permute-start(f32[1024,512]{1,0:T(8,128)S(1)} %constant_dynamic-update-slice_fusion), channel_id=1, source_target_pairs={{0,8},{8,0},{16,24},{24,16},{1,9},{9,1},{17,25},{25,17},{2,10},{10... | collective-permute-start | bytes 6291464 | tf_op jit(solution)/shard_map/ppermute | solution.py:29
  127.7 22.1 %collective-permute-start.18 = (f32[64,2048]{1,0:T(8,128)S(1)}, f32[64,2048]{1,0:T(8,128)S(1)}, u32[]{:S(2)}, u32[]{:S(2)}) collective-permute-start(f32[64,2048]{1,0:T(8,128)S(1)} %collective-permute-done.17.refs_12_), channel_id=1, source_target_pairs={{0,16},{8,24},{16,0},{24,8},{1,17},{9,25},{17,1},{25,9},{2,18},{10... | collective-permute-start | bytes 1572872 | tf_op jit(solution)/shard_map/ppermute | solution.py:29
  153.0 23.5 %collective-permute-start.26 = (f32[64,2048]{1,0:T(8,128)}, f32[64,2048]{1,0:T(8,128)}, u32[]{:S(2)}, u32[]{:S(2)}) collective-permute-start(f32[64,2048]{1,0:T(8,128)} %collective-permute-done.25.refs_4_), channel_id=1, source_target_pairs={{0,16},{8,24},{16,0},{24,8},{1,17},{9,25},{17,1},{25,9},{2,18},{10... | collective-permute-start | bytes 1572872 | tf_op jit(solution)/shard_map/ppermute | solution.py:29
  154.4 37.3 %collective-permute-start.4 = (f32[512,512]{1,0:T(8,128)S(1)}, f32[512,512]{1,0:T(8,128)}, u32[]{:S(2)}, u32[]{:S(2)}) collective-permute-start(f32[512,512]{1,0:T(8,128)S(1)} %fusion.2.gram_a), channel_id=1, source_target_pairs={{0,8},{8,0},{16,24},{24,16},{1,9},{9,1},{17,25},{25,17},{2,10},{10... | collective-permute-start | bytes 3145736 | tf_op jit(solution)/shard_map/ppermute | solution.py:29
  154.6 24.2 %collective-permute-start.23 = (f32[64,2048]{1,0:T(8,128)}, f32[64,2048]{1,0:T(8,128)}, u32[]{:S(2)}, u32[]{:S(2)}) collective-permute-start(f32[64,2048]{1,0:T(8,128)} %collective-permute-done.21.refs_0_), channel_id=1, source_target_pairs={{0,8},{8,0},{16,24},{24,16},{1,9},{9,1},{17,25},{25,17},{2,10},{10... | collective-permute-start | bytes 1572872 | tf_op jit(solution)/shard_map/ppermute | solution.py:29
  178.8 70.2 %collective-permute-start.34 = (f32[64,2048]{1,0:T(8,128)}, f32[64,2048]{1,0:T(8,128)S(1)}, u32[]{:S(2)}, u32[]{:S(2)}) collective-permute-start(f32[64,2048]{1,0:T(8,128)} %copy-done.12), channel_id=1, source_target_pairs={{0,16},{8,24},{16,0},{24,8},{1,17},{9,25},{17,1},{25,9},{2,18},{10... | collective-permute-start | bytes 1572872 | tf_op jit(solution)/shard_map/ppermute | solution.py:29
  179.4 70.2 %collective-permute-start.12 = (f32[64,2048]{1,0:T(8,128)}, f32[64,2048]{1,0:T(8,128)S(1)}, u32[]{:S(2)}, u32[]{:S(2)}) collective-permute-start(f32[64,2048]{1,0:T(8,128)} %copy-done.16), channel_id=1, source_target_pairs={{0,8},{8,0},{16,24},{24,16},{1,9},{9,1},{17,25},{25,17},{2,10},{10... | collective-permute-start | bytes 1572872 | tf_op jit(solution)/shard_map/ppermute | solution.py:29
  191.7 58.0 %collective-permute-start.16 = (f32[64,2048]{1,0:T(8,128)}, f32[64,2048]{1,0:T(8,128)S(1)}, u32[]{:S(2)}, u32[]{:S(2)}) collective-permute-start(f32[64,2048]{1,0:T(8,128)} %copy-done.18), channel_id=1, source_target_pairs={{0,8},{8,0},{16,24},{24,16},{1,9},{9,1},{17,25},{25,17},{2,10},{10... | collective-permute-start | bytes 1572872 | tf_op jit(solution)/shard_map/ppermute | solution.py:29
  191.7 58.4 %collective-permute-start.20 = (f32[64,2048]{1,0:T(8,128)}, f32[64,2048]{1,0:T(8,128)S(1)}, u32[]{:S(2)}, u32[]{:S(2)}) collective-permute-start(f32[64,2048]{1,0:T(8,128)} %copy-done.20), channel_id=1, source_target_pairs={{0,8},{8,0},{16,24},{24,16},{1,9},{9,1},{17,25},{25,17},{2,10},{10... | collective-permute-start | bytes 1572872 | tf_op jit(solution)/shard_map/ppermute | solution.py:29
  192.2 58.0 %collective-permute-start.24 = (f32[64,2048]{1,0:T(8,128)}, f32[64,2048]{1,0:T(8,128)S(1)}, u32[]{:S(2)}, u32[]{:S(2)}) collective-permute-start(f32[64,2048]{1,0:T(8,128)} %collective-permute-done.22.refs_1_), channel_id=1, source_target_pairs={{0,8},{8,0},{16,24},{24,16},{1,9},{9,1},{17,25},{25,17},{2,10},{10... | collective-permute-start | bytes 1572872 | tf_op jit(solution)/shard_map/ppermute | solution.py:29
  249.0 32.8 %collective-permute-start.31 = (f32[64,2048]{1,0:T(8,128)S(1)}, f32[64,2048]{1,0:T(8,128)S(1)}, u32[]{:S(2)}, u32[]{:S(2)}) collective-permute-start(f32[64,2048]{1,0:T(8,128)S(1)} %copy-done.9), channel_id=1, source_target_pairs={{0,8},{8,0},{16,24},{24,16},{1,9},{9,1},{17,25},{25,17},{2,10},{10... | collective-permute-start | bytes 1572872 | tf_op jit(solution)/shard_map/ppermute | solution.py:29
  249.6 32.3 %collective-permute-start.35 = (f32[64,2048]{1,0:T(8,128)S(1)}, f32[64,2048]{1,0:T(8,128)S(1)}, u32[]{:S(2)}, u32[]{:S(2)}) collective-permute-start(f32[64,2048]{1,0:T(8,128)S(1)} %copy-done.13), channel_id=1, source_target_pairs={{0,8},{8,0},{16,24},{24,16},{1,9},{9,1},{17,25},{25,17},{2,10},{10... | collective-permute-start | bytes 1572872 | tf_op jit(solution)/shard_map/ppermute | solution.py:29
  250.1 31.8 %collective-permute-start.32 = (f32[64,2048]{1,0:T(8,128)}, f32[64,2048]{1,0:T(8,128)S(1)}, u32[]{:S(2)}, u32[]{:S(2)}) collective-permute-start(f32[64,2048]{1,0:T(8,128)} %collective-permute-done.30.refs_1_), channel_id=1, source_target_pairs={{0,8},{8,0},{16,24},{24,16},{1,9},{9,1},{17,25},{25,17},{2,10},{10... | collective-permute-start | bytes 1572872 | tf_op jit(solution)/shard_map/ppermute | solution.py:29
  250.2 31.7 %collective-permute-start.36 = (f32[64,2048]{1,0:T(8,128)S(1)}, f32[64,2048]{1,0:T(8,128)S(1)}, u32[]{:S(2)}, u32[]{:S(2)}) collective-permute-start(f32[64,2048]{1,0:T(8,128)S(1)} %collective-permute-done.34.refs_5_), channel_id=1, source_target_pairs={{0,8},{8,0},{16,24},{24,16},{1,9},{9,1},{17,25},{25,17},{2,10},{10... | collective-permute-start | bytes 1572872 | tf_op jit(solution)/shard_map/ppermute | solution.py:29
  (52 other events, 957.3 us)

commit v2 on v1

v2 whole, which is shorter than its diff:
```python
import functools

import jax
import jax.numpy as jnp
import numpy as np
from jax import lax
from jax.experimental import pallas as pl
from jax.experimental.pallas import tpu as pltpu
from jax.sharding import PartitionSpec as P

FRONT_COLS = 16384
PANEL = 512
STEP = 256
WIDE = 512
LANES = 128
NB = 128
SUB = 8

HI = lax.Precision.HIGHEST
F32 = jnp.float32
BF16 = jnp.bfloat16
MIB = 2**20


def swap(x, rt_bit, ct_bit):
    n_rt, n_ct = lax.axis_size("rt"), lax.axis_size("ct")
    if not rt_bit:
        return lax.ppermute(x, "ct", [(c, c ^ ct_bit) for c in range(n_ct)])
    if not ct_bit:
        return lax.ppermute(x, "rt", [(r, r ^ rt_bit) for r in range(n_rt)])
    pairs = [
        (r * n_ct + c, (r ^ rt_bit) * n_ct + (c ^ ct_bit)) for r in range(n_rt) for c in range(n_ct)
    ]
    return lax.ppermute(x, ("rt", "ct"), pairs)


def bits_down(size, last):
    bit, bits = size // 2, []
    while bit >= last:
        bits.append(bit)
        bit //= 2
    return bits


def combos(bits):
    order = [0]
    for bit in bits:
        order = order + [value ^ bit for value in order]
    return order


def halves(x):
    high = x.astype(BF16)
    return high, (x - high.astype(F32)).astype(BF16)


def dot(a, b):
    return jnp.dot(a, b, preferred_element_type=F32)


def dot_nt(a, b, precision=None):
    return lax.dot_general(
        a, b, (((1,), (1,)), ((), ())), precision=precision, preferred_element_type=F32
    )


def dot_tn(a, b, precision=None):
    return lax.dot_general(
        a, b, (((0,), (0,)), ((), ())), precision=precision, preferred_element_type=F32
    )


MARK = jax.ShapeDtypeStruct((SUB, LANES), F32)


def params(mib):
    return pltpu.CompilerParams(vmem_limit_bytes=mib * MIB)


def widen_kernel(tiles, window, places, waits, info, child, cmap, limits, *outs):
    rows = child.shape[0]
    my_block = info[info.shape[0] - 2]
    first_row = info[info.shape[0] - 1]
    row_ids = first_row + lax.broadcasted_iota(jnp.int32, (rows, window), 0)
    col_ids = lax.broadcasted_iota(jnp.int32, (STEP, window), 0)
    for place, out in zip(places, outs[waits:-1]):
        block = my_block ^ place

        def tile(i, carry, block=block, out=out):
            t = block * tiles + i
            cols = pl.ds(pl.multiple_of(info[t] * LANES, LANES), window)
            live = jnp.where(row_ids < limits[:, cols], child[:, cols], 0.0)
            hot = jnp.where(col_ids == cmap[:, cols] - t * STEP, 1.0, 0.0).astype(BF16)
            spread = dot_nt(jnp.concatenate(halves(live), axis=0), hot)
            out[:, pl.ds(pl.multiple_of(i * STEP, STEP), STEP)] = spread[:rows] + spread[rows:]
            return carry

        lax.fori_loop(0, tiles, tile, 0, unroll=4)


def widen(info, child, cmap, limits, places, n_ct, tokens):
    rows, width = child.shape
    block_cols = FRONT_COLS // n_ct
    window = STEP + LANES
    whole = pl.BlockSpec(memory_space=pltpu.VMEM)
    made = pl.pallas_call(
        functools.partial(widen_kernel, block_cols // STEP, window, tuple(places), len(tokens)),
        out_shape=[jax.ShapeDtypeStruct((rows, block_cols), F32)] * len(places) + [MARK],
        in_specs=[pl.BlockSpec(memory_space=pltpu.SMEM), whole, whole, whole]
        + [pl.BlockSpec(memory_space=pl.ANY)] * len(tokens),
        out_specs=[whole] * len(places) + [pl.BlockSpec(memory_space=pl.ANY)],
        compiler_params=params(56),
        cost_estimate=pl.CostEstimate(
            flops=4 * rows * window * block_cols * len(places),
            bytes_accessed=4 * rows * (width + block_cols * len(places)),
            transcendentals=0,
        ),
    )(info, child, cmap, limits, *tokens)
    return dict(zip(places, made)), made[-1]


def small_inverse(tile):
    a = [
        [jnp.broadcast_to(tile[i : i + 1, k : k + 1], (SUB, NB)) for k in range(i + 1)]
        for i in range(SUB)
    ]
    scale = [None] * SUB
    lower = [[None] * SUB for _ in range(SUB)]
    inverse = [[None] * SUB for _ in range(SUB)]
    for j in range(SUB):
        scale[j] = lax.rsqrt(a[j][j])
        for i in range(j + 1, SUB):
            lower[i][j] = a[i][j] * scale[j]
        for i in range(j + 1, SUB):
            for k in range(j + 1, i + 1):
                a[i][k] = a[i][k] - lower[i][j] * lower[k][j]
    for j in range(SUB):
        inverse[j][j] = scale[j]
        for i in range(j + 1, SUB):
            total = lower[i][j] * inverse[j][j]
            for k in range(j + 1, i):
                total = total + lower[i][k] * inverse[k][j]
            inverse[i][j] = -scale[i] * total
    return inverse


def apply_small(inverse, tiles):
    sub = lax.broadcasted_iota(jnp.int32, (SUB, NB), 0)
    outs = [None] * len(tiles)
    for k in range(SUB):
        column = jnp.zeros((SUB, NB), F32)
        for i in range(k, SUB):
            column = jnp.where(sub == i, inverse[i][k], column)
        for n, tile in enumerate(tiles):
            term = column * jnp.broadcast_to(tile[k : k + 1, :], (SUB, NB))
            outs[n] = term if outs[n] is None else outs[n] + term
    return outs


def identity(n):
    shape = (n, n)
    same = lax.broadcasted_iota(jnp.int32, shape, 0) == lax.broadcasted_iota(jnp.int32, shape, 1)
    return jnp.where(same, 1.0, 0.0)


def thirds(x):
    high = x.astype(BF16)
    rest = x - high.astype(F32)
    mid = rest.astype(BF16)
    return high, mid, (rest - mid.astype(F32)).astype(BF16)


def diagonal_inverse(block, out, work):
    lane = lax.broadcasted_iota(jnp.int32, (SUB, NB), 1)
    work[:NB, :NB] = block
    work[:NB, NB:] = identity(NB)
    work[NB:, :] = jnp.zeros((SUB, 2 * NB), F32)

    def body(s, carry):
        tile, before = carry
        h, m, l = thirds(before)
        left = jnp.concatenate([x[:, :NB] for x in (h, h, m, h, l, m)], axis=0)
        right = jnp.concatenate([h, m, h, l, h, m], axis=0)
        work[:NB, :] = work[:NB, :] - dot_tn(left, right)
        after = work[pl.ds(pl.multiple_of(SUB * s + SUB, SUB), SUB), :]
        shift = lax.rem(NB - SUB * s, NB)
        inverse = small_inverse(pltpu.roll(tile[:, :NB], shift, 1))
        turned = pltpu.roll(after[:, :NB], shift, 1)
        top, top_right = apply_small(inverse, [tile[:, :NB], tile[:, NB:]])
        out[pl.ds(pl.multiple_of(SUB * s, SUB), SUB), :] = top_right
        top = jnp.concatenate([jnp.where(lane >= SUB * s, top, 0.0), top_right], axis=1)
        columns = [jnp.broadcast_to(turned[:, k : k + 1], (SUB, NB)) for k in range(SUB)]
        for i in range(SUB):
            weight = inverse[i][0] * columns[0]
            for k in range(1, i + 1):
                weight = weight + inverse[i][k] * columns[k]
            weight = jnp.concatenate([weight, weight], axis=1)
            after = after - weight * jnp.broadcast_to(top[i : i + 1], (SUB, 2 * NB))
        return after, top

    lax.fori_loop(0, NB // SUB, body, (work[:SUB, :], jnp.zeros((SUB, 2 * NB), F32)))


def factor_kernel(gram_a, gram_b, *refs):
    out, _, whole, small, work = refs[-5:]
    n = out.shape[0]
    whole[:, :n] = gram_a[...] + gram_b[...]
    whole[:, n:] = identity(n)
    for lo in range(0, n, NB):
        hi = lo + NB
        diagonal_inverse(whole[lo:hi, lo:hi], small, work)
        rows = jnp.dot(small[...], whole[lo:hi, lo : n + hi], precision=HI, preferred_element_type=F32)
        out[lo:hi, :hi] = rows[:, n - lo :]
        if hi < n:
            out[lo:hi, hi:] = jnp.zeros((NB, n - hi), F32)
            whole[hi:, hi : n + hi] -= dot_tn(rows[:, NB : n - lo], rows[:, NB:], HI)


def inverse_factor(gram_a, gram_b, tokens):
    n = gram_a.shape[0]
    whole = pl.BlockSpec(memory_space=pltpu.VMEM)
    return pl.pallas_call(
        factor_kernel,
        out_shape=[jax.ShapeDtypeStruct((n, n), F32), MARK],
        in_specs=[whole] * 2 + [pl.BlockSpec(memory_space=pl.ANY)] * len(tokens),
        out_specs=[whole, pl.BlockSpec(memory_space=pl.ANY)],
        scratch_shapes=[
            pltpu.VMEM((n, 2 * n), F32),
            pltpu.VMEM((NB, NB), F32),
            pltpu.VMEM((NB + SUB, 2 * NB), F32),
        ],
        compiler_params=params(56),
        cost_estimate=pl.CostEstimate(
            flops=30 * 10**9, bytes_accessed=12 * n * n, transcendentals=0
        ),
    )(gram_a, gram_b, *tokens)


def gate_kernel(*refs):
    pass


def gate(arrays, tokens):
    if not arrays:
        return []
    anywhere = pl.BlockSpec(memory_space=pl.ANY)
    return pl.pallas_call(
        gate_kernel,
        out_shape=[jax.ShapeDtypeStruct(x.shape, x.dtype) for x in arrays],
        in_specs=[anywhere] * (len(arrays) + len(tokens)),
        out_specs=[anywhere] * len(arrays),
        input_output_aliases={k: k for k in range(len(arrays))},
        cost_estimate=pl.CostEstimate(flops=0, bytes_accessed=0, transcendentals=0),
    )(*arrays, *tokens)


def join_kernel(count, cut, *refs):
    parts, outs = refs[:count], refs[-cut - 1 : -1]
    width = outs[0].shape[1]
    row = 0
    for part in parts:
        rows = part.shape[0]
        for k, out in enumerate(outs):
            out[row : row + rows, :] = part[:, k * width : (k + 1) * width]
        row += rows


def join(parts, tokens=(), cut=1):
    rows, width = sum(x.shape[0] for x in parts), parts[0].shape[1]
    whole = pl.BlockSpec(memory_space=pltpu.VMEM)
    out = pl.pallas_call(
        functools.partial(join_kernel, len(parts), cut),
        out_shape=[jax.ShapeDtypeStruct((rows, width // cut), F32)] * cut + [MARK],
        in_specs=[whole] * len(parts) + [pl.BlockSpec(memory_space=pl.ANY)] * len(tokens),
        out_specs=[whole] * cut + [pl.BlockSpec(memory_space=pl.ANY)],
        compiler_params=params(16 if width == PANEL or width == PANEL // 2 else 56),
        cost_estimate=pl.CostEstimate(
            flops=0, bytes_accessed=8 * rows * width, transcendentals=0
        ),
    )(*parts, *tokens)
    return (out[:cut] if cut > 1 else out[0]), out[-1]


def gram_kernel(a_mine, a_other, b_mine, b_other, *refs):
    panel, gram = refs[-3:-1]
    half, width = a_mine.shape
    quarter = half // 2
    panel[:half, :width] = a_mine[...]
    panel[half:, :width] = a_other[...]
    for k, source in enumerate((b_mine, b_other)):
        panel[k * quarter : (k + 1) * quarter, width:] = source[:quarter, :]
        panel[half + k * quarter : half + (k + 1) * quarter, width:] = source[quarter:, :]
    rows = panel[...]
    gram[...] = dot_tn(rows, rows, HI)


def gram_of(a_mine, a_other, b_mine, b_other, tokens):
    half, width = a_mine.shape
    whole = pl.BlockSpec(memory_space=pltpu.VMEM)
    return pl.pallas_call(
        gram_kernel,
        out_shape=[
            jax.ShapeDtypeStruct((2 * half, 2 * width), F32),
            jax.ShapeDtypeStruct((2 * width, 2 * width), F32),
            MARK,
        ],
        in_specs=[whole] * 4 + [pl.BlockSpec(memory_space=pl.ANY)] * len(tokens),
        out_specs=[whole] * 2 + [pl.BlockSpec(memory_space=pl.ANY)],
        compiler_params=params(24),
        cost_estimate=pl.CostEstimate(
            flops=4 * half * 4 * width * width, bytes_accessed=4 * half * width, transcendentals=0
        ),
    )(a_mine, a_other, b_mine, b_other, *tokens)


def basis_kernel(count, waits, *refs):
    inverse, refs = refs[:count], refs[count:]
    own, other, targets = refs[:3]
    q_high, q_low, basis, turned_high, turned_low = refs[3 + waits :]
    d = pl.program_id(0)
    group, panel = targets.shape[-1], inverse[0].shape[1]
    rows = jnp.concatenate(
        [own[...].reshape(group // 2, panel), other[...].reshape(group // 2, panel)], axis=0
    )
    inv_high, inv_low = halves(inverse[0][...])
    high, low = halves(rows)
    q = dot_nt(inv_high, high) + (dot_nt(inv_low, high) + dot_nt(inv_high, low))
    q_h, q_l = halves(q)
    q_high[...] = q_h
    q_low[...] = q_l
    front = basis.shape[1]
    ids = lax.broadcasted_iota(jnp.int32, (front, group), 0)
    hot = jnp.where(ids == targets[0], 1.0, 0.0).astype(BF16)
    part = dot_nt(q_h, hot) + dot_nt(q_l, hot)

    @pl.when(d == 0)
    def _():
        basis[...] = part

    @pl.when(d > 0)
    def _():
        basis[...] += part

    @pl.when(d == pl.num_programs(0) - 1)
    def _():
        turned_h, turned_l = halves(basis[...].T)
        turned_high[...] = turned_h
        turned_low[...] = turned_l


def basis_rows(inverse, own, other, targets, tokens, front_rows, order):
    last, half, upper, src, panel = own.shape
    n_ct = last * upper
    group = 2 * half * src
    depth = upper.bit_length() - 1

    def place(step):
        d = sum(jnp.where(step == k, value, 0) for k, value in enumerate(order))
        spot = sum(((d >> (k + 1)) & 1) << (depth - 1 - k) for k in range(depth))
        return (d & 1, 0, spot, 0, 0)

    wide = jax.ShapeDtypeStruct((panel, n_ct * group), BF16)
    return pl.pallas_call(
        functools.partial(basis_kernel, len(inverse), len(tokens)),
        grid=(n_ct,),
        out_shape=[
            wide,
            wide,
            jax.ShapeDtypeStruct((panel, front_rows), F32),
            jax.ShapeDtypeStruct((front_rows, panel), BF16),
            jax.ShapeDtypeStruct((front_rows, panel), BF16),
        ],
        in_specs=[
            *[pl.BlockSpec((panel, panel), lambda d: (0, 0)) for _ in inverse],
            pl.BlockSpec((1, half, 1, src, panel), place),
            pl.BlockSpec((1, half, 1, src, panel), place),
            pl.BlockSpec((1, 1, group), lambda d: (d, 0, 0)),
            *[pl.BlockSpec(memory_space=pl.ANY) for _ in tokens],
        ],
        out_specs=[
            pl.BlockSpec((panel, group), lambda d: (0, d)),
            pl.BlockSpec((panel, group), lambda d: (0, d)),
            pl.BlockSpec((panel, front_rows), lambda d: (0, 0)),
            pl.BlockSpec((front_rows, panel), lambda d: (0, 0)),
            pl.BlockSpec((front_rows, panel), lambda d: (0, 0)),
        ],
        compiler_params=params(56),
        cost_estimate=pl.CostEstimate(
            flops=8 * panel * panel * n_ct * group, bytes_accessed=6 * MIB, transcendentals=0
        ),
    )(*inverse, own, other, targets, *tokens)


def mix(q_high, q_low, hot, pieces, spots, src):
    rows = jnp.concatenate([pieces[n][lo : lo + src, :] for n, lo in spots], axis=0)
    high, low = halves(rows)
    factor = dot(q_high[...], high) + (dot(q_low[...], high) + dot(q_high[...], low))
    return factor, dot(hot[...], high) + dot(hot[...], low)


def build_hot(targets, hot):
    @pl.when(pl.program_id(0) == 0)
    def _():
        ids = lax.broadcasted_iota(jnp.int32, hot.shape, 0)
        hot[...] = jnp.where(ids == targets[...], 1.0, 0.0).astype(BF16)


def first_kernel(count, spots, src, q_high, q_low, targets, *refs):
    pieces, (factor, placed, hot) = refs[:count], refs[-3:]
    build_hot(targets, hot)
    factor[...], placed[...] = mix(q_high, q_low, hot, pieces, spots, src)


def more_kernel(count, spots, src, q_high, q_low, targets, factor_in, placed_in, *refs):
    pieces, (factor, placed, hot) = refs[:count], refs[-3:]
    build_hot(targets, hot)
    add_factor, add_placed = mix(q_high, q_low, hot, pieces, spots, src)
    factor[...] = factor_in[...] + add_factor
    placed[...] = placed_in[...] + add_placed


def last_kernel(count, spots, src, q_high, q_low, targets, factor_in, placed_in, turned_high, turned_low, *refs):
    pieces, (factor, remainder, hot) = refs[:count], refs[-3:]
    build_hot(targets, hot)
    add_factor, add_placed = mix(q_high, q_low, hot, pieces, spots, src)
    total = factor_in[...] + add_factor
    factor[...] = total
    high, low = halves(total)
    removed = dot(turned_high[...], high) + (dot(turned_low[...], high) + dot(turned_high[...], low))
    remainder[...] = (placed_in[...] + add_placed) - removed


def mix_call(kernel, group, extra, turned, pieces, spots, q_high, q_low, targets, src, front_rows, tokens):
    panel = q_high.shape[0]
    block_cols = pieces[0].shape[1]
    depth = len(spots) * src
    column = lambda j: (0, j)
    fixed = lambda j: (0, group)
    still = lambda j: (0, 0)
    flops = depth * block_cols * (3 * panel + 2 * front_rows)
    flops += 3 * panel * front_rows * block_cols if turned else 0
    return pl.pallas_call(
        functools.partial(kernel, len(pieces), spots, src),
        grid=(block_cols // WIDE,),
        out_shape=[
            jax.ShapeDtypeStruct((panel, block_cols), F32),
            jax.ShapeDtypeStruct((front_rows, block_cols), F32),
        ],
        in_specs=[
            pl.BlockSpec((panel, depth), fixed),
            pl.BlockSpec((panel, depth), fixed),
            pl.BlockSpec((1, depth), fixed),
        ]
        + [pl.BlockSpec((x.shape[0], WIDE), column) for x in extra]
        + [pl.BlockSpec(x.shape, still) for x in turned]
        + [pl.BlockSpec((x.shape[0], WIDE), column) for x in pieces]
        + [pl.BlockSpec(memory_space=pl.ANY)] * len(tokens),
        out_specs=[
            pl.BlockSpec((panel, WIDE), column),
            pl.BlockSpec((front_rows, WIDE), column),
        ],
        scratch_shapes=[pltpu.VMEM((front_rows, depth), BF16)],
        compiler_params=params(56),
        cost_estimate=pl.CostEstimate(
            flops=flops,
            bytes_accessed=block_cols * (depth + (1 + bool(extra)) * (panel + front_rows)),
            transcendentals=0,
        ),
    )(q_high, q_low, targets, *extra, *turned, *pieces, *tokens)


def shards(children, row_map, column_map, staircase):
    n_rt, n_ct = lax.axis_size("rt"), lax.axis_size("ct")
    my_rt, my_ct = lax.axis_index("rt"), lax.axis_index("ct")
    src, child_cols = children.shape
    total_rows = row_map.shape[0]
    child_rows = total_rows // 2
    front_rows = total_rows // n_rt
    tile_cols = child_cols // staircase.shape[1]
    n_dev = n_rt * n_ct

    first_row = (my_rt * n_ct + my_ct) * src
    which = first_row // child_rows
    first_within = first_row - which * child_rows
    cmap = lax.dynamic_index_in_dim(column_map, which, 0, keepdims=False)
    stairs = lax.dynamic_index_in_dim(staircase, which, 0, keepdims=False)
    limits = jnp.broadcast_to(stairs[:, None], (stairs.shape[0], tile_cols)).reshape(-1)

    edges = STEP * jnp.arange(FRONT_COLS // STEP, dtype=jnp.int32)
    starts = jnp.sum((cmap[None, :] < edges[:, None]).astype(jnp.int32), axis=1)
    starts = jnp.minimum(starts // LANES, (child_cols - STEP - LANES) // LANES)
    info = jnp.concatenate([starts, my_ct[None], first_within[None]]).astype(jnp.int32)
    two, eight = n_ct // 2, n_ct // 8
    near = list(range(1, two))
    near = [near[: -2 * eight], near[-2 * eight : -eight], near[-eight:]]
    far = [list(range(two + k * eight, two + (k + 1) * eight)) for k in range(4)]
    order = [0] + near[0] + near[1] + far[0] + near[2] + far[1] + far[2] + far[3]
    spread = functools.partial(widen, info, children, cmap[None, :], limits[None, :], n_ct=n_ct)
    blocks, mark = spread([0] + near[0] + far[0], tokens=[])

    within = first_within + jnp.arange(src, dtype=jnp.int32)
    panel = jnp.where(within[:, None] < limits[None, :PANEL], children[:, :PANEL], 0.0)
    ct_bits, rt_bits = bits_down(n_ct, 1), bits_down(n_rt, 2)
    steps = [(0, bit) for bit in ct_bits[:-1]] + [(bit, 0) for bit in rt_bits[:-1]]

    rt_order = combos(rt_bits)
    rt_order = rt_order + [r ^ 1 for r in rt_order]
    sources = (my_rt ^ np.array(rt_order, np.int32))[None, :] * n_ct + (
        my_ct ^ np.array(order, np.int32)
    )[:, None]
    targets = row_map.reshape(n_dev, src)[sources.reshape(-1)] - my_rt * front_rows
    targets = targets.reshape(n_ct, 1, n_rt * src)
    flat_targets = targets.reshape(1, total_rows)

    arrived = {0: blocks[0]}

    def over_ct(group, tokens):
        for d, x in zip(group, gate([blocks[d] for d in group], tokens)):
            arrived[d] = swap(x, 0, d)
        return [arrived[d] for d in group]

    def over_rt(bundle, tokens):
        parts = [arrived[d] for d in bundle]
        mine = [join(parts, tokens)[0]] if len(parts) > 1 else list(gate(parts, tokens))
        for bit in rt_bits:
            mine = mine + [swap(x, bit, 0) for x in mine]
        return mine

    for n, (rt_bit, ct_bit) in enumerate(steps):
        last = n == len(steps) - 1
        parts = [panel, swap(panel, rt_bit, ct_bit)]
        panel, mark = join(parts, [mark] if n == 0 else done if last else [], 2 if last else 1)
        if n == 0:
            over_ct(far[0], [mark])
            done = over_ct(near[0], [mark])
            own = over_rt([0], [mark])
            more, after = spread(near[1] + near[2] + far[1] + far[2] + far[3], tokens=[mark])
            blocks |= more
            done = done + own[1:] + [after]
    left, right = panel
    over_ct(near[1], [mark])
    left, mark = join([left, swap(left, rt_bits[-1], 0)], [arrived[d] for d in far[0]])
    right, after = join([right, swap(right, 0, ct_bits[-1])])
    over_ct(far[1], [mark, after])
    left_other, right_other = swap(left, 0, ct_bits[-1]), swap(right, rt_bits[-1], 0)
    panel, gram, mark = gram_of(
        left, left_other, right, right_other, [arrived[d] for d in near[1]]
    )
    other_gram, other_panel = swap(gram, 1, 0), swap(panel, 1, 0)
    over_ct(far[2], [mark])
    over_ct(near[2], [mark])
    first = over_rt(near[0] + near[1] + far[0], [mark])
    inverse, mark = inverse_factor(gram, other_gram, [first[0], other_panel])
    joined_first, mark = join(
        own + first, [mark] + [arrived[d] for d in near[2] + far[1] + far[2]]
    )
    other_first = swap(joined_first, 1, 0)
    over_ct(far[3], [mark])
    second = over_rt(near[2] + far[1], [mark])
    inverse = [inverse]
    half = n_rt // 2
    q_high, q_low, basis, turned_high, turned_low = basis_rows(
        inverse,
        panel.reshape(2, half, n_ct // 2, src, PANEL),
        other_panel.reshape(2, half, n_ct // 2, src, PANEL),
        targets,
        second[:1] + [mark],
        front_rows,
        order,
    )

    size, rest = src * half, first[0].shape[0]
    first_spots = [(side, n * src) for side in range(2) for n in range(half)]
    first_spots += [
        (side, size + n * rest + k * src)
        for k in range(rest // src)
        for side in range(2)
        for n in range(half)
    ]

    def pair_spots(joined, count):
        height = joined.shape[0] // half
        return tuple(
            (side, n * height + k * src) for k in range(count) for side in range(2) for n in range(half)
        )

    call = functools.partial(mix_call, q_high=q_high, q_low=q_low, targets=flat_targets, src=src, front_rows=front_rows)
    waited = list(gate([arrived[d] for d in far[3]] + second[1:], [basis]))
    for d in far[3]:
        arrived[d] = waited.pop(0)
    joined_second, mark = join(second[:1] + waited)
    other_second = swap(joined_second, 1, 0)
    third, fourth = over_rt(far[2], [mark]), over_rt(far[3], [mark])
    state = call(
        first_kernel,
        0,
        (),
        (),
        (joined_first, other_first),
        tuple(first_spots),
        tokens=[third[0], fourth[0], mark],
    )
    waited = list(gate([other_second] + third[1:], [state[0]]))
    other_second, third = waited[0], third[:1] + waited[1:]
    joined_third, mark = join(third + fourth[:1])
    other_third = swap(joined_third, 1, 0)
    state = call(
        more_kernel,
        2,
        tuple(state),
        (),
        (joined_second, other_second),
        pair_spots(joined_second, 2 * eight),
        tokens=[mark],
    )
    fourth = list(gate(fourth[1:], [state[0]]))
    mine = [joined_third] + fourth
    arrays = tuple(mine + [other_third] + [swap(x, 1, 0) for x in fourth])
    height = eight * src
    spots = [
        (side * len(mine), n * height + k * src)
        for k in range(eight)
        for side in range(2)
        for n in range(half)
    ]
    spots += [
        (side * len(mine) + n, (half * height if n == 0 else 0) + k * src)
        for k in range(eight)
        for side in range(2)
        for n in range(half)
    ]
    factor, remainder = call(
        last_kernel, 3, tuple(state), (turned_high, turned_low), arrays, tuple(spots), tokens=[]
    )
    return factor, basis, remainder


def solution(mesh):
    placed = (P(("rt", "ct"), None), P(), P(), P())
    return jax.shard_map(
        shards,
        mesh=mesh,
        in_specs=placed,
        out_specs=(P(None, "ct"), P(None, "rt"), P("rt", "ct")),
        check_vma=False,
    )
```

time: 304 us -> 201 us (0.66)
  waiting for transfers between devices: 133 us -> 36.4 us
  starting transfers between devices: 30.2 us -> 25.9 us
  Pallas kernels: 114 us -> 118 us
  matrix products: 3.52 us -> 0 us
    ppermute x10 -> x11, waiting for transfers between devices: 80.5 us -> 20.7 us  [swap(): return lax.ppermute(x, 'ct', [(c, c ^ ct_bit) for c in range(n_ct)])]
    ppermute x27 -> x13, waiting for transfers between devices: 52.8 us -> 15.7 us  [swap(): return lax.ppermute(x, 'rt', [(r, r ^ rt_bit) for r in range(n_rt)])]
    pallas_call x5 -> x28, Pallas kernels: 98.3 us -> 105 us  [the longest x3 40.1 us: mix_call(): pl.pallas_call(functools.partial(kernel, len(pieces), spots, src), grid=(...]
    ppermute x27 -> x13, starting transfers between devices: 12.6 us -> 8.44 us  [swap(): return lax.ppermute(x, 'rt', [(r, r ^ rt_bit) for r in range(n_rt)])]
    unnamed x85 -> x64, local copies, waits for them, and re-layouts: 14.1 us -> 10.4 us
    pallas_call x1 -> x2, Pallas kernels: 16.2 us -> 12.6 us  [widen(): pl.pallas_call(functools.partial(widen_kernel, block_cols // STEP, window...]
    dot_general x1 -> x0, matrix products: 3.52 us -> none  [dot_tn(): lax.dot_general(a, b, (((0,), (0,)), ((), ())), precision=precision, pref...]
    ppermute x10 -> x11, starting transfers between devices: 17.6 us -> 17.5 us  [swap(): return lax.ppermute(x, 'ct', [(c, c ^ ct_bit) for c in range(n_ct)])]
  transfers between devices with their start and end apart: 37 -> 24, of which waited for: 14 -> 10; matrix products, arithmetic and copies ran while one was open for 2% -> 2% of each run, Pallas kernels for 32% -> 47%
where the time goes in v2:
time: 201 us; the launch traced here: 197 us
  Pallas kernels  118 us (59%)
  waiting for transfers between devices  36.4 us (18%)
  starting transfers between devices  25.9 us (13%)
  local copies, waits for them, and re-layouts  14 us (7%)
  other arithmetic  2.31 us (1%)
    pallas_call x3, Pallas kernels, mix_call(): pl.pallas_call(functools.partial(kernel, len(pieces), spots, src), grid=(...  40.1 us
    pallas_call x1, Pallas kernels, inverse_factor(): pl.pallas_call(factor_kernel, out_shape=[jax.ShapeDtypeStruct((n, n), F32...  29.9 us
    ppermute x11, waiting for transfers between devices, swap(): return lax.ppermute(x, 'ct', [(c, c ^ ct_bit) for c in range(n_ct)])  20.7 us
    ppermute x11, starting transfers between devices, swap(): return lax.ppermute(x, 'ct', [(c, c ^ ct_bit) for c in range(n_ct)])  17.5 us
    pallas_call x1, Pallas kernels, basis_rows(): pl.pallas_call(functools.partial(basis_kernel, len(inverse), len(tokens))...  15.8 us
    ppermute x13, waiting for transfers between devices, swap(): return lax.ppermute(x, 'rt', [(r, r ^ rt_bit) for r in range(n_rt)])  15.7 us
    pallas_call x9, Pallas kernels, join(): pl.pallas_call(functools.partial(join_kernel, len(parts), cut), out_shape...  15.3 us
    pallas_call x2, Pallas kernels, widen(): pl.pallas_call(functools.partial(widen_kernel, block_cols // STEP, window...  12.6 us
  transfers between devices with their start and end apart: 24, of which 10 were waited for; matrix products, arithmetic and copies ran while one was open for 2% of the time, Pallas kernels for 47%

profile of v2, /device:TPU:0, one launch (start us, length us, event | category | flops | bytes accessed | tf_op | source)
XLA Modules:
  0.0 197.4 jit_solution(1850238925410163007)
XLA Ops:
  2.5 4.1 %collective-permute-start = (f32[64,512]{1,0:T(8,128)S(1)}, f32[64,512]{1,0:T(8,128)S(1)}, u32[]{:S(2)}, u32[]{:S(2)}) collective-permute-start(f32[64,512]{1,0:T(8,128)S(1)} %slice_select_fusion.refs_0_), channel_id=1, source_target_pairs={{0,4},{1,5},{2,6},{3,7},{4,0},{5,1},{6,2},{7,3},{8,12},{9,13},{10,... | collective-permute-start | bytes 393224 | tf_op jit(solution)/shard_map/ppermute | solution.py:28
  9.3 5.4 %shard_map.85 = (f32[64,2048]{1,0:T(8,128)}, f32[64,2048]{1,0:T(8,128)}, f32[64,2048]{1,0:T(8,128)}, f32[8,128]{1,0:T(8,128)}) custom-call(s32[66]{0:T(128)} %pad_add_fusion.info, f32[64,12288]{1,0:T(8,128)} %child.3, s32[1,12288]{1,0:T(1,128)} %copy-done.26, s32[1,12288]{1,0:T(1,128)} %bitcast.19), custom_call_target="tpu_custom_call" | custom-call | flops 603979776 | bytes 4718592 | tf_op jit(solution)/shard_map/pallas_call | solution.py:106
  21.3 7.3 %shard_map.89 = (f32[64,2048]{1,0:T(8,128)}, f32[64,2048]{1,0:T(8,128)}, f32[64,2048]{1,0:T(8,128)}, f32[64,2048]{1,0:T(8,128)}, f32[64,2048]{1,0:T(8,128)}, /*index=5*/f32[8,128]{1,0:T(8,128)}) custom-call(s32[66]{0:T(128)} %pad_add_fusion.info, f32[64,12288]{1,0:T(8,128)} %child.3, s32[1,12288]{1,0:T(1,128)} %copy-done.26, s32[1,12288]{1,0:T(1,128)} %bitcast.20, ...), custom_call_target="tpu_custom_call" | custom-call | flops 1006632960 | bytes 5767168 | tf_op jit(solution)/shard_map/pallas_call | solution.py:106
  35.7 3.0 %collective-permute-done.7.refs_1_ = f32[256,256]{1,0:T(8,128)S(1)} collective-permute-done((f32[256,256]{1,0:T(8,128)S(1)}, f32[256,256]{1,0:T(8,128)S(1)}, u32[]{:S(2)}, u32[]{:S(2)}) %collective-permute-start.7) | collective-permute-done | bytes 262176 | tf_op jit(solution)/shard_map/ppermute | solution.py:28
  40.3 5.3 %collective-permute-done.5.refs_2_ = f32[64,2048]{1,0:T(8,128)S(1)} collective-permute-done((f32[64,2048]{1,0:T(8,128)}, f32[64,2048]{1,0:T(8,128)S(1)}, u32[]{:S(2)}, u32[]{:S(2)}) %collective-permute-start.5) | collective-permute-done | bytes 524320 | tf_op jit(solution)/shard_map/ppermute | solution.py:28
  46.8 6.7 %collective-permute-done.9.refs_0_.refs_1_ = f32[64,2048]{1,0:T(8,128)S(1)} collective-permute-done((f32[64,2048]{1,0:T(8,128)}, f32[64,2048]{1,0:T(8,128)S(1)}, u32[]{:S(2)}, u32[]{:S(2)}) %collective-permute-start.9) | collective-permute-done | bytes 524320 | tf_op jit(solution)/shard_map/ppermute | solution.py:28
  53.5 4.4 %collective-permute-done.6.a_other = f32[512,256]{1,0:T(8,128)S(1)} collective-permute-done((f32[512,256]{1,0:T(8,128)S(1)}, f32[512,256]{1,0:T(8,128)S(1)}, u32[]{:S(2)}, u32[]{:S(2)}) %collective-permute-start.6) | collective-permute-done | bytes 524320 | tf_op jit(solution)/shard_map/ppermute | solution.py:28
  57.9 3.9 %shard_map.95 = (f32[1024,512]{1,0:T(8,128)}, f32[512,512]{1,0:T(8,128)S(1)}, f32[8,128]{1,0:T(8,128)S(1)}) custom-call(f32[512,256]{1,0:T(8,128)S(1)} %get-tuple-element.58.a_mine, f32[512,256]{1,0:T(8,128)S(1)} %collective-permute-done.6.a_other, f32[512,256]{1,0:T(8,128)S(1)} %get-tuple-element.60.b_mine, f32[512,256]{1,0:T(8,128)S(1)} %collective-permute-done.8.b_other, ...), custom_call_target="tpu_custom_call" | custom-call | flops 536870912 | bytes 524288 | tf_op jit(solution)/shard_map/pallas_call | solution.py:300
  63.0 3.1 %collective-permute-start.12 = (f32[64,2048]{1,0:T(8,128)}, f32[64,2048]{1,0:T(8,128)S(1)}, u32[]{:S(2)}, u32[]{:S(2)}) collective-permute-start(f32[64,2048]{1,0:T(8,128)} %shard_map.98), channel_id=1, source_target_pairs={{0,3},{1,2},{2,1},{3,0},{4,7},{5,6},{6,5},{7,4},{8,11},{9,10},{10,... | collective-permute-start | bytes 1572872 | tf_op jit(solution)/shard_map/ppermute | solution.py:28
  66.1 2.2 %collective-permute-start.15 = (f32[64,2048]{1,0:T(8,128)}, f32[64,2048]{1,0:T(8,128)S(1)}, u32[]{:S(2)}, u32[]{:S(2)}) collective-permute-start(f32[64,2048]{1,0:T(8,128)} %shard_map.100), channel_id=1, source_target_pairs={{0,6},{1,7},{2,4},{3,5},{4,2},{5,3},{6,0},{7,1},{8,14},{9,15},{10,... | collective-permute-start | bytes 1572872 | tf_op jit(solution)/shard_map/ppermute | solution.py:28
  68.2 2.7 %shard_map.96 = (f32[192,2048]{1,0:T(8,128)}, f32[8,128]{1,0:T(8,128)}) custom-call(f32[64,2048]{1,0:T(8,128)} %copy-done.3, f32[64,2048]{1,0:T(8,128)} %copy-done.4, f32[64,2048]{1,0:T(8,128)} %copy-done.5, f32[8,128]{1,0:T(8,128)} %copy-done.6), custom_call_target="tpu_custom_call" | custom-call | bytes 3145728 | tf_op jit(solution)/shard_map/pallas_call | solution.py:271
  71.5 29.9 %shard_map.97 = (f32[512,512]{1,0:T(8,128)}, f32[8,128]{1,0:T(8,128)}) custom-call(f32[512,512]{1,0:T(8,128)} %copy-done.13, f32[512,512]{1,0:T(8,128)} %collective-permute-done.10.gram_b, f32[192,2048]{1,0:T(8,128)} %get-tuple-element.65.refs_0_.refs_2_, f32[1024,512]{1,0:T(8,128)} %collective-permute-done.11.refs_1_), custom_call_target="tpu_custom_call" | custom-call | flops 30000001024 | bytes 3145728 | tf_op jit(solution)/shard_map/pallas_call | solution.py:222
  101.4 5.1 %collective-permute-done.14.refs_3_ = f32[192,2048]{1,0:T(8,128)S(1)} collective-permute-done((f32[192,2048]{1,0:T(8,128)}, f32[192,2048]{1,0:T(8,128)S(1)}, u32[]{:S(2)}, u32[]{:S(2)}) %collective-permute-start.14) | collective-permute-done | bytes 1572896 | tf_op jit(solution)/shard_map/ppermute | solution.py:30
  107.7 4.5 %shard_map.101 = (f32[512,2048]{1,0:T(8,128)}, f32[8,128]{1,0:T(8,128)}) custom-call(f32[64,2048]{1,0:T(8,128)} %shard_map.88.refs_0_, f32[64,2048]{1,0:T(8,128)} %copy-done.2, f32[192,2048]{1,0:T(8,128)} %get-tuple-element.65.refs_0_.refs_2_, f32[192,2048]{1,0:T(8,128)} %copy-done.23, f32[8,128]{1,0:T(8,128)} %get-tuple-element.72.refs_4_, ...), custom_call_target="tpu_custom_call" | custom-call | bytes 8388608 | tf_op jit(solution)/shard_map/pallas_call | solution.py:271
  112.3 2.3 %shard_map.102 = (f32[128,2048]{1,0:T(8,128)}, f32[8,128]{1,0:T(8,128)}) custom-call(f32[64,2048]{1,0:T(8,128)} %copy-done.21, f32[64,2048]{1,0:T(8,128)} %copy-done.20, f32[8,128]{1,0:T(8,128)} %get-tuple-element.74.refs_2_.refs_5_.refs_1_), custom_call_target="tpu_custom_call" | custom-call | bytes 2097152 | tf_op jit(solution)/shard_map/pallas_call | solution.py:271
  116.0 1.7 collective-permute-start.17
  118.3 15.8 %shard_map.103 = (bf16[512,2048]{1,0:T(8,128)(2,1)}, bf16[512,2048]{1,0:T(8,128)(2,1)}, f32[512,512]{1,0:T(8,128)}, bf16[512,512]{1,0:T(8,128)(2,1)}, bf16[512,512]{1,0:T(8,128)(2,1)}) custom-call(f32[512,512]{1,0:T(8,128)} %get-tuple-element.67.refs_0_, f32[2,2,4,64,512]{4,3,2,1,0:T(8,128)} %bitcast.5.refs_1_, f32[2,2,4,64,512]{4,3,2,1,0:T(8,128)} %bitcast.6.refs_2_, ...), custom_call_target="tpu_custom_call" | custom-call | flops 4294967296 | bytes 6291456 | tf_op jit(solution)/shard_map/pallas_call | solution.py:363
  134.2 6.2 %collective-permute-done.18.refs_1_ = f32[128,2048]{1,0:T(8,128)S(1)} collective-permute-done((f32[128,2048]{1,0:T(8,128)}, f32[128,2048]{1,0:T(8,128)S(1)}, u32[]{:S(2)}, u32[]{:S(2)}) %collective-permute-start.18) | collective-permute-done | bytes 1048608 | tf_op jit(solution)/shard_map/ppermute | solution.py:30
  141.3 3.0 %shard_map.106 = (f32[256,2048]{1,0:T(8,128)}, f32[8,128]{1,0:T(8,128)}) custom-call(f32[128,2048]{1,0:T(8,128)} %get-tuple-element.75.refs_4_.refs_0_, f32[128,2048]{1,0:T(8,128)} %get-tuple-element.81.refs_1_), custom_call_target="tpu_custom_call" | custom-call | bytes 4194304 | tf_op jit(solution)/shard_map/pallas_call | solution.py:271
  145.6 15.0 %shard_map.109 = (f32[512,2048]{1,0:T(8,128)}, f32[512,2048]{1,0:T(8,128)}) custom-call(bf16[512,2048]{1,0:T(8,128)(2,1)} %get-tuple-element.76.q_high, bf16[512,2048]{1,0:T(8,128)(2,1)} %get-tuple-element.77.q_low, s32[1,2048]{1,0:T(1,128)} %sub.45.targets, f32[512,2048]{1,0:T(8,128)} %get-tuple-element.78.refs_0_, ...), custom_call_target="tpu_custom_call" | custom-call | flops 5368709120 | bytes 4194304 | tf_op jit(solution)/shard_map/pallas_call | solution.py:442
  162.1 2.7 %shard_map.111 = (f32[192,2048]{1,0:T(8,128)}, f32[8,128]{1,0:T(8,128)}) custom-call(f32[64,2048]{1,0:T(8,128)} %shard_map.107.refs_2_.refs_0_, f32[64,2048]{1,0:T(8,128)} %get-tuple-element.88.refs_1_, f32[64,2048]{1,0:T(8,128)} %shard_map.108.refs_3_.refs_2_), custom_call_target="tpu_custom_call" | custom-call | bytes 3145728 | tf_op jit(solution)/shard_map/pallas_call | solution.py:271
  166.5 11.3 %shard_map.112 = (f32[512,2048]{1,0:T(8,128)}, f32[512,2048]{1,0:T(8,128)}) custom-call(bf16[512,2048]{1,0:T(8,128)(2,1)} %get-tuple-element.76.q_high, bf16[512,2048]{1,0:T(8,128)(2,1)} %get-tuple-element.77.q_low, s32[1,2048]{1,0:T(1,128)} %sub.45.targets, f32[512,2048]{1,0:T(8,128)} %get-tuple-element.84.refs_2_.factor_in, ...), custom_call_target="tpu_custom_call" | custom-call | flops 2684354560 | bytes 5242880 | tf_op jit(solution)/shard_map/pallas_call | solution.py:442
  179.9 2.1 %collective-permute-done.23.refs_3_ = f32[64,2048]{1,0:T(8,128)S(1)} collective-permute-done((f32[64,2048]{1,0:T(8,128)}, f32[64,2048]{1,0:T(8,128)S(1)}, u32[]{:S(2)}, u32[]{:S(2)}) %collective-permute-start.23) | collective-permute-done | bytes 524320 | tf_op jit(solution)/shard_map/ppermute | solution.py:30
  183.4 13.8 %shard_map.114 = (f32[512,2048]{1,0:T(8,128)}, f32[512,2048]{1,0:T(8,128)}) custom-call(bf16[512,2048]{1,0:T(8,128)(2,1)} %get-tuple-element.76.q_high, bf16[512,2048]{1,0:T(8,128)(2,1)} %get-tuple-element.77.q_low, s32[1,2048]{1,0:T(1,128)} %sub.45.targets, f32[512,2048]{1,0:T(8,128)} %get-tuple-element.90.refs_1_.factor_in, ...), custom_call_target="tpu_custom_call" | custom-call | flops 4294967296 | bytes 5242880 | tf_op jit(solution)/shard_map/pallas_call | solution.py:442
  (139 shorter events, 34.8 us)
Async XLA Ops:
  2.5 12.2 %collective-permute-start = (f32[64,512]{1,0:T(8,128)S(1)}, f32[64,512]{1,0:T(8,128)S(1)}, u32[]{:S(2)}, u32[]{:S(2)}) collective-permute-start(f32[64,512]{1,0:T(8,128)S(1)} %slice_select_fusion.refs_0_), channel_id=1, source_target_pairs={{0,4},{1,5},{2,6},{3,7},{4,0},{5,1},{6,2},{7,3},{8,12},{9,13},{10,... | collective-permute-start | bytes 393224 | tf_op jit(solution)/shard_map/ppermute | solution.py:28
  16.0 14.0 %collective-permute-start.2 = (f32[64,2048]{1,0:T(8,128)}, f32[64,2048]{1,0:T(8,128)S(1)}, u32[]{:S(2)}, u32[]{:S(2)}) collective-permute-start(f32[64,2048]{1,0:T(8,128)} %shard_map.87), channel_id=1, source_target_pairs={{0,1},{1,0},{2,3},{3,2},{4,5},{5,4},{6,7},{7,6},{8,9},{9,8},{10,11... | collective-permute-start | bytes 1572872 | tf_op jit(solution)/shard_map/ppermute | solution.py:28
  17.5 13.3 %collective-permute-start.3 = (f32[64,2048]{1,0:T(8,128)}, f32[64,2048]{1,0:T(8,128)S(1)}, u32[]{:S(2)}, u32[]{:S(2)}) collective-permute-start(f32[64,2048]{1,0:T(8,128)} %shard_map.88.refs_0_), channel_id=1, source_target_pairs={{0,16},{8,24},{16,0},{24,8},{1,17},{9,25},{17,1},{25,9},{2,18},{10... | collective-permute-start | bytes 1572872 | tf_op jit(solution)/shard_map/ppermute | solution.py:30
  18.9 11.0 %collective-permute-start.1 = (f32[128,512]{1,0:T(8,128)S(1)}, f32[128,512]{1,0:T(8,128)S(1)}, u32[]{:S(2)}, u32[]{:S(2)}) collective-permute-start(f32[128,512]{1,0:T(8,128)S(1)} %get-tuple-element.51.refs_0_), channel_id=1, source_target_pairs={{0,2},{1,3},{2,0},{3,1},{4,6},{5,7},{6,4},{7,5},{8,10},{9,11},{10,... | collective-permute-start | bytes 786440 | tf_op jit(solution)/shard_map/ppermute | solution.py:28
  20.5 25.0 %collective-permute-start.5 = (f32[64,2048]{1,0:T(8,128)}, f32[64,2048]{1,0:T(8,128)S(1)}, u32[]{:S(2)}, u32[]{:S(2)}) collective-permute-start(f32[64,2048]{1,0:T(8,128)} %shard_map.91), channel_id=1, source_target_pairs={{0,4},{1,5},{2,6},{3,7},{4,0},{5,1},{6,2},{7,3},{8,12},{9,13},{10,... | collective-permute-start | bytes 1572872 | tf_op jit(solution)/shard_map/ppermute | solution.py:28
  32.1 6.6 %collective-permute-start.7 = (f32[256,256]{1,0:T(8,128)S(1)}, f32[256,256]{1,0:T(8,128)S(1)}, u32[]{:S(2)}, u32[]{:S(2)}) collective-permute-start(f32[256,256]{1,0:T(8,128)S(1)} %get-tuple-element.59.refs_0_), channel_id=1, source_target_pairs={{0,1},{1,0},{2,3},{3,2},{4,5},{5,4},{6,7},{7,6},{8,9},{9,8},{10,11... | collective-permute-start | bytes 786440 | tf_op jit(solution)/shard_map/ppermute | solution.py:28
  32.6 13.0 %collective-permute-start.4 = (f32[256,256]{1,0:T(8,128)S(1)}, f32[256,256]{1,0:T(8,128)S(1)}, u32[]{:S(2)}, u32[]{:S(2)}) collective-permute-start(f32[256,256]{1,0:T(8,128)S(1)} %get-tuple-element.56.refs_0_), channel_id=1, source_target_pairs={{0,16},{8,24},{16,0},{24,8},{1,17},{9,25},{17,1},{25,9},{2,18},{10... | collective-permute-start | bytes 786440 | tf_op jit(solution)/shard_map/ppermute | solution.py:30
  34.1 19.4 %collective-permute-start.9 = (f32[64,2048]{1,0:T(8,128)}, f32[64,2048]{1,0:T(8,128)S(1)}, u32[]{:S(2)}, u32[]{:S(2)}) collective-permute-start(f32[64,2048]{1,0:T(8,128)} %shard_map.94), channel_id=1, source_target_pairs={{0,2},{1,3},{2,0},{3,1},{4,6},{5,7},{6,4},{7,5},{8,10},{9,11},{10,... | collective-permute-start | bytes 1572872 | tf_op jit(solution)/shard_map/ppermute | solution.py:28
  38.7 14.8 %collective-permute-start.8 = (f32[512,256]{1,0:T(8,128)S(1)}, f32[512,256]{1,0:T(8,128)S(1)}, u32[]{:S(2)}, u32[]{:S(2)}) collective-permute-start(f32[512,256]{1,0:T(8,128)S(1)} %get-tuple-element.60.b_mine), channel_id=1, source_target_pairs={{0,16},{8,24},{16,0},{24,8},{1,17},{9,25},{17,1},{25,9},{2,18},{10... | collective-permute-start | bytes 1572872 | tf_op jit(solution)/shard_map/ppermute | solution.py:30
  46.3 11.6 %collective-permute-start.6 = (f32[512,256]{1,0:T(8,128)S(1)}, f32[512,256]{1,0:T(8,128)S(1)}, u32[]{:S(2)}, u32[]{:S(2)}) collective-permute-start(f32[512,256]{1,0:T(8,128)S(1)} %get-tuple-element.58.a_mine), channel_id=1, source_target_pairs={{0,1},{1,0},{2,3},{3,2},{4,5},{5,4},{6,7},{7,6},{8,9},{9,8},{10,11... | collective-permute-start | bytes 1572872 | tf_op jit(solution)/shard_map/ppermute | solution.py:28
  62.4 9.0 %collective-permute-start.11 = (f32[1024,512]{1,0:T(8,128)}, f32[1024,512]{1,0:T(8,128)}, u32[]{:S(2)}, u32[]{:S(2)}) collective-permute-start(f32[1024,512]{1,0:T(8,128)} %get-tuple-element.66), channel_id=1, source_target_pairs={{0,8},{8,0},{16,24},{24,16},{1,9},{9,1},{17,25},{25,17},{2,10},{10... | collective-permute-start | bytes 6291464 | tf_op jit(solution)/shard_map/ppermute | solution.py:30
  62.4 8.5 %collective-permute-start.10 = (f32[512,512]{1,0:T(8,128)S(1)}, f32[512,512]{1,0:T(8,128)}, u32[]{:S(2)}, u32[]{:S(2)}) collective-permute-start(f32[512,512]{1,0:T(8,128)S(1)} %get-tuple-element.63.gram_a), channel_id=1, source_target_pairs={{0,8},{8,0},{16,24},{24,16},{1,9},{9,1},{17,25},{25,17},{2,10},{10... | collective-permute-start | bytes 3145736 | tf_op jit(solution)/shard_map/ppermute | solution.py:30
  62.9 38.4 %collective-permute-start.13 = (f32[64,2048]{1,0:T(8,128)}, f32[64,2048]{1,0:T(8,128)S(1)}, u32[]{:S(2)}, u32[]{:S(2)}) collective-permute-start(f32[64,2048]{1,0:T(8,128)} %shard_map.99), channel_id=1, source_target_pairs={{0,5},{1,4},{2,7},{3,6},{4,1},{5,0},{6,3},{7,2},{8,13},{9,12},{10,... | collective-permute-start | bytes 1572872 | tf_op jit(solution)/shard_map/ppermute | solution.py:28
  63.0 38.4 %collective-permute-start.12 = (f32[64,2048]{1,0:T(8,128)}, f32[64,2048]{1,0:T(8,128)S(1)}, u32[]{:S(2)}, u32[]{:S(2)}) collective-permute-start(f32[64,2048]{1,0:T(8,128)} %shard_map.98), channel_id=1, source_target_pairs={{0,3},{1,2},{2,1},{3,0},{4,7},{5,6},{6,5},{7,4},{8,11},{9,10},{10,... | collective-permute-start | bytes 1572872 | tf_op jit(solution)/shard_map/ppermute | solution.py:28
  66.1 35.3 %collective-permute-start.15 = (f32[64,2048]{1,0:T(8,128)}, f32[64,2048]{1,0:T(8,128)S(1)}, u32[]{:S(2)}, u32[]{:S(2)}) collective-permute-start(f32[64,2048]{1,0:T(8,128)} %shard_map.100), channel_id=1, source_target_pairs={{0,6},{1,7},{2,4},{3,5},{4,2},{5,3},{6,0},{7,1},{8,14},{9,15},{10,... | collective-permute-start | bytes 1572872 | tf_op jit(solution)/shard_map/ppermute | solution.py:28
  70.9 35.7 %collective-permute-start.14 = (f32[192,2048]{1,0:T(8,128)}, f32[192,2048]{1,0:T(8,128)S(1)}, u32[]{:S(2)}, u32[]{:S(2)}) collective-permute-start(f32[192,2048]{1,0:T(8,128)} %get-tuple-element.65.refs_0_.refs_2_), channel_id=1, source_target_pairs={{0,16},{8,24},{16,0},{24,8},{1,17},{9,25},{17,1},{25,9},{2,18},{10... | collective-permute-start | bytes 4718600 | tf_op jit(solution)/shard_map/ppermute | solution.py:30
  112.2 33.4 %collective-permute-start.16 = (f32[512,2048]{1,0:T(8,128)}, f32[512,2048]{1,0:T(8,128)}, u32[]{:S(2)}, u32[]{:S(2)}) collective-permute-start(f32[512,2048]{1,0:T(8,128)} %get-tuple-element.78.refs_0_), channel_id=1, source_target_pairs={{0,8},{8,0},{16,24},{24,16},{1,9},{9,1},{17,25},{25,17},{2,10},{10... | collective-permute-start | bytes 12582920 | tf_op jit(solution)/shard_map/ppermute | solution.py:30
  114.6 25.8 %collective-permute-start.18 = (f32[128,2048]{1,0:T(8,128)}, f32[128,2048]{1,0:T(8,128)S(1)}, u32[]{:S(2)}, u32[]{:S(2)}) collective-permute-start(f32[128,2048]{1,0:T(8,128)} %get-tuple-element.75.refs_4_.refs_0_), channel_id=1, source_target_pairs={{0,16},{8,24},{16,0},{24,8},{1,17},{9,25},{17,1},{25,9},{2,18},{10... | collective-permute-start | bytes 3145736 | tf_op jit(solution)/shard_map/ppermute | solution.py:30
  116.0 18.2 %collective-permute-start.17 = (f32[64,2048]{1,0:T(8,128)}, f32[64,2048]{1,0:T(8,128)S(1)}, u32[]{:S(2)}, u32[]{:S(2)}) collective-permute-start(f32[64,2048]{1,0:T(8,128)} %shard_map.104), channel_id=1, source_target_pairs={{0,7},{1,6},{2,5},{3,4},{4,3},{5,2},{6,1},{7,0},{8,15},{9,14},{10,... | collective-permute-start | bytes 1572872 | tf_op jit(solution)/shard_map/ppermute | solution.py:28
  144.3 16.3 %collective-permute-start.19 = (f32[256,2048]{1,0:T(8,128)}, f32[256,2048]{1,0:T(8,128)S(1)}, u32[]{:S(2)}, u32[]{:S(2)}) collective-permute-start(f32[256,2048]{1,0:T(8,128)} %get-tuple-element.86.refs_0_), channel_id=1, source_target_pairs={{0,8},{8,0},{16,24},{24,16},{1,9},{9,1},{17,25},{25,17},{2,10},{10... | collective-permute-start | bytes 6291464 | tf_op jit(solution)/shard_map/ppermute | solution.py:30
  144.3 16.3 %collective-permute-start.20 = (f32[64,2048]{1,0:T(8,128)}, f32[64,2048]{1,0:T(8,128)S(1)}, u32[]{:S(2)}, u32[]{:S(2)}) collective-permute-start(f32[64,2048]{1,0:T(8,128)} %shard_map.107.refs_2_.refs_0_), channel_id=1, source_target_pairs={{0,16},{8,24},{16,0},{24,8},{1,17},{9,25},{17,1},{25,9},{2,18},{10... | collective-permute-start | bytes 1572872 | tf_op jit(solution)/shard_map/ppermute | solution.py:30
  164.8 17.3 %collective-permute-start.22 = (f32[192,2048]{1,0:T(8,128)}, f32[192,2048]{1,0:T(8,128)S(1)}, u32[]{:S(2)}, u32[]{:S(2)}) collective-permute-start(f32[192,2048]{1,0:T(8,128)} %get-tuple-element.94.refs_0_), channel_id=1, source_target_pairs={{0,8},{8,0},{16,24},{24,16},{1,9},{9,1},{17,25},{25,17},{2,10},{10... | collective-permute-start | bytes 4718600 | tf_op jit(solution)/shard_map/ppermute | solution.py:30
  165.0 14.1 %collective-permute-start.21 = (f32[64,2048]{1,0:T(8,128)S(1)}, f32[64,2048]{1,0:T(8,128)S(1)}, u32[]{:S(2)}, u32[]{:S(2)}) collective-permute-start(f32[64,2048]{1,0:T(8,128)S(1)} %copy-done.17), channel_id=1, source_target_pairs={{0,16},{8,24},{16,0},{24,8},{1,17},{9,25},{17,1},{25,9},{2,18},{10... | collective-permute-start | bytes 1572872 | tf_op jit(solution)/shard_map/ppermute | solution.py:30
  179.9 2.1 %collective-permute-start.23 = (f32[64,2048]{1,0:T(8,128)}, f32[64,2048]{1,0:T(8,128)S(1)}, u32[]{:S(2)}, u32[]{:S(2)}) collective-permute-start(f32[64,2048]{1,0:T(8,128)} %shard_map.113.refs_1_), channel_id=1, source_target_pairs={{0,8},{8,0},{16,24},{24,16},{1,9},{9,1},{17,25},{25,17},{2,10},{10... | collective-permute-start | bytes 1572872 | tf_op jit(solution)/shard_map/ppermute | solution.py:30
  (30 other events, 206.5 us)

commit v3 on v2

--- a/solution.py
+++ b/solution.py
@@ -83,16 +83,22 @@
     first_row = info[info.shape[0] - 1]
     row_ids = first_row + lax.broadcasted_iota(jnp.int32, (rows, window), 0)
     col_ids = lax.broadcasted_iota(jnp.int32, (STEP, window), 0)
-    for place, out in zip(places, outs[waits:-1]):
+    made = iter(outs[waits:-1])
+    for place, cut in places:
         block = my_block ^ place
-
-        def tile(i, carry, block=block, out=out):
+        parts = [next(made) for _ in range(cut)]
+
+        def tile(i, carry, block=block, parts=parts):
             t = block * tiles + i
             cols = pl.ds(pl.multiple_of(info[t] * LANES, LANES), window)
             live = jnp.where(row_ids < limits[:, cols], child[:, cols], 0.0)
             hot = jnp.where(col_ids == cmap[:, cols] - t * STEP, 1.0, 0.0).astype(BF16)
             spread = dot_nt(jnp.concatenate(halves(live), axis=0), hot)
-            out[:, pl.ds(pl.multiple_of(i * STEP, STEP), STEP)] = spread[:rows] + spread[rows:]
+            spread = spread[:rows] + spread[rows:]
+            there = pl.ds(pl.multiple_of(i * STEP, STEP), STEP)
+            height = rows // len(parts)
+            for k, part in enumerate(parts):
+                part[:, there] = spread[k * height : (k + 1) * height]
             return carry
 
         lax.fori_loop(0, tiles, tile, 0, unroll=4)
@@ -105,18 +111,24 @@
     whole = pl.BlockSpec(memory_space=pltpu.VMEM)
     made = pl.pallas_call(
         functools.partial(widen_kernel, block_cols // STEP, window, tuple(places), len(tokens)),
-        out_shape=[jax.ShapeDtypeStruct((rows, block_cols), F32)] * len(places) + [MARK],
+        out_shape=[
+            jax.ShapeDtypeStruct((rows // cut, block_cols), F32)
+            for _, cut in places
+            for _ in range(cut)
+        ]
+        + [MARK],
         in_specs=[pl.BlockSpec(memory_space=pltpu.SMEM), whole, whole, whole]
         + [pl.BlockSpec(memory_space=pl.ANY)] * len(tokens),
-        out_specs=[whole] * len(places) + [pl.BlockSpec(memory_space=pl.ANY)],
-        compiler_params=params(56),
+        out_specs=[whole] * sum(cut for _, cut in places) + [pl.BlockSpec(memory_space=pl.ANY)],
+        compiler_params=params(63),
         cost_estimate=pl.CostEstimate(
             flops=4 * rows * window * block_cols * len(places),
             bytes_accessed=4 * rows * (width + block_cols * len(places)),
             transcendentals=0,
         ),
     )(info, child, cmap, limits, *tokens)
-    return dict(zip(places, made)), made[-1]
+    keys = [(d, k) for d, cut in places for k in range(cut)]
+    return dict(zip(keys, made)), made[-1]
 
 
 def small_inverse(tile):
@@ -229,7 +241,7 @@
             pltpu.VMEM((NB, NB), F32),
             pltpu.VMEM((NB + SUB, 2 * NB), F32),
         ],
-        compiler_params=params(56),
+        compiler_params=params(63),
         cost_estimate=pl.CostEstimate(
             flops=30 * 10**9, bytes_accessed=12 * n * n, transcendentals=0
         ),
@@ -273,7 +285,7 @@
         out_shape=[jax.ShapeDtypeStruct((rows, width // cut), F32)] * cut + [MARK],
         in_specs=[whole] * len(parts) + [pl.BlockSpec(memory_space=pl.ANY)] * len(tokens),
         out_specs=[whole] * cut + [pl.BlockSpec(memory_space=pl.ANY)],
-        compiler_params=params(16 if width == PANEL or width == PANEL // 2 else 56),
+        compiler_params=params(16 if width <= PANEL else 63),
         cost_estimate=pl.CostEstimate(
             flops=0, bytes_accessed=8 * rows * width, transcendentals=0
         ),
@@ -384,15 +396,15 @@
             pl.BlockSpec((front_rows, panel), lambda d: (0, 0)),
             pl.BlockSpec((front_rows, panel), lambda d: (0, 0)),
         ],
-        compiler_params=params(56),
+        compiler_params=params(63),
         cost_estimate=pl.CostEstimate(
             flops=8 * panel * panel * n_ct * group, bytes_accessed=6 * MIB, transcendentals=0
         ),
     )(*inverse, own, other, targets, *tokens)
 
 
-def mix(q_high, q_low, hot, pieces, spots, src):
-    rows = jnp.concatenate([pieces[n][lo : lo + src, :] for n, lo in spots], axis=0)
+def mix(q_high, q_low, hot, pieces, spots):
+    rows = jnp.concatenate([pieces[n][lo : lo + size, :] for n, lo, size in spots], axis=0)
     high, low = halves(rows)
     factor = dot(q_high[...], high) + (dot(q_low[...], high) + dot(q_high[...], low))
     return factor, dot(hot[...], high) + dot(hot[...], low)
@@ -405,24 +417,24 @@
         hot[...] = jnp.where(ids == targets[...], 1.0, 0.0).astype(BF16)
 
 
-def first_kernel(count, spots, src, q_high, q_low, targets, *refs):
+def first_kernel(count, spots, q_high, q_low, targets, *refs):
     pieces, (factor, placed, hot) = refs[:count], refs[-3:]
     build_hot(targets, hot)
-    factor[...], placed[...] = mix(q_high, q_low, hot, pieces, spots, src)
-
-
-def more_kernel(count, spots, src, q_high, q_low, targets, factor_in, placed_in, *refs):
+    factor[...], placed[...] = mix(q_high, q_low, hot, pieces, spots)
+
+
+def more_kernel(count, spots, q_high, q_low, targets, factor_in, placed_in, *refs):
     pieces, (factor, placed, hot) = refs[:count], refs[-3:]
     build_hot(targets, hot)
-    add_factor, add_placed = mix(q_high, q_low, hot, pieces, spots, src)
+    add_factor, add_placed = mix(q_high, q_low, hot, pieces, spots)
     factor[...] = factor_in[...] + add_factor
     placed[...] = placed_in[...] + add_placed
 
 
-def last_kernel(count, spots, src, q_high, q_low, targets, factor_in, placed_in, turned_high, turned_low, *refs):
+def last_kernel(count, spots, q_high, q_low, targets, factor_in, placed_in, turned_high, turned_low, *refs):
     pieces, (factor, remainder, hot) = refs[:count], refs[-3:]
     build_hot(targets, hot)
-    add_factor, add_placed = mix(q_high, q_low, hot, pieces, spots, src)
+    add_factor, add_placed = mix(q_high, q_low, hot, pieces, spots)
     total = factor_in[...] + add_factor
     factor[...] = total
     high, low = halves(total)
@@ -430,17 +442,17 @@
     remainder[...] = (placed_in[...] + add_placed) - removed
 
 
-def mix_call(kernel, group, extra, turned, pieces, spots, q_high, q_low, targets, src, front_rows, tokens):
+def mix_call(kernel, group, extra, turned, pieces, spots, q_high, q_low, targets, front_rows, tokens):
     panel = q_high.shape[0]
     block_cols = pieces[0].shape[1]
-    depth = len(spots) * src
+    depth = sum(size for _, _, size in spots)
     column = lambda j: (0, j)
     fixed = lambda j: (0, group)
     still = lambda j: (0, 0)
     flops = depth * block_cols * (3 * panel + 2 * front_rows)
     flops += 3 * panel * front_rows * block_cols if turned else 0
     return pl.pallas_call(
-        functools.partial(kernel, len(pieces), spots, src),
+        functools.partial(kernel, len(pieces), spots),
         grid=(block_cols // WIDE,),
         out_shape=[
             jax.ShapeDtypeStruct((panel, block_cols), F32),
@@ -460,7 +472,7 @@
             pl.BlockSpec((front_rows, WIDE), column),
         ],
         scratch_shapes=[pltpu.VMEM((front_rows, depth), BF16)],
-        compiler_params=params(56),
+        compiler_params=params(63),
         cost_estimate=pl.CostEstimate(
             flops=flops,
             bytes_accessed=block_cols * (depth + (1 + bool(extra)) * (panel + front_rows)),
@@ -491,17 +503,17 @@
     starts = jnp.minimum(starts // LANES, (child_cols - STEP - LANES) // LANES)
     info = jnp.concatenate([starts, my_ct[None], first_within[None]]).astype(jnp.int32)
     two, eight = n_ct // 2, n_ct // 8
-    near = list(range(1, two))
+    near = sorted(range(1, two), key=lambda d: d % 2)
     near = [near[: -2 * eight], near[-2 * eight : -eight], near[-eight:]]
     far = [list(range(two + k * eight, two + (k + 1) * eight)) for k in range(4)]
-    order = [0] + near[0] + near[1] + far[0] + near[2] + far[1] + far[2] + far[3]
+    order = [0] + near[0] + far[0] + near[1] + far[1] + near[2] + far[2] + far[3]
     spread = functools.partial(widen, info, children, cmap[None, :], limits[None, :], n_ct=n_ct)
-    blocks, mark = spread([0] + near[0] + far[0], tokens=[])
+    ones = lambda groups: [(d, 1) for group in groups for d in group]
+    blocks, mark = spread(ones([near[0]]), tokens=[])
 
     within = first_within + jnp.arange(src, dtype=jnp.int32)
     panel = jnp.where(within[:, None] < limits[None, :PANEL], children[:, :PANEL], 0.0)
     ct_bits, rt_bits = bits_down(n_ct, 1), bits_down(n_rt, 2)
-    steps = [(0, bit) for bit in ct_bits[:-1]] + [(bit, 0) for bit in rt_bits[:-1]]
 
     rt_order = combos(rt_bits)
     rt_order = rt_order + [r ^ 1 for r in rt_order]
@@ -512,126 +524,99 @@
     targets = targets.reshape(n_ct, 1, n_rt * src)
     flat_targets = targets.reshape(1, total_rows)
 
-    arrived = {0: blocks[0]}
-
-    def over_ct(group, tokens):
-        for d, x in zip(group, gate([blocks[d] for d in group], tokens)):
-            arrived[d] = swap(x, 0, d)
-        return [arrived[d] for d in group]
-
-    def over_rt(bundle, tokens):
-        parts = [arrived[d] for d in bundle]
-        mine = [join(parts, tokens)[0]] if len(parts) > 1 else list(gate(parts, tokens))
+    half = n_rt // 2
+
+    def over_ct(group, tokens, part=0):
+        operands = gate([blocks[d, part] for d in group], tokens)
+        return [swap(x, 0, d) for d, x in zip(group, operands)]
+
+    def over_rt(mine):
+        mine = [mine]
         for bit in rt_bits:
             mine = mine + [swap(x, bit, 0) for x in mine]
         return mine
 
-    for n, (rt_bit, ct_bit) in enumerate(steps):
-        last = n == len(steps) - 1
-        parts = [panel, swap(panel, rt_bit, ct_bit)]
-        panel, mark = join(parts, [mark] if n == 0 else done if last else [], 2 if last else 1)
-        if n == 0:
-            over_ct(far[0], [mark])
-            done = over_ct(near[0], [mark])
-            own = over_rt([0], [mark])
-            more, after = spread(near[1] + near[2] + far[1] + far[2] + far[3], tokens=[mark])
-            blocks |= more
-            done = done + own[1:] + [after]
-    left, right = panel
-    over_ct(near[1], [mark])
-    left, mark = join([left, swap(left, rt_bits[-1], 0)], [arrived[d] for d in far[0]])
-    right, after = join([right, swap(right, 0, ct_bits[-1])])
-    over_ct(far[1], [mark, after])
+    def one(arrays):
+        return arrays[0] if len(arrays) == 1 else join(arrays)[0]
+
+    parts = [panel] + [swap(panel, 0, bits) for bits in combos(ct_bits[:-1])[1:]]
+    for bit in rt_bits[:-1]:
+        panel, _ = join(parts)
+        parts = [panel, swap(panel, bit, 0)]
+    (left, right), mark = join(parts, [mark], cut=2)
+    near_a = over_ct(near[0], [mark])
+    later = ones([[0]] + near[1:] + far[1:]) + [(d, 2) for d in far[0]]
+    more, after = spread(later, tokens=[mark])
+    blocks |= more
+    left, mark = join([left, swap(left, rt_bits[-1], 0)], [after])
+    right, _ = join([right, swap(right, 0, ct_bits[-1])])
+    far_a = over_ct(far[0], [mark])
     left_other, right_other = swap(left, 0, ct_bits[-1]), swap(right, rt_bits[-1], 0)
-    panel, gram, mark = gram_of(
-        left, left_other, right, right_other, [arrived[d] for d in near[1]]
-    )
+    panel, gram, mark = gram_of(left, left_other, right, right_other, near_a + far_a)
     other_gram, other_panel = swap(gram, 1, 0), swap(panel, 1, 0)
-    over_ct(far[2], [mark])
-    over_ct(near[2], [mark])
-    first = over_rt(near[0] + near[1] + far[0], [mark])
-    inverse, mark = inverse_factor(gram, other_gram, [first[0], other_panel])
-    joined_first, mark = join(
-        own + first, [mark] + [arrived[d] for d in near[2] + far[1] + far[2]]
-    )
-    other_first = swap(joined_first, 1, 0)
-    over_ct(far[3], [mark])
-    second = over_rt(near[2] + far[1], [mark])
+    far_e = over_ct(far[0], [mark], 1)
+    far_b, near_b = over_ct(far[1], [mark]), over_ct(near[1], [mark])
+    joined, after = join([blocks[0, 0]] + near_a + far_a, [mark])
+    first = over_rt(joined)
+    inverse, mark = inverse_factor(gram, other_gram, [other_panel, after])
+
+    late = list(gate(first + near_b + far_e + far_b, [mark]))
+    first, late = late[:half], late[half:]
+    far_c, near_c = over_ct(far[2], late[:1]), over_ct(near[2], late[:1])
+    joined, mark = join(late[eight : 2 * eight] + late[:eight] + late[2 * eight :])
+    second = over_rt(joined)
+    first, after = join(first)
+    first = [first, swap(first, 1, 0)]
     inverse = [inverse]
-    half = n_rt // 2
     q_high, q_low, basis, turned_high, turned_low = basis_rows(
         inverse,
         panel.reshape(2, half, n_ct // 2, src, PANEL),
         other_panel.reshape(2, half, n_ct // 2, src, PANEL),
         targets,
-        second[:1] + [mark],
+        [mark, after],
         front_rows,
         order,
     )
 
-    size, rest = src * half, first[0].shape[0]
-    first_spots = [(side, n * src) for side in range(2) for n in range(half)]
-    first_spots += [
-        (side, size + n * rest + k * src)
-        for k in range(rest // src)
-        for side in range(2)
-        for n in range(half)
-    ]
-
-    def pair_spots(joined, count):
-        height = joined.shape[0] // half
-        return tuple(
-            (side, n * height + k * src) for k in range(count) for side in range(2) for n in range(half)
-        )
-
-    call = functools.partial(mix_call, q_high=q_high, q_low=q_low, targets=flat_targets, src=src, front_rows=front_rows)
-    waited = list(gate([arrived[d] for d in far[3]] + second[1:], [basis]))
-    for d in far[3]:
-        arrived[d] = waited.pop(0)
-    joined_second, mark = join(second[:1] + waited)
-    other_second = swap(joined_second, 1, 0)
-    third, fourth = over_rt(far[2], [mark]), over_rt(far[3], [mark])
-    state = call(
-        first_kernel,
-        0,
-        (),
-        (),
-        (joined_first, other_first),
-        tuple(first_spots),
-        tokens=[third[0], fourth[0], mark],
-    )
-    waited = list(gate([other_second] + third[1:], [state[0]]))
-    other_second, third = waited[0], third[:1] + waited[1:]
-    joined_third, mark = join(third + fourth[:1])
-    other_third = swap(joined_third, 1, 0)
-    state = call(
-        more_kernel,
-        2,
-        tuple(state),
-        (),
-        (joined_second, other_second),
-        pair_spots(joined_second, 2 * eight),
-        tokens=[mark],
-    )
-    fourth = list(gate(fourth[1:], [state[0]]))
-    mine = [joined_third] + fourth
-    arrays = tuple(mine + [other_third] + [swap(x, 1, 0) for x in fourth])
-    height = eight * src
-    spots = [
-        (side * len(mine), n * height + k * src)
-        for k in range(eight)
-        for side in range(2)
-        for n in range(half)
-    ]
-    spots += [
-        (side * len(mine) + n, (half * height if n == 0 else 0) + k * src)
-        for k in range(eight)
-        for side in range(2)
-        for n in range(half)
-    ]
-    factor, remainder = call(
-        last_kernel, 3, tuple(state), (turned_high, turned_low), arrays, tuple(spots), tokens=[]
-    )
+    call = functools.partial(mix_call, q_high=q_high, q_low=q_low, targets=flat_targets, front_rows=front_rows)
+    late = list(gate(second + near_c + far_c, [basis]))
+    second, late = late[:half], late[half:]
+    far_d = over_ct(far[3], late[:1])
+    third, fourth = over_rt(one(late[:eight])), over_rt(one(late[eight:]))
+    second += [swap(x, 1, 0) for x in second]
+
+    def rows_of(mine, start, size):
+        return [(mine + n, start, size) for n in range(n_rt)]
+
+    def group(bundles):
+        arrays, spots = [], []
+        for mine in bundles:
+            for row in range(0, mine[0].shape[0], src):
+                spots += rows_of(len(arrays), row, src)
+            arrays += mine
+        return tuple(arrays), tuple(spots)
+
+    part, height = src // 2, first[0].shape[0] // half
+    whole_rows = height - part * eight
+    places = [(side, n * height) for side in range(2) for n in range(half)]
+    spots = [(side, at + row, src) for row in range(0, whole_rows, src) for side, at in places]
+    for k in range(eight):
+        for n, (side, at) in enumerate(places):
+            spots += [(side, at + whole_rows + k * part, part), (2 + n, k * part, part)]
+    for row in range(part * eight, second[0].shape[0], src):
+        spots += rows_of(2, row, src)
+    arrays = tuple(first) + tuple(second)
+    state = call(first_kernel, 0, (), (), arrays, tuple(spots), tokens=late[:1])
+    late = list(gate(third + fourth + far_d, [state[0]]))
+    third, fourth, late = late[:half], late[half : 2 * half], late[2 * half :]
+    fifth = over_rt(one(late))
+    third += [swap(x, 1, 0) for x in third]
+    fourth += [swap(x, 1, 0) for x in fourth]
+    state = call(more_kernel, 5, tuple(state), (), *group((third,)), tokens=fourth[half:])
+    fifth = list(gate(fifth, [state[0]]))
+    fifth += [swap(x, 1, 0) for x in fifth]
+    turned = (turned_high, turned_low)
+    factor, remainder = call(last_kernel, 3, tuple(state), turned, *group((fourth, fifth)), tokens=[])
     return factor, basis, remainder
 
 

time: 201 us -> 190 us (0.945)
  waiting for transfers between devices: 36.4 us -> 28.2 us
  starting transfers between devices: 25.9 us -> 31.7 us
  local copies, waits for them, and re-layouts: 14 us -> 8.66 us
  Pallas kernels: 118 us -> 115 us
    ppermute x13 -> x18, waiting for transfers between devices: 15.7 us -> 6.64 us  [swap(): return lax.ppermute(x, 'rt', [(r, r ^ rt_bit) for r in range(n_rt)])]
    unnamed x64 -> x46, local copies, waits for them, and re-layouts: 10.4 us -> 5.15 us
    pallas_call x9 -> x6, Pallas kernels: 15.3 us -> 11 us  [join(): pl.pallas_call(functools.partial(join_kernel, len(parts), cut), out_shape...]
    ppermute x11 -> x13, starting transfers between devices: 17.5 us -> 21.5 us  [swap(): return lax.ppermute(x, 'ct', [(c, c ^ ct_bit) for c in range(n_ct)])]
    ppermute x13 -> x18, starting transfers between devices: 8.44 us -> 10.2 us  [swap(): return lax.ppermute(x, 'rt', [(r, r ^ rt_bit) for r in range(n_rt)])]
    ppermute x11 -> x13, waiting for transfers between devices: 20.7 us -> 21.6 us  [swap(): return lax.ppermute(x, 'ct', [(c, c ^ ct_bit) for c in range(n_ct)])]
  transfers between devices with their start and end apart: 24 -> 31, of which waited for: 10 -> 10; matrix products, arithmetic and copies ran while one was open for 2% -> 3% of each run, Pallas kernels for 47% -> 50%
where the time goes in v3:
time: 190 us; the launch traced here: 187 us
  Pallas kernels  115 us (61%)
  starting transfers between devices  31.7 us (17%)
  waiting for transfers between devices  28.2 us (15%)
  local copies, waits for them, and re-layouts  8.66 us (5%)
  other arithmetic  2.31 us (1%)
    pallas_call x3, Pallas kernels, mix_call(): pl.pallas_call(functools.partial(kernel, len(pieces), spots), grid=(block...  41.3 us
    pallas_call x1, Pallas kernels, inverse_factor(): pl.pallas_call(factor_kernel, out_shape=[jax.ShapeDtypeStruct((n, n), F32...  30 us
    ppermute x13, waiting for transfers between devices, swap(): return lax.ppermute(x, 'ct', [(c, c ^ ct_bit) for c in range(n_ct)])  21.6 us
    ppermute x13, starting transfers between devices, swap(): return lax.ppermute(x, 'ct', [(c, c ^ ct_bit) for c in range(n_ct)])  21.5 us
    pallas_call x1, Pallas kernels, basis_rows(): pl.pallas_call(functools.partial(basis_kernel, len(inverse), len(tokens))...  15.8 us
    pallas_call x2, Pallas kernels, widen(): pl.pallas_call(functools.partial(widen_kernel, block_cols // STEP, window...  12.7 us
    pallas_call x6, Pallas kernels, join(): pl.pallas_call(functools.partial(join_kernel, len(parts), cut), out_shape...  11 us
    ppermute x18, starting transfers between devices, swap(): return lax.ppermute(x, 'rt', [(r, r ^ rt_bit) for r in range(n_rt)])  10.2 us
  transfers between devices with their start and end apart: 31, of which 10 were waited for; matrix products, arithmetic and copies ran while one was open for 3% of the time, Pallas kernels for 50%

profile of v3, /device:TPU:0, one launch (start us, length us, event | category | flops | bytes accessed | tf_op | source)
XLA Modules:
  0.0 187.3 jit_solution(8941318921036455218)
XLA Ops:
  2.5 5.1 %collective-permute-start.2 = (f32[64,512]{1,0:T(8,128)S(1)}, f32[64,512]{1,0:T(8,128)S(1)}, u32[]{:S(2)}, u32[]{:S(2)}) collective-permute-start(f32[64,512]{1,0:T(8,128)S(1)} %slice_select_fusion.refs_0_), channel_id=1, source_target_pairs={{0,6},{1,7},{2,4},{3,5},{4,2},{5,3},{6,0},{7,1},{8,14},{9,15},{10,... | collective-permute-start | bytes 393224 | tf_op jit(solution)/shard_map/ppermute | solution.py:28
  10.9 3.6 %shard_map.85 = (f32[64,2048]{1,0:T(8,128)}, f32[8,128]{1,0:T(8,128)}) custom-call(s32[66]{0:T(128)} %pad_add_fusion.info, f32[64,12288]{1,0:T(8,128)} %child.3, s32[1,12288]{1,0:T(1,128)} %copy-done.17, s32[1,12288]{1,0:T(1,128)} %bitcast.19), custom_call_target="tpu_custom_call" | custom-call | flops 201326592 | bytes 3670016 | tf_op jit(solution)/shard_map/pallas_call | solution.py:112
  15.0 3.7 %collective-permute-done.refs_1_ = f32[64,512]{1,0:T(8,128)S(1)} collective-permute-done((f32[64,512]{1,0:T(8,128)S(1)}, f32[64,512]{1,0:T(8,128)S(1)}, u32[]{:S(2)}, u32[]{:S(2)}) %collective-permute-start) | collective-permute-done | bytes 131104 | tf_op jit(solution)/shard_map/ppermute | solution.py:28
  20.1 1.5 collective-permute-start.5
  23.1 9.2 %shard_map.87 = (f32[64,2048]{1,0:T(8,128)}, f32[64,2048]{1,0:T(8,128)}, f32[64,2048]{1,0:T(8,128)}, f32[64,2048]{1,0:T(8,128)}, f32[64,2048]{1,0:T(8,128)}, /*i...) custom-call(s32[66]{0:T(128)} %pad_add_fusion.info, f32[64,12288]{1,0:T(8,128)} %child.3, ...), custom_call_target="tpu_custom_call" | custom-call | flops 1409286144 | bytes 6815744 | tf_op jit(solution)/shard_map/pallas_call | solution.py:112
  36.7 3.1 %collective-permute-start.8 = (f32[32,2048]{1,0:T(8,128)}, f32[32,2048]{1,0:T(8,128)S(1)}, u32[]{:S(2)}, u32[]{:S(2)}) collective-permute-start(f32[32,2048]{1,0:T(8,128)} %shard_map.91), channel_id=1, source_target_pairs={{0,4},{1,5},{2,6},{3,7},{4,0},{5,1},{6,2},{7,3},{8,12},{9,13},{10,... | collective-permute-start | bytes 786440 | tf_op jit(solution)/shard_map/ppermute | solution.py:28
  39.8 10.0 %collective-permute-done.8.refs_1_.refs_2_ = f32[32,2048]{1,0:T(8,128)S(1)} collective-permute-done((f32[32,2048]{1,0:T(8,128)}, f32[32,2048]{1,0:T(8,128)S(1)}, u32[]{:S(2)}, u32[]{:S(2)}) %collective-permute-start.8) | collective-permute-done | bytes 262176 | tf_op jit(solution)/shard_map/ppermute | solution.py:28
  49.8 4.6 %shard_map.92 = (f32[1024,512]{1,0:T(8,128)}, f32[512,512]{1,0:T(8,128)}, f32[8,128]{1,0:T(8,128)S(1)}) custom-call(f32[512,256]{1,0:T(8,128)S(1)} %get-tuple-element.62.a_mine, f32[512,256]{1,0:T(8,128)S(1)} %collective-permute-done.4.a_other, f32[512,256]{1,0:T(8,128)S(1)} %get-tuple-element.64.b_mine, f32[512,256]{1,0:T(8,128)S(1)} %collective-permute-done.6.b_other, ...), custom_call_target="tpu_custom_call" | custom-call | flops 536870912 | bytes 524288 | tf_op jit(solution)/shard_map/pallas_call | solution.py:312
  55.0 1.5 collective-permute-start.12
  56.5 2.9 %collective-permute-start.14 = (f32[64,2048]{1,0:T(8,128)}, f32[64,2048]{1,0:T(8,128)}, u32[]{:S(2)}, u32[]{:S(2)}) collective-permute-start(f32[64,2048]{1,0:T(8,128)} %shard_map.97), channel_id=1, source_target_pairs={{0,5},{1,4},{2,7},{3,6},{4,1},{5,0},{6,3},{7,2},{8,13},{9,12},{10,... | collective-permute-start | bytes 1572872 | tf_op jit(solution)/shard_map/ppermute | solution.py:28
  59.4 2.4 %shard_map.93 = (f32[160,2048]{1,0:T(8,128)}, f32[8,128]{1,0:T(8,128)}) custom-call(f32[64,2048]{1,0:T(8,128)} %get-tuple-element.70.refs_0_, f32[64,2048]{1,0:T(8,128)} %copy-done.2, f32[32,2048]{1,0:T(8,128)} %copy-done.3, f32[8,128]{1,0:T(8,128)} %copy-done.4), custom_call_target="tpu_custom_call" | custom-call | bytes 2621440 | tf_op jit(solution)/shard_map/pallas_call | solution.py:283
  63.3 30.0 %shard_map.94 = (f32[512,512]{1,0:T(8,128)}, f32[8,128]{1,0:T(8,128)}) custom-call(f32[512,512]{1,0:T(8,128)} %get-tuple-element.68.gram_a, f32[512,512]{1,0:T(8,128)} %collective-permute-done.9.gram_b, f32[1024,512]{1,0:T(8,128)} %collective-permute-done.10.refs_0_, f32[8,128]{1,0:T(8,128)} %get-tuple-element.72.refs_1_), custom_call_target="tpu_custom_call" | custom-call | flops 30000001024 | bytes 3145728 | tf_op jit(solution)/shard_map/pallas_call | solution.py:234
  94.1 2.4 %shard_map.99 = (f32[160,2048]{1,0:T(8,128)}, f32[8,128]{1,0:T(8,128)}) custom-call(f32[32,2048]{1,0:T(8,128)} %get-tuple-element.79.refs_0_, f32[64,2048]{1,0:T(8,128)} %get-tuple-element.80.refs_1_, f32[64,2048]{1,0:T(8,128)} %get-tuple-element.81.refs_2_), custom_call_target="tpu_custom_call" | custom-call | bytes 2621440 | tf_op jit(solution)/shard_map/pallas_call | solution.py:283
  97.1 3.3 %shard_map.100 = (f32[320,2048]{1,0:T(8,128)}, f32[8,128]{1,0:T(8,128)}) custom-call(f32[160,2048]{1,0:T(8,128)} %get-tuple-element.83.refs_0_, f32[160,2048]{1,0:T(8,128)} %get-tuple-element.84.refs_1_), custom_call_target="tpu_custom_call" | custom-call | bytes 5242880 | tf_op jit(solution)/shard_map/pallas_call | solution.py:283
  101.7 2.1 %collective-permute-start.18 = (f32[64,2048]{1,0:T(8,128)}, f32[64,2048]{1,0:T(8,128)}, u32[]{:S(2)}, u32[]{:S(2)}) collective-permute-start(f32[64,2048]{1,0:T(8,128)} %shard_map.103), channel_id=1, source_target_pairs={{0,6},{1,7},{2,4},{3,5},{4,2},{5,3},{6,0},{7,1},{8,14},{9,15},{10,... | collective-permute-start | bytes 1572872 | tf_op jit(solution)/shard_map/ppermute | solution.py:28
  104.5 15.8 %shard_map.101 = (bf16[512,2048]{1,0:T(8,128)(2,1)}, bf16[512,2048]{1,0:T(8,128)(2,1)}, f32[512,512]{1,0:T(8,128)}, bf16[512,512]{1,0:T(8,128)(2,1)}, bf16[512,512]{1,0:T(8,128)(2,1)}) custom-call(f32[512,512]{1,0:T(8,128)} %get-tuple-element.73.refs_0_, f32[2,2,4,64,512]{4,3,2,1,0:T(8,128)} %bitcast.5.refs_1_, f32[2,2,4,64,512]{4,3,2,1,0:T(8,128)} %bitcast.6.refs_2_, ...), custom_call_target="tpu_custom_call" | custom-call | flops 4294967296 | bytes 6291456 | tf_op jit(solution)/shard_map/pallas_call | solution.py:375
  120.3 7.4 %collective-permute-done.18.refs_3_ = f32[64,2048]{1,0:T(8,128)} collective-permute-done((f32[64,2048]{1,0:T(8,128)}, f32[64,2048]{1,0:T(8,128)}, u32[]{:S(2)}, u32[]{:S(2)}) %collective-permute-start.18) | collective-permute-done | bytes 524320 | tf_op jit(solution)/shard_map/ppermute | solution.py:28
  128.9 1.5 collective-permute-start.21
  130.5 3.8 %collective-permute-start.23 = (f32[64,2048]{1,0:T(8,128)}, f32[64,2048]{1,0:T(8,128)S(1)}, u32[]{:S(2)}, u32[]{:S(2)}) collective-permute-start(f32[64,2048]{1,0:T(8,128)} %shard_map.106), channel_id=1, source_target_pairs={{0,7},{1,6},{2,5},{3,4},{4,3},{5,2},{6,1},{7,0},{8,15},{9,14},{10,... | collective-permute-start | bytes 1572872 | tf_op jit(solution)/shard_map/ppermute | solution.py:28
  134.7 18.5 %shard_map.105 = (f32[512,2048]{1,0:T(8,128)}, f32[512,2048]{1,0:T(8,128)}) custom-call(bf16[512,2048]{1,0:T(8,128)(2,1)} %get-tuple-element.86.q_high, bf16[512,2048]{1,0:T(8,128)(2,1)} %get-tuple-element.87.q_low, s32[1,2048]{1,0:T(1,128)} %sub.45.targets, f32[320,2048]{1,0:T(8,128)} %get-tuple-element.88.refs_0_, ...), custom_call_target="tpu_custom_call" | custom-call | flops 6710886400 | bytes 4718592 | tf_op jit(solution)/shard_map/pallas_call | solution.py:454
  155.4 1.5 collective-permute-start.28
  159.6 9.0 %shard_map.108 = (f32[512,2048]{1,0:T(8,128)}, f32[512,2048]{1,0:T(8,128)}) custom-call(bf16[512,2048]{1,0:T(8,128)(2,1)} %get-tuple-element.86.q_high, bf16[512,2048]{1,0:T(8,128)(2,1)} %get-tuple-element.87.q_low, s32[1,2048]{1,0:T(1,128)} %sub.45.targets, f32[512,2048]{1,0:T(8,128)} %get-tuple-element.96.refs_5_.factor_in, ...), custom_call_target="tpu_custom_call" | custom-call | flops 1342177280 | bytes 4718592 | tf_op jit(solution)/shard_map/pallas_call | solution.py:454
  170.2 2.3 %collective-permute-done.29.refs_6_ = f32[64,2048]{1,0:T(8,128)S(1)} collective-permute-done((f32[64,2048]{1,0:T(8,128)}, f32[64,2048]{1,0:T(8,128)S(1)}, u32[]{:S(2)}, u32[]{:S(2)}) %collective-permute-start.29) | collective-permute-done | bytes 524320 | tf_op jit(solution)/shard_map/ppermute | solution.py:30
  173.3 13.9 %shard_map.110 = (f32[512,2048]{1,0:T(8,128)}, f32[512,2048]{1,0:T(8,128)}) custom-call(bf16[512,2048]{1,0:T(8,128)(2,1)} %get-tuple-element.86.q_high, bf16[512,2048]{1,0:T(8,128)(2,1)} %get-tuple-element.87.q_low, s32[1,2048]{1,0:T(1,128)} %sub.45.targets, f32[512,2048]{1,0:T(8,128)} %get-tuple-element.104.refs_2_.factor_in, ...), custom_call_target="tpu_custom_call" | custom-call | flops 4294967296 | bytes 5242880 | tf_op jit(solution)/shard_map/pallas_call | solution.py:454
  (131 shorter events, 27.4 us)
Async XLA Ops:
  2.5 12.0 %collective-permute-start.2 = (f32[64,512]{1,0:T(8,128)S(1)}, f32[64,512]{1,0:T(8,128)S(1)}, u32[]{:S(2)}, u32[]{:S(2)}) collective-permute-start(f32[64,512]{1,0:T(8,128)S(1)} %slice_select_fusion.refs_0_), channel_id=1, source_target_pairs={{0,6},{1,7},{2,4},{3,5},{4,2},{5,3},{6,0},{7,1},{8,14},{9,15},{10,... | collective-permute-start | bytes 393224 | tf_op jit(solution)/shard_map/ppermute | solution.py:28
  7.6 7.4 %collective-permute-start.1 = (f32[64,512]{1,0:T(8,128)S(1)}, f32[64,512]{1,0:T(8,128)S(1)}, u32[]{:S(2)}, u32[]{:S(2)}) collective-permute-start(f32[64,512]{1,0:T(8,128)S(1)} %slice_select_fusion.refs_0_), channel_id=1, source_target_pairs={{0,2},{1,3},{2,0},{3,1},{4,6},{5,7},{6,4},{7,5},{8,10},{9,11},{10,... | collective-permute-start | bytes 393224 | tf_op jit(solution)/shard_map/ppermute | solution.py:28
  7.6 11.1 %collective-permute-start = (f32[64,512]{1,0:T(8,128)S(1)}, f32[64,512]{1,0:T(8,128)S(1)}, u32[]{:S(2)}, u32[]{:S(2)}) collective-permute-start(f32[64,512]{1,0:T(8,128)S(1)} %slice_select_fusion.refs_0_), channel_id=1, source_target_pairs={{0,4},{1,5},{2,6},{3,7},{4,0},{5,1},{6,2},{7,3},{8,12},{9,13},{10,... | collective-permute-start | bytes 393224 | tf_op jit(solution)/shard_map/ppermute | solution.py:28
  20.1 12.2 %collective-permute-start.5 = (f32[256,256]{1,0:T(8,128)}, f32[256,256]{1,0:T(8,128)}, u32[]{:S(2)}, u32[]{:S(2)}) collective-permute-start(f32[256,256]{1,0:T(8,128)} %get-tuple-element.63.refs_0_), channel_id=1, source_target_pairs={{0,1},{1,0},{2,3},{3,2},{4,5},{5,4},{6,7},{7,6},{8,9},{9,8},{10,11... | collective-permute-start | bytes 786440 | tf_op jit(solution)/shard_map/ppermute | solution.py:28
  21.6 12.3 %collective-permute-start.3 = (f32[256,256]{1,0:T(8,128)S(1)}, f32[256,256]{1,0:T(8,128)}, u32[]{:S(2)}, u32[]{:S(2)}) collective-permute-start(f32[256,256]{1,0:T(8,128)S(1)} %get-tuple-element.59.refs_0_), channel_id=1, source_target_pairs={{0,16},{8,24},{16,0},{24,8},{1,17},{9,25},{17,1},{25,9},{2,18},{10... | collective-permute-start | bytes 786440 | tf_op jit(solution)/shard_map/ppermute | solution.py:30
  23.1 16.7 %collective-permute-start.7 = (f32[64,2048]{1,0:T(8,128)}, f32[64,2048]{1,0:T(8,128)S(1)}, u32[]{:S(2)}, u32[]{:S(2)}) collective-permute-start(f32[64,2048]{1,0:T(8,128)} %shard_map.90), channel_id=1, source_target_pairs={{0,2},{1,3},{2,0},{3,1},{4,6},{5,7},{6,4},{7,5},{8,10},{9,11},{10,... | collective-permute-start | bytes 1572872 | tf_op jit(solution)/shard_map/ppermute | solution.py:28
  33.3 16.4 %collective-permute-start.6 = (f32[512,256]{1,0:T(8,128)S(1)}, f32[512,256]{1,0:T(8,128)S(1)}, u32[]{:S(2)}, u32[]{:S(2)}) collective-permute-start(f32[512,256]{1,0:T(8,128)S(1)} %get-tuple-element.64.b_mine), channel_id=1, source_target_pairs={{0,16},{8,24},{16,0},{24,8},{1,17},{9,25},{17,1},{25,9},{2,18},{10... | collective-permute-start | bytes 1572872 | tf_op jit(solution)/shard_map/ppermute | solution.py:30
  36.2 13.6 %collective-permute-start.4 = (f32[512,256]{1,0:T(8,128)S(1)}, f32[512,256]{1,0:T(8,128)S(1)}, u32[]{:S(2)}, u32[]{:S(2)}) collective-permute-start(f32[512,256]{1,0:T(8,128)S(1)} %get-tuple-element.62.a_mine), channel_id=1, source_target_pairs={{0,1},{1,0},{2,3},{3,2},{4,5},{5,4},{6,7},{7,6},{8,9},{9,8},{10,11... | collective-permute-start | bytes 1572872 | tf_op jit(solution)/shard_map/ppermute | solution.py:28
  36.7 13.1 %collective-permute-start.8 = (f32[32,2048]{1,0:T(8,128)}, f32[32,2048]{1,0:T(8,128)S(1)}, u32[]{:S(2)}, u32[]{:S(2)}) collective-permute-start(f32[32,2048]{1,0:T(8,128)} %shard_map.91), channel_id=1, source_target_pairs={{0,4},{1,5},{2,6},{3,7},{4,0},{5,1},{6,2},{7,3},{8,12},{9,13},{10,... | collective-permute-start | bytes 786440 | tf_op jit(solution)/shard_map/ppermute | solution.py:28
  54.4 8.9 %collective-permute-start.10 = (f32[1024,512]{1,0:T(8,128)}, f32[1024,512]{1,0:T(8,128)}, u32[]{:S(2)}, u32[]{:S(2)}) collective-permute-start(f32[1024,512]{1,0:T(8,128)} %get-tuple-element.69), channel_id=1, source_target_pairs={{0,8},{8,0},{16,24},{24,16},{1,9},{9,1},{17,25},{25,17},{2,10},{10... | collective-permute-start | bytes 6291464 | tf_op jit(solution)/shard_map/ppermute | solution.py:30
  54.4 7.5 %collective-permute-start.9 = (f32[512,512]{1,0:T(8,128)}, f32[512,512]{1,0:T(8,128)}, u32[]{:S(2)}, u32[]{:S(2)}) collective-permute-start(f32[512,512]{1,0:T(8,128)} %get-tuple-element.68.gram_a), channel_id=1, source_target_pairs={{0,8},{8,0},{16,24},{24,16},{1,9},{9,1},{17,25},{25,17},{2,10},{10... | collective-permute-start | bytes 3145736 | tf_op jit(solution)/shard_map/ppermute | solution.py:30
  55.0 38.3 %collective-permute-start.13 = (f32[32,2048]{1,0:T(8,128)}, f32[32,2048]{1,0:T(8,128)S(1)}, u32[]{:S(2)}, u32[]{:S(2)}) collective-permute-start(f32[32,2048]{1,0:T(8,128)} %shard_map.96), channel_id=1, source_target_pairs={{0,4},{1,5},{2,6},{3,7},{4,0},{5,1},{6,2},{7,3},{8,12},{9,13},{10,... | collective-permute-start | bytes 786440 | tf_op jit(solution)/shard_map/ppermute | solution.py:28
  55.0 38.2 %collective-permute-start.12 = (f32[64,2048]{1,0:T(8,128)}, f32[64,2048]{1,0:T(8,128)S(1)}, u32[]{:S(2)}, u32[]{:S(2)}) collective-permute-start(f32[64,2048]{1,0:T(8,128)} %shard_map.95), channel_id=1, source_target_pairs={{0,1},{1,0},{2,3},{3,2},{4,5},{5,4},{6,7},{7,6},{8,9},{9,8},{10,11... | collective-permute-start | bytes 1572872 | tf_op jit(solution)/shard_map/ppermute | solution.py:28
  56.5 36.7 %collective-permute-start.14 = (f32[64,2048]{1,0:T(8,128)}, f32[64,2048]{1,0:T(8,128)}, u32[]{:S(2)}, u32[]{:S(2)}) collective-permute-start(f32[64,2048]{1,0:T(8,128)} %shard_map.97), channel_id=1, source_target_pairs={{0,5},{1,4},{2,7},{3,6},{4,1},{5,0},{6,3},{7,2},{8,13},{9,12},{10,... | collective-permute-start | bytes 1572872 | tf_op jit(solution)/shard_map/ppermute | solution.py:28
  61.8 31.4 %collective-permute-start.11 = (f32[160,2048]{1,0:T(8,128)}, f32[160,2048]{1,0:T(8,128)}, u32[]{:S(2)}, u32[]{:S(2)}) collective-permute-start(f32[160,2048]{1,0:T(8,128)} %get-tuple-element.74.refs_0_), channel_id=1, source_target_pairs={{0,16},{8,24},{16,0},{24,8},{1,17},{9,25},{17,1},{25,9},{2,18},{10... | collective-permute-start | bytes 3932168 | tf_op jit(solution)/shard_map/ppermute | solution.py:30
  96.5 31.2 %collective-permute-start.16 = (f32[160,2048]{1,0:T(8,128)}, f32[160,2048]{1,0:T(8,128)}, u32[]{:S(2)}, u32[]{:S(2)}) collective-permute-start(f32[160,2048]{1,0:T(8,128)} %get-tuple-element.89.refs_0_), channel_id=1, source_target_pairs={{0,16},{8,24},{16,0},{24,8},{1,17},{9,25},{17,1},{25,9},{2,18},{10... | collective-permute-start | bytes 3932168 | tf_op jit(solution)/shard_map/ppermute | solution.py:30
  100.5 34.3 %collective-permute-start.15 = (f32[320,2048]{1,0:T(8,128)}, f32[320,2048]{1,0:T(8,128)}, u32[]{:S(2)}, u32[]{:S(2)}) collective-permute-start(f32[320,2048]{1,0:T(8,128)} %get-tuple-element.88.refs_0_), channel_id=1, source_target_pairs={{0,8},{8,0},{16,24},{24,16},{1,9},{9,1},{17,25},{25,17},{2,10},{10... | collective-permute-start | bytes 7864328 | tf_op jit(solution)/shard_map/ppermute | solution.py:30
  101.3 19.0 %collective-permute-start.17 = (f32[64,2048]{1,0:T(8,128)}, f32[64,2048]{1,0:T(8,128)S(1)}, u32[]{:S(2)}, u32[]{:S(2)}) collective-permute-start(f32[64,2048]{1,0:T(8,128)} %shard_map.102), channel_id=1, source_target_pairs={{0,3},{1,2},{2,1},{3,0},{4,7},{5,6},{6,5},{7,4},{8,11},{9,10},{10,... | collective-permute-start | bytes 1572872 | tf_op jit(solution)/shard_map/ppermute | solution.py:28
  101.7 26.0 %collective-permute-start.18 = (f32[64,2048]{1,0:T(8,128)}, f32[64,2048]{1,0:T(8,128)}, u32[]{:S(2)}, u32[]{:S(2)}) collective-permute-start(f32[64,2048]{1,0:T(8,128)} %shard_map.103), channel_id=1, source_target_pairs={{0,6},{1,7},{2,4},{3,5},{4,2},{5,3},{6,0},{7,1},{8,14},{9,15},{10,... | collective-permute-start | bytes 1572872 | tf_op jit(solution)/shard_map/ppermute | solution.py:28
  127.8 6.9 %collective-permute-start.20 = (f32[160,2048]{1,0:T(8,128)}, f32[160,2048]{1,0:T(8,128)}, u32[]{:S(2)}, u32[]{:S(2)}) collective-permute-start(f32[160,2048]{1,0:T(8,128)} %get-tuple-element.94.refs_3_), channel_id=1, source_target_pairs={{0,8},{8,0},{16,24},{24,16},{1,9},{9,1},{17,25},{25,17},{2,10},{10... | collective-permute-start | bytes 3932168 | tf_op jit(solution)/shard_map/ppermute | solution.py:30
  128.9 25.5 %collective-permute-start.21 = (f32[64,2048]{1,0:T(8,128)}, f32[64,2048]{1,0:T(8,128)}, u32[]{:S(2)}, u32[]{:S(2)}) collective-permute-start(f32[64,2048]{1,0:T(8,128)} %get-tuple-element.95.refs_6_.refs_1_.refs_0_), channel_id=1, source_target_pairs={{0,16},{8,24},{16,0},{24,8},{1,17},{9,25},{17,1},{25,9},{2,18},{10... | collective-permute-start | bytes 1572872 | tf_op jit(solution)/shard_map/ppermute | solution.py:30
  130.5 22.8 %collective-permute-start.23 = (f32[64,2048]{1,0:T(8,128)}, f32[64,2048]{1,0:T(8,128)S(1)}, u32[]{:S(2)}, u32[]{:S(2)}) collective-permute-start(f32[64,2048]{1,0:T(8,128)} %shard_map.106), channel_id=1, source_target_pairs={{0,7},{1,6},{2,5},{3,4},{4,3},{5,2},{6,1},{7,0},{8,15},{9,14},{10,... | collective-permute-start | bytes 1572872 | tf_op jit(solution)/shard_map/ppermute | solution.py:28
  134.2 20.2 %collective-permute-start.22 = (f32[64,2048]{1,0:T(8,128)}, f32[64,2048]{1,0:T(8,128)}, u32[]{:S(2)}, u32[]{:S(2)}) collective-permute-start(f32[64,2048]{1,0:T(8,128)} %get-tuple-element.98.refs_2_), channel_id=1, source_target_pairs={{0,16},{8,24},{16,0},{24,8},{1,17},{9,25},{17,1},{25,9},{2,18},{10... | collective-permute-start | bytes 1572872 | tf_op jit(solution)/shard_map/ppermute | solution.py:30
  155.4 14.2 %collective-permute-start.28 = (f32[64,2048]{1,0:T(8,128)}, f32[64,2048]{1,0:T(8,128)}, u32[]{:S(2)}, u32[]{:S(2)}) collective-permute-start(f32[64,2048]{1,0:T(8,128)} %get-tuple-element.108.refs_0_), channel_id=1, source_target_pairs={{0,16},{8,24},{16,0},{24,8},{1,17},{9,25},{17,1},{25,9},{2,18},{10... | collective-permute-start | bytes 1572872 | tf_op jit(solution)/shard_map/ppermute | solution.py:30
  (28 other events, 125.1 us)

commit v4 on v3

--- a/solution.py
+++ b/solution.py
@@ -12,6 +12,7 @@
 PANEL = 512
 STEP = 256
 WIDE = 512
+UNROLL = 8
 LANES = 128
 NB = 128
 SUB = 8
@@ -101,7 +102,7 @@
                 part[:, there] = spread[k * height : (k + 1) * height]
             return carry
 
-        lax.fori_loop(0, tiles, tile, 0, unroll=4)
+        lax.fori_loop(0, tiles, tile, 0, unroll=UNROLL)
 
 
 def widen(info, child, cmap, limits, places, n_ct, tokens):
@@ -565,24 +566,23 @@
     far_c, near_c = over_ct(far[2], late[:1]), over_ct(near[2], late[:1])
     joined, mark = join(late[eight : 2 * eight] + late[:eight] + late[2 * eight :])
     second = over_rt(joined)
-    first, after = join(first)
-    first = [first, swap(first, 1, 0)]
     inverse = [inverse]
     q_high, q_low, basis, turned_high, turned_low = basis_rows(
         inverse,
         panel.reshape(2, half, n_ct // 2, src, PANEL),
         other_panel.reshape(2, half, n_ct // 2, src, PANEL),
         targets,
-        [mark, after],
+        [mark],
         front_rows,
         order,
     )
 
     call = functools.partial(mix_call, q_high=q_high, q_low=q_low, targets=flat_targets, front_rows=front_rows)
-    late = list(gate(second + near_c + far_c, [basis]))
-    second, late = late[:half], late[half:]
+    late = list(gate(first + second + near_c + far_c, [basis]))
+    first, second, late = late[:half], late[half : 2 * half], late[2 * half :]
     far_d = over_ct(far[3], late[:1])
     third, fourth = over_rt(one(late[:eight])), over_rt(one(late[eight:]))
+    first += [swap(x, 1, 0) for x in first]
     second += [swap(x, 1, 0) for x in second]
 
     def rows_of(mine, start, size):
@@ -596,15 +596,15 @@
             arrays += mine
         return tuple(arrays), tuple(spots)
 
-    part, height = src // 2, first[0].shape[0] // half
+    part, height = src // 2, first[0].shape[0]
     whole_rows = height - part * eight
-    places = [(side, n * height) for side in range(2) for n in range(half)]
+    places = [(n, 0) for n in range(n_rt)]
     spots = [(side, at + row, src) for row in range(0, whole_rows, src) for side, at in places]
     for k in range(eight):
         for n, (side, at) in enumerate(places):
-            spots += [(side, at + whole_rows + k * part, part), (2 + n, k * part, part)]
+            spots += [(side, at + whole_rows + k * part, part), (n_rt + n, k * part, part)]
     for row in range(part * eight, second[0].shape[0], src):
-        spots += rows_of(2, row, src)
+        spots += rows_of(n_rt, row, src)
     arrays = tuple(first) + tuple(second)
     state = call(first_kernel, 0, (), (), arrays, tuple(spots), tokens=late[:1])
     late = list(gate(third + fourth + far_d, [state[0]]))

time: 190 us -> 186 us (0.979); the launches traced: 187 us -> 186 us
  Pallas kernels: 115 us -> 110 us
  waiting for transfers between devices: 28.2 us -> 32.8 us
    ppermute x18 -> x19, waiting for transfers between devices: 6.64 us -> 12.2 us  [swap(): return lax.ppermute(x, 'rt', [(r, r ^ rt_bit) for r in range(n_rt)])]
    pallas_call x6 -> x5, Pallas kernels: 11 us -> 7.66 us  [join(): pl.pallas_call(functools.partial(join_kernel, len(parts), cut), out_shape...]
    pallas_call x2, Pallas kernels: 12.7 us -> 10.7 us  [widen(): pl.pallas_call(functools.partial(widen_kernel, block_cols // STEP, window...]
    ppermute x18 -> x19, starting transfers between devices: 10.2 us -> 9.78 us  [swap(): return lax.ppermute(x, 'rt', [(r, r ^ rt_bit) for r in range(n_rt)])]
  transfers between devices with their start and end apart: 31 -> 32, of which waited for: 10 -> 14; matrix products, arithmetic and copies ran while one was open for 3% -> 3% of each run, Pallas kernels for 50% -> 48%
where the time goes in v4:
time: 186 us
  Pallas kernels  110 us (59%)
  waiting for transfers between devices  32.8 us (18%)
  starting transfers between devices  30.3 us (16%)
  local copies, waits for them, and re-layouts  9.43 us (5%)
  other arithmetic  2.25 us (1%)
    pallas_call x3, Pallas kernels, mix_call(): pl.pallas_call(functools.partial(kernel, len(pieces), spots), grid=(block...  41.4 us
    pallas_call x1, Pallas kernels, inverse_factor(): pl.pallas_call(factor_kernel, out_shape=[jax.ShapeDtypeStruct((n, n), F32...  30 us
    ppermute x13, waiting for transfers between devices, swap(): return lax.ppermute(x, 'ct', [(c, c ^ ct_bit) for c in range(n_ct)])  20.6 us
    ppermute x13, starting transfers between devices, swap(): return lax.ppermute(x, 'ct', [(c, c ^ ct_bit) for c in range(n_ct)])  20.5 us
    pallas_call x1, Pallas kernels, basis_rows(): pl.pallas_call(functools.partial(basis_kernel, len(inverse), len(tokens))...  15.8 us
    ppermute x19, waiting for transfers between devices, swap(): return lax.ppermute(x, 'rt', [(r, r ^ rt_bit) for r in range(n_rt)])  12.2 us
    pallas_call x2, Pallas kernels, widen(): pl.pallas_call(functools.partial(widen_kernel, block_cols // STEP, window...  10.7 us
    ppermute x19, starting transfers between devices, swap(): return lax.ppermute(x, 'rt', [(r, r ^ rt_bit) for r in range(n_rt)])  9.78 us
  transfers between devices with their start and end apart: 32, of which 14 were waited for; matrix products, arithmetic and copies ran while one was open for 3% of the time, Pallas kernels for 48%

profile of v4, /device:TPU:0, one launch (start us, length us, event | category | flops | bytes accessed | tf_op | source)
XLA Modules:
  0.0 185.9 jit_solution(428755727375993785)
XLA Ops:
  2.5 5.1 %collective-permute-start.2 = (f32[64,512]{1,0:T(8,128)S(1)}, f32[64,512]{1,0:T(8,128)S(1)}, u32[]{:S(2)}, u32[]{:S(2)}) collective-permute-start(f32[64,512]{1,0:T(8,128)S(1)} %slice_select_fusion.refs_0_), channel_id=1, source_target_pairs={{0,6},{1,7},{2,4},{3,5},{4,2},{5,3},{6,0},{7,1},{8,14},{9,15},{10,... | collective-permute-start | bytes 393224 | tf_op jit(solution)/shard_map/ppermute | solution.py:29
  10.9 3.4 %shard_map.85 = (f32[64,2048]{1,0:T(8,128)}, f32[8,128]{1,0:T(8,128)}) custom-call(s32[66]{0:T(128)} %pad_add_fusion.info, f32[64,12288]{1,0:T(8,128)} %child.3, s32[1,12288]{1,0:T(1,128)} %copy-done.17, s32[1,12288]{1,0:T(1,128)} %bitcast.19), custom_call_target="tpu_custom_call" | custom-call | flops 201326592 | bytes 3670016 | tf_op jit(solution)/shard_map/pallas_call | solution.py:113
  15.0 3.7 %collective-permute-done.refs_1_ = f32[64,512]{1,0:T(8,128)S(1)} collective-permute-done((f32[64,512]{1,0:T(8,128)S(1)}, f32[64,512]{1,0:T(8,128)S(1)}, u32[]{:S(2)}, u32[]{:S(2)}) %collective-permute-start) | collective-permute-done | bytes 131104 | tf_op jit(solution)/shard_map/ppermute | solution.py:29
  20.1 1.5 collective-permute-start.5
  23.1 7.3 %shard_map.87 = (f32[64,2048]{1,0:T(8,128)}, f32[64,2048]{1,0:T(8,128)}, f32[64,2048]{1,0:T(8,128)}, f32[64,2048]{1,0:T(8,128)}, f32[64,2048]{1,0:T(8,128)}, /*i...) custom-call(s32[66]{0:T(128)} %pad_add_fusion.info, f32[64,12288]{1,0:T(8,128)} %child.3, ...), custom_call_target="tpu_custom_call" | custom-call | flops 1409286144 | bytes 6815744 | tf_op jit(solution)/shard_map/pallas_call | solution.py:113
  34.8 3.0 %collective-permute-start.8 = (f32[32,2048]{1,0:T(8,128)}, f32[32,2048]{1,0:T(8,128)S(1)}, u32[]{:S(2)}, u32[]{:S(2)}) collective-permute-start(f32[32,2048]{1,0:T(8,128)} %shard_map.91), channel_id=1, source_target_pairs={{0,4},{1,5},{2,6},{3,7},{4,0},{5,1},{6,2},{7,3},{8,12},{9,13},{10,... | collective-permute-start | bytes 786440 | tf_op jit(solution)/shard_map/ppermute | solution.py:29
  37.8 10.0 %collective-permute-done.8.refs_1_.refs_2_ = f32[32,2048]{1,0:T(8,128)S(1)} collective-permute-done((f32[32,2048]{1,0:T(8,128)}, f32[32,2048]{1,0:T(8,128)S(1)}, u32[]{:S(2)}, u32[]{:S(2)}) %collective-permute-start.8) | collective-permute-done | bytes 262176 | tf_op jit(solution)/shard_map/ppermute | solution.py:29
  47.9 4.6 %shard_map.92 = (f32[1024,512]{1,0:T(8,128)}, f32[512,512]{1,0:T(8,128)}, f32[8,128]{1,0:T(8,128)S(1)}) custom-call(f32[512,256]{1,0:T(8,128)S(1)} %get-tuple-element.62.a_mine, f32[512,256]{1,0:T(8,128)S(1)} %collective-permute-done.4.a_other, f32[512,256]{1,0:T(8,128)S(1)} %get-tuple-element.64.b_mine, f32[512,256]{1,0:T(8,128)S(1)} %collective-permute-done.6.b_other, ...), custom_call_target="tpu_custom_call" | custom-call | flops 536870912 | bytes 524288 | tf_op jit(solution)/shard_map/pallas_call | solution.py:313
  53.1 1.5 collective-permute-start.12
  54.6 2.9 %collective-permute-start.14 = (f32[64,2048]{1,0:T(8,128)}, f32[64,2048]{1,0:T(8,128)}, u32[]{:S(2)}, u32[]{:S(2)}) collective-permute-start(f32[64,2048]{1,0:T(8,128)} %shard_map.97), channel_id=1, source_target_pairs={{0,5},{1,4},{2,7},{3,6},{4,1},{5,0},{6,3},{7,2},{8,13},{9,12},{10,... | collective-permute-start | bytes 1572872 | tf_op jit(solution)/shard_map/ppermute | solution.py:29
  57.5 2.4 %shard_map.93 = (f32[160,2048]{1,0:T(8,128)}, f32[8,128]{1,0:T(8,128)}) custom-call(f32[64,2048]{1,0:T(8,128)} %get-tuple-element.70.refs_0_, f32[64,2048]{1,0:T(8,128)} %copy-done.2, f32[32,2048]{1,0:T(8,128)} %copy-done.3, f32[8,128]{1,0:T(8,128)} %copy-done.4), custom_call_target="tpu_custom_call" | custom-call | bytes 2621440 | tf_op jit(solution)/shard_map/pallas_call | solution.py:284
  61.3 30.0 %shard_map.94 = (f32[512,512]{1,0:T(8,128)}, f32[8,128]{1,0:T(8,128)}) custom-call(f32[512,512]{1,0:T(8,128)} %get-tuple-element.68.gram_a, f32[512,512]{1,0:T(8,128)} %collective-permute-done.9.gram_b, f32[1024,512]{1,0:T(8,128)} %collective-permute-done.10.refs_0_, f32[8,128]{1,0:T(8,128)} %get-tuple-element.72.refs_1_), custom_call_target="tpu_custom_call" | custom-call | flops 30000001024 | bytes 3145728 | tf_op jit(solution)/shard_map/pallas_call | solution.py:235
  92.3 2.5 %shard_map.99 = (f32[160,2048]{1,0:T(8,128)}, f32[8,128]{1,0:T(8,128)}) custom-call(f32[32,2048]{1,0:T(8,128)} %get-tuple-element.79.refs_0_, f32[64,2048]{1,0:T(8,128)} %get-tuple-element.80.refs_1_, f32[64,2048]{1,0:T(8,128)} %get-tuple-element.81.refs_2_), custom_call_target="tpu_custom_call" | custom-call | bytes 2621440 | tf_op jit(solution)/shard_map/pallas_call | solution.py:284
  96.6 2.1 %collective-permute-start.17 = (f32[64,2048]{1,0:T(8,128)}, f32[64,2048]{1,0:T(8,128)}, u32[]{:S(2)}, u32[]{:S(2)}) collective-permute-start(f32[64,2048]{1,0:T(8,128)} %shard_map.102), channel_id=1, source_target_pairs={{0,6},{1,7},{2,4},{3,5},{4,2},{5,3},{6,0},{7,1},{8,14},{9,15},{10,... | collective-permute-start | bytes 1572872 | tf_op jit(solution)/shard_map/ppermute | solution.py:29
  99.4 15.8 %shard_map.100 = (bf16[512,2048]{1,0:T(8,128)(2,1)}, bf16[512,2048]{1,0:T(8,128)(2,1)}, f32[512,512]{1,0:T(8,128)}, bf16[512,512]{1,0:T(8,128)(2,1)}, bf16[512,512]{1,0:T(8,128)(2,1)}) custom-call(f32[512,512]{1,0:T(8,128)} %get-tuple-element.73.refs_0_, f32[2,2,4,64,512]{4,3,2,1,0:T(8,128)} %bitcast.5.refs_1_, f32[2,2,4,64,512]{4,3,2,1,0:T(8,128)} %bitcast.6.refs_2_, ...), custom_call_target="tpu_custom_call" | custom-call | flops 4294967296 | bytes 6291456 | tf_op jit(solution)/shard_map/pallas_call | solution.py:376
  115.2 6.2 %collective-permute-done.16.refs_4_ = f32[64,2048]{1,0:T(8,128)S(1)} collective-permute-done((f32[64,2048]{1,0:T(8,128)}, f32[64,2048]{1,0:T(8,128)S(1)}, u32[]{:S(2)}, u32[]{:S(2)}) %collective-permute-start.16) | collective-permute-done | bytes 524320 | tf_op jit(solution)/shard_map/ppermute | solution.py:29
  121.4 3.2 %collective-permute-done.15.refs_3_ = f32[160,2048]{1,0:T(8,128)} collective-permute-done((f32[160,2048]{1,0:T(8,128)}, f32[160,2048]{1,0:T(8,128)}, u32[]{:S(2)}, u32[]{:S(2)}) %collective-permute-start.15) | collective-permute-done | bytes 1310752 | tf_op jit(solution)/shard_map/ppermute | solution.py:31
  128.0 2.7 %collective-permute-start.24 = (f32[64,2048]{1,0:T(8,128)}, f32[64,2048]{1,0:T(8,128)S(1)}, u32[]{:S(2)}, u32[]{:S(2)}) collective-permute-start(f32[64,2048]{1,0:T(8,128)} %shard_map.105), channel_id=1, source_target_pairs={{0,7},{1,6},{2,5},{3,4},{4,3},{5,2},{6,1},{7,0},{8,15},{9,14},{10,... | collective-permute-start | bytes 1572872 | tf_op jit(solution)/shard_map/ppermute | solution.py:29
  131.7 1.9 %collective-permute-done.21.refs_7_ = f32[160,2048]{1,0:T(8,128)} collective-permute-done((f32[160,2048]{1,0:T(8,128)}, f32[160,2048]{1,0:T(8,128)}, u32[]{:S(2)}, u32[]{:S(2)}) %collective-permute-start.21) | collective-permute-done | bytes 1310752 | tf_op jit(solution)/shard_map/ppermute | solution.py:31
  133.6 18.5 %shard_map.104 = (f32[512,2048]{1,0:T(8,128)}, f32[512,2048]{1,0:T(8,128)}) custom-call(bf16[512,2048]{1,0:T(8,128)(2,1)} %get-tuple-element.83.q_high, bf16[512,2048]{1,0:T(8,128)(2,1)} %get-tuple-element.84.q_low, s32[1,2048]{1,0:T(1,128)} %sub.45.targets, f32[160,2048]{1,0:T(8,128)} %get-tuple-element.91.refs_0_, f32[160,2048]{1,0:T(8,128)} %get-tuple-element.92.refs_1_, ...), custom_call_target="tpu_custom_call" | custom-call | flops 6710886400 | bytes 4718592 | tf_op jit(solution)/shard_map/pallas_call | solution.py:455
  155.0 1.5 collective-permute-done.26.refs_3_
  158.1 9.0 %shard_map.107 = (f32[512,2048]{1,0:T(8,128)}, f32[512,2048]{1,0:T(8,128)}) custom-call(bf16[512,2048]{1,0:T(8,128)(2,1)} %get-tuple-element.83.q_high, bf16[512,2048]{1,0:T(8,128)(2,1)} %get-tuple-element.84.q_low, s32[1,2048]{1,0:T(1,128)} %sub.45.targets, f32[512,2048]{1,0:T(8,128)} %get-tuple-element.96.refs_5_.factor_in, ...), custom_call_target="tpu_custom_call" | custom-call | flops 1342177280 | bytes 4718592 | tf_op jit(solution)/shard_map/pallas_call | solution.py:455
  168.7 2.3 %collective-permute-done.30.refs_6_ = f32[64,2048]{1,0:T(8,128)S(1)} collective-permute-done((f32[64,2048]{1,0:T(8,128)}, f32[64,2048]{1,0:T(8,128)S(1)}, u32[]{:S(2)}, u32[]{:S(2)}) %collective-permute-start.30) | collective-permute-done | bytes 524320 | tf_op jit(solution)/shard_map/ppermute | solution.py:31
  171.9 13.9 %shard_map.109 = (f32[512,2048]{1,0:T(8,128)}, f32[512,2048]{1,0:T(8,128)}) custom-call(bf16[512,2048]{1,0:T(8,128)(2,1)} %get-tuple-element.83.q_high, bf16[512,2048]{1,0:T(8,128)(2,1)} %get-tuple-element.84.q_low, s32[1,2048]{1,0:T(1,128)} %sub.45.targets, f32[512,2048]{1,0:T(8,128)} %get-tuple-element.104.refs_2_.factor_in, ...), custom_call_target="tpu_custom_call" | custom-call | flops 4294967296 | bytes 5242880 | tf_op jit(solution)/shard_map/pallas_call | solution.py:455
  (132 shorter events, 29.9 us)
Async XLA Ops:
  2.5 11.8 %collective-permute-start.2 = (f32[64,512]{1,0:T(8,128)S(1)}, f32[64,512]{1,0:T(8,128)S(1)}, u32[]{:S(2)}, u32[]{:S(2)}) collective-permute-start(f32[64,512]{1,0:T(8,128)S(1)} %slice_select_fusion.refs_0_), channel_id=1, source_target_pairs={{0,6},{1,7},{2,4},{3,5},{4,2},{5,3},{6,0},{7,1},{8,14},{9,15},{10,... | collective-permute-start | bytes 393224 | tf_op jit(solution)/shard_map/ppermute | solution.py:29
  7.6 7.4 %collective-permute-start.1 = (f32[64,512]{1,0:T(8,128)S(1)}, f32[64,512]{1,0:T(8,128)S(1)}, u32[]{:S(2)}, u32[]{:S(2)}) collective-permute-start(f32[64,512]{1,0:T(8,128)S(1)} %slice_select_fusion.refs_0_), channel_id=1, source_target_pairs={{0,2},{1,3},{2,0},{3,1},{4,6},{5,7},{6,4},{7,5},{8,10},{9,11},{10,... | collective-permute-start | bytes 393224 | tf_op jit(solution)/shard_map/ppermute | solution.py:29
  7.6 11.1 %collective-permute-start = (f32[64,512]{1,0:T(8,128)S(1)}, f32[64,512]{1,0:T(8,128)S(1)}, u32[]{:S(2)}, u32[]{:S(2)}) collective-permute-start(f32[64,512]{1,0:T(8,128)S(1)} %slice_select_fusion.refs_0_), channel_id=1, source_target_pairs={{0,4},{1,5},{2,6},{3,7},{4,0},{5,1},{6,2},{7,3},{8,12},{9,13},{10,... | collective-permute-start | bytes 393224 | tf_op jit(solution)/shard_map/ppermute | solution.py:29
  20.1 10.3 %collective-permute-start.5 = (f32[256,256]{1,0:T(8,128)}, f32[256,256]{1,0:T(8,128)}, u32[]{:S(2)}, u32[]{:S(2)}) collective-permute-start(f32[256,256]{1,0:T(8,128)} %get-tuple-element.63.refs_0_), channel_id=1, source_target_pairs={{0,1},{1,0},{2,3},{3,2},{4,5},{5,4},{6,7},{7,6},{8,9},{9,8},{10,11... | collective-permute-start | bytes 786440 | tf_op jit(solution)/shard_map/ppermute | solution.py:29
  21.6 10.4 %collective-permute-start.3 = (f32[256,256]{1,0:T(8,128)S(1)}, f32[256,256]{1,0:T(8,128)}, u32[]{:S(2)}, u32[]{:S(2)}) collective-permute-start(f32[256,256]{1,0:T(8,128)S(1)} %get-tuple-element.59.refs_0_), channel_id=1, source_target_pairs={{0,16},{8,24},{16,0},{24,8},{1,17},{9,25},{17,1},{25,9},{2,18},{10... | collective-permute-start | bytes 786440 | tf_op jit(solution)/shard_map/ppermute | solution.py:31
  23.1 14.7 %collective-permute-start.7 = (f32[64,2048]{1,0:T(8,128)}, f32[64,2048]{1,0:T(8,128)S(1)}, u32[]{:S(2)}, u32[]{:S(2)}) collective-permute-start(f32[64,2048]{1,0:T(8,128)} %shard_map.90), channel_id=1, source_target_pairs={{0,2},{1,3},{2,0},{3,1},{4,6},{5,7},{6,4},{7,5},{8,10},{9,11},{10,... | collective-permute-start | bytes 1572872 | tf_op jit(solution)/shard_map/ppermute | solution.py:29
  31.4 16.4 %collective-permute-start.6 = (f32[512,256]{1,0:T(8,128)S(1)}, f32[512,256]{1,0:T(8,128)S(1)}, u32[]{:S(2)}, u32[]{:S(2)}) collective-permute-start(f32[512,256]{1,0:T(8,128)S(1)} %get-tuple-element.64.b_mine), channel_id=1, source_target_pairs={{0,16},{8,24},{16,0},{24,8},{1,17},{9,25},{17,1},{25,9},{2,18},{10... | collective-permute-start | bytes 1572872 | tf_op jit(solution)/shard_map/ppermute | solution.py:31
  34.3 13.6 %collective-permute-start.4 = (f32[512,256]{1,0:T(8,128)S(1)}, f32[512,256]{1,0:T(8,128)S(1)}, u32[]{:S(2)}, u32[]{:S(2)}) collective-permute-start(f32[512,256]{1,0:T(8,128)S(1)} %get-tuple-element.62.a_mine), channel_id=1, source_target_pairs={{0,1},{1,0},{2,3},{3,2},{4,5},{5,4},{6,7},{7,6},{8,9},{9,8},{10,11... | collective-permute-start | bytes 1572872 | tf_op jit(solution)/shard_map/ppermute | solution.py:29
  34.8 13.1 %collective-permute-start.8 = (f32[32,2048]{1,0:T(8,128)}, f32[32,2048]{1,0:T(8,128)S(1)}, u32[]{:S(2)}, u32[]{:S(2)}) collective-permute-start(f32[32,2048]{1,0:T(8,128)} %shard_map.91), channel_id=1, source_target_pairs={{0,4},{1,5},{2,6},{3,7},{4,0},{5,1},{6,2},{7,3},{8,12},{9,13},{10,... | collective-permute-start | bytes 786440 | tf_op jit(solution)/shard_map/ppermute | solution.py:29
  52.5 8.9 %collective-permute-start.10 = (f32[1024,512]{1,0:T(8,128)}, f32[1024,512]{1,0:T(8,128)}, u32[]{:S(2)}, u32[]{:S(2)}) collective-permute-start(f32[1024,512]{1,0:T(8,128)} %get-tuple-element.69), channel_id=1, source_target_pairs={{0,8},{8,0},{16,24},{24,16},{1,9},{9,1},{17,25},{25,17},{2,10},{10... | collective-permute-start | bytes 6291464 | tf_op jit(solution)/shard_map/ppermute | solution.py:31
  52.5 7.5 %collective-permute-start.9 = (f32[512,512]{1,0:T(8,128)}, f32[512,512]{1,0:T(8,128)}, u32[]{:S(2)}, u32[]{:S(2)}) collective-permute-start(f32[512,512]{1,0:T(8,128)} %get-tuple-element.68.gram_a), channel_id=1, source_target_pairs={{0,8},{8,0},{16,24},{24,16},{1,9},{9,1},{17,25},{25,17},{2,10},{10... | collective-permute-start | bytes 3145736 | tf_op jit(solution)/shard_map/ppermute | solution.py:31
  53.1 38.3 %collective-permute-start.13 = (f32[32,2048]{1,0:T(8,128)}, f32[32,2048]{1,0:T(8,128)S(1)}, u32[]{:S(2)}, u32[]{:S(2)}) collective-permute-start(f32[32,2048]{1,0:T(8,128)} %shard_map.96), channel_id=1, source_target_pairs={{0,4},{1,5},{2,6},{3,7},{4,0},{5,1},{6,2},{7,3},{8,12},{9,13},{10,... | collective-permute-start | bytes 786440 | tf_op jit(solution)/shard_map/ppermute | solution.py:29
  53.1 38.2 %collective-permute-start.12 = (f32[64,2048]{1,0:T(8,128)}, f32[64,2048]{1,0:T(8,128)S(1)}, u32[]{:S(2)}, u32[]{:S(2)}) collective-permute-start(f32[64,2048]{1,0:T(8,128)} %shard_map.95), channel_id=1, source_target_pairs={{0,1},{1,0},{2,3},{3,2},{4,5},{5,4},{6,7},{7,6},{8,9},{9,8},{10,11... | collective-permute-start | bytes 1572872 | tf_op jit(solution)/shard_map/ppermute | solution.py:29
  54.6 36.8 %collective-permute-start.14 = (f32[64,2048]{1,0:T(8,128)}, f32[64,2048]{1,0:T(8,128)}, u32[]{:S(2)}, u32[]{:S(2)}) collective-permute-start(f32[64,2048]{1,0:T(8,128)} %shard_map.97), channel_id=1, source_target_pairs={{0,5},{1,4},{2,7},{3,6},{4,1},{5,0},{6,3},{7,2},{8,13},{9,12},{10,... | collective-permute-start | bytes 1572872 | tf_op jit(solution)/shard_map/ppermute | solution.py:29
  59.9 31.5 %collective-permute-start.11 = (f32[160,2048]{1,0:T(8,128)}, f32[160,2048]{1,0:T(8,128)}, u32[]{:S(2)}, u32[]{:S(2)}) collective-permute-start(f32[160,2048]{1,0:T(8,128)} %get-tuple-element.74.refs_0_), channel_id=1, source_target_pairs={{0,16},{8,24},{16,0},{24,8},{1,17},{9,25},{17,1},{25,9},{2,18},{10... | collective-permute-start | bytes 3932168 | tf_op jit(solution)/shard_map/ppermute | solution.py:31
  94.7 29.9 %collective-permute-start.15 = (f32[160,2048]{1,0:T(8,128)}, f32[160,2048]{1,0:T(8,128)}, u32[]{:S(2)}, u32[]{:S(2)}) collective-permute-start(f32[160,2048]{1,0:T(8,128)} %get-tuple-element.87.refs_2_), channel_id=1, source_target_pairs={{0,16},{8,24},{16,0},{24,8},{1,17},{9,25},{17,1},{25,9},{2,18},{10... | collective-permute-start | bytes 3932168 | tf_op jit(solution)/shard_map/ppermute | solution.py:31
  96.2 25.2 %collective-permute-start.16 = (f32[64,2048]{1,0:T(8,128)}, f32[64,2048]{1,0:T(8,128)S(1)}, u32[]{:S(2)}, u32[]{:S(2)}) collective-permute-start(f32[64,2048]{1,0:T(8,128)} %shard_map.101), channel_id=1, source_target_pairs={{0,3},{1,2},{2,1},{3,0},{4,7},{5,6},{6,5},{7,4},{8,11},{9,10},{10,... | collective-permute-start | bytes 1572872 | tf_op jit(solution)/shard_map/ppermute | solution.py:29
  96.6 24.8 %collective-permute-start.17 = (f32[64,2048]{1,0:T(8,128)}, f32[64,2048]{1,0:T(8,128)}, u32[]{:S(2)}, u32[]{:S(2)}) collective-permute-start(f32[64,2048]{1,0:T(8,128)} %shard_map.102), channel_id=1, source_target_pairs={{0,6},{1,7},{2,4},{3,5},{4,2},{5,3},{6,0},{7,1},{8,14},{9,15},{10,... | collective-permute-start | bytes 1572872 | tf_op jit(solution)/shard_map/ppermute | solution.py:29
  125.1 6.6 %collective-permute-start.20 = (f32[160,2048]{1,0:T(8,128)}, f32[160,2048]{1,0:T(8,128)}, u32[]{:S(2)}, u32[]{:S(2)}) collective-permute-start(f32[160,2048]{1,0:T(8,128)} %get-tuple-element.93.refs_4_), channel_id=1, source_target_pairs={{0,8},{8,0},{16,24},{24,16},{1,9},{9,1},{17,25},{25,17},{2,10},{10... | collective-permute-start | bytes 3932168 | tf_op jit(solution)/shard_map/ppermute | solution.py:31
  125.1 8.5 %collective-permute-start.21 = (f32[160,2048]{1,0:T(8,128)}, f32[160,2048]{1,0:T(8,128)}, u32[]{:S(2)}, u32[]{:S(2)}) collective-permute-start(f32[160,2048]{1,0:T(8,128)} %get-tuple-element.94.refs_5_), channel_id=1, source_target_pairs={{0,8},{8,0},{16,24},{24,16},{1,9},{9,1},{17,25},{25,17},{2,10},{10... | collective-permute-start | bytes 3932168 | tf_op jit(solution)/shard_map/ppermute | solution.py:31
  126.3 25.9 %collective-permute-start.22 = (f32[64,2048]{1,0:T(8,128)}, f32[64,2048]{1,0:T(8,128)}, u32[]{:S(2)}, u32[]{:S(2)}) collective-permute-start(f32[64,2048]{1,0:T(8,128)} %get-tuple-element.95.refs_8_.refs_1_.refs_0_), channel_id=1, source_target_pairs={{0,16},{8,24},{16,0},{24,8},{1,17},{9,25},{17,1},{25,9},{2,18},{10... | collective-permute-start | bytes 1572872 | tf_op jit(solution)/shard_map/ppermute | solution.py:31
  128.0 24.1 %collective-permute-start.24 = (f32[64,2048]{1,0:T(8,128)}, f32[64,2048]{1,0:T(8,128)S(1)}, u32[]{:S(2)}, u32[]{:S(2)}) collective-permute-start(f32[64,2048]{1,0:T(8,128)} %shard_map.105), channel_id=1, source_target_pairs={{0,7},{1,6},{2,5},{3,4},{4,3},{5,2},{6,1},{7,0},{8,15},{9,14},{10,... | collective-permute-start | bytes 1572872 | tf_op jit(solution)/shard_map/ppermute | solution.py:29
  130.7 21.4 %collective-permute-start.23 = (f32[64,2048]{1,0:T(8,128)}, f32[64,2048]{1,0:T(8,128)}, u32[]{:S(2)}, u32[]{:S(2)}) collective-permute-start(f32[64,2048]{1,0:T(8,128)} %get-tuple-element.98.refs_2_), channel_id=1, source_target_pairs={{0,16},{8,24},{16,0},{24,8},{1,17},{9,25},{17,1},{25,9},{2,18},{10... | collective-permute-start | bytes 1572872 | tf_op jit(solution)/shard_map/ppermute | solution.py:31
  153.9 14.3 %collective-permute-start.29 = (f32[64,2048]{1,0:T(8,128)}, f32[64,2048]{1,0:T(8,128)}, u32[]{:S(2)}, u32[]{:S(2)}) collective-permute-start(f32[64,2048]{1,0:T(8,128)} %get-tuple-element.108.refs_0_), channel_id=1, source_target_pairs={{0,16},{8,24},{16,0},{24,8},{1,17},{9,25},{17,1},{25,9},{2,18},{10... | collective-permute-start | bytes 1572872 | tf_op jit(solution)/shard_map/ppermute | solution.py:31
  (29 other events, 116.7 us)

commit v5 on v4

--- a/solution.py
+++ b/solution.py
@@ -566,6 +566,7 @@
     far_c, near_c = over_ct(far[2], late[:1]), over_ct(near[2], late[:1])
     joined, mark = join(late[eight : 2 * eight] + late[:eight] + late[2 * eight :])
     second = over_rt(joined)
+    crossed = swap(first[0], 1, 0)
     inverse = [inverse]
     q_high, q_low, basis, turned_high, turned_low = basis_rows(
         inverse,
@@ -578,11 +579,12 @@
     )
 
     call = functools.partial(mix_call, q_high=q_high, q_low=q_low, targets=flat_targets, front_rows=front_rows)
-    late = list(gate(first + second + near_c + far_c, [basis]))
+    late = list(gate(first + [crossed] + second + near_c + far_c, [basis]))
+    crossed = late.pop(half)
     first, second, late = late[:half], late[half : 2 * half], late[2 * half :]
     far_d = over_ct(far[3], late[:1])
     third, fourth = over_rt(one(late[:eight])), over_rt(one(late[eight:]))
-    first += [swap(x, 1, 0) for x in first]
+    first += [crossed] + [swap(x, 1, 0) for x in first[1:]]
     second += [swap(x, 1, 0) for x in second]
 
     def rows_of(mine, start, size):

time: 186 us -> 185 us (level)
  transfers between devices with their start and end apart: 32 -> 32, of which waited for: 14 -> 13; matrix products, arithmetic and copies ran while one was open for 3% -> 3% of each run, Pallas kernels for 48% -> 48%
where the time goes in v5:
time: 185 us
  Pallas kernels  110 us (59%)
  waiting for transfers between devices  32.2 us (17%)
  starting transfers between devices  30.3 us (16%)
  local copies, waits for them, and re-layouts  8.67 us (5%)
  other arithmetic  2.27 us (1%)
    pallas_call x3, Pallas kernels, mix_call(): pl.pallas_call(functools.partial(kernel, len(pieces), spots), grid=(block...  41.4 us
    pallas_call x1, Pallas kernels, inverse_factor(): pl.pallas_call(factor_kernel, out_shape=[jax.ShapeDtypeStruct((n, n), F32...  30 us
    ppermute x13, waiting for transfers between devices, swap(): return lax.ppermute(x, 'ct', [(c, c ^ ct_bit) for c in range(n_ct)])  21.8 us
    ppermute x13, starting transfers between devices, swap(): return lax.ppermute(x, 'ct', [(c, c ^ ct_bit) for c in range(n_ct)])  20 us
    pallas_call x1, Pallas kernels, basis_rows(): pl.pallas_call(functools.partial(basis_kernel, len(inverse), len(tokens))...  15.8 us
    pallas_call x2, Pallas kernels, widen(): pl.pallas_call(functools.partial(widen_kernel, block_cols // STEP, window...  10.7 us
    ppermute x19, waiting for transfers between devices, swap(): return lax.ppermute(x, 'rt', [(r, r ^ rt_bit) for r in range(n_rt)])  10.4 us
    ppermute x19, starting transfers between devices, swap(): return lax.ppermute(x, 'rt', [(r, r ^ rt_bit) for r in range(n_rt)])  10.3 us
  transfers between devices with their start and end apart: 32, of which 13 were waited for; matrix products, arithmetic and copies ran while one was open for 3% of the time, Pallas kernels for 48%

profile of v5, /device:TPU:0, one launch (start us, length us, event | category | flops | bytes accessed | tf_op | source)
XLA Modules:
  0.0 184.6 jit_solution(11218198924962250844)
XLA Ops:
  2.5 5.1 %collective-permute-start.2 = (f32[64,512]{1,0:T(8,128)S(1)}, f32[64,512]{1,0:T(8,128)S(1)}, u32[]{:S(2)}, u32[]{:S(2)}) collective-permute-start(f32[64,512]{1,0:T(8,128)S(1)} %slice_select_fusion.refs_0_), channel_id=1, source_target_pairs={{0,6},{1,7},{2,4},{3,5},{4,2},{5,3},{6,0},{7,1},{8,14},{9,15},{10,... | collective-permute-start | bytes 393224 | tf_op jit(solution)/shard_map/ppermute | solution.py:29
  10.9 3.4 %shard_map.85 = (f32[64,2048]{1,0:T(8,128)}, f32[8,128]{1,0:T(8,128)}) custom-call(s32[66]{0:T(128)} %pad_add_fusion.info, f32[64,12288]{1,0:T(8,128)} %child.3, s32[1,12288]{1,0:T(1,128)} %copy-done.17, s32[1,12288]{1,0:T(1,128)} %bitcast.19), custom_call_target="tpu_custom_call" | custom-call | flops 201326592 | bytes 3670016 | tf_op jit(solution)/shard_map/pallas_call | solution.py:113
  15.0 3.7 %collective-permute-done.refs_1_ = f32[64,512]{1,0:T(8,128)S(1)} collective-permute-done((f32[64,512]{1,0:T(8,128)S(1)}, f32[64,512]{1,0:T(8,128)S(1)}, u32[]{:S(2)}, u32[]{:S(2)}) %collective-permute-start) | collective-permute-done | bytes 131104 | tf_op jit(solution)/shard_map/ppermute | solution.py:29
  20.1 1.5 collective-permute-start.5
  21.6 1.5 collective-permute-start.3
  23.1 7.3 %shard_map.87 = (f32[64,2048]{1,0:T(8,128)}, f32[64,2048]{1,0:T(8,128)}, f32[64,2048]{1,0:T(8,128)}, f32[64,2048]{1,0:T(8,128)}, f32[64,2048]{1,0:T(8,128)}, /*i...) custom-call(s32[66]{0:T(128)} %pad_add_fusion.info, f32[64,12288]{1,0:T(8,128)} %child.3, ...), custom_call_target="tpu_custom_call" | custom-call | flops 1409286144 | bytes 6815744 | tf_op jit(solution)/shard_map/pallas_call | solution.py:113
  34.8 3.0 %collective-permute-start.8 = (f32[32,2048]{1,0:T(8,128)}, f32[32,2048]{1,0:T(8,128)S(1)}, u32[]{:S(2)}, u32[]{:S(2)}) collective-permute-start(f32[32,2048]{1,0:T(8,128)} %shard_map.91), channel_id=1, source_target_pairs={{0,4},{1,5},{2,6},{3,7},{4,0},{5,1},{6,2},{7,3},{8,12},{9,13},{10,... | collective-permute-start | bytes 786440 | tf_op jit(solution)/shard_map/ppermute | solution.py:29
  37.9 10.0 %collective-permute-done.8.refs_1_.refs_2_ = f32[32,2048]{1,0:T(8,128)S(1)} collective-permute-done((f32[32,2048]{1,0:T(8,128)}, f32[32,2048]{1,0:T(8,128)S(1)}, u32[]{:S(2)}, u32[]{:S(2)}) %collective-permute-start.8) | collective-permute-done | bytes 262176 | tf_op jit(solution)/shard_map/ppermute | solution.py:29
  47.9 4.6 %shard_map.92 = (f32[1024,512]{1,0:T(8,128)}, f32[512,512]{1,0:T(8,128)}, f32[8,128]{1,0:T(8,128)S(1)}) custom-call(f32[512,256]{1,0:T(8,128)S(1)} %get-tuple-element.63.a_mine, f32[512,256]{1,0:T(8,128)S(1)} %collective-permute-done.4.a_other, f32[512,256]{1,0:T(8,128)S(1)} %get-tuple-element.65.b_mine, f32[512,256]{1,0:T(8,128)S(1)} %collective-permute-done.6.b_other, ...), custom_call_target="tpu_custom_call" | custom-call | flops 536870912 | bytes 524288 | tf_op jit(solution)/shard_map/pallas_call | solution.py:313
  53.2 1.5 collective-permute-start.12
  54.7 2.9 %collective-permute-start.14 = (f32[64,2048]{1,0:T(8,128)}, f32[64,2048]{1,0:T(8,128)}, u32[]{:S(2)}, u32[]{:S(2)}) collective-permute-start(f32[64,2048]{1,0:T(8,128)} %shard_map.97), channel_id=1, source_target_pairs={{0,5},{1,4},{2,7},{3,6},{4,1},{5,0},{6,3},{7,2},{8,13},{9,12},{10,... | collective-permute-start | bytes 1572872 | tf_op jit(solution)/shard_map/ppermute | solution.py:29
  57.5 2.4 %shard_map.93 = (f32[160,2048]{1,0:T(8,128)}, f32[8,128]{1,0:T(8,128)}) custom-call(f32[64,2048]{1,0:T(8,128)} %get-tuple-element.71.refs_0_, f32[64,2048]{1,0:T(8,128)} %copy-done.2, f32[32,2048]{1,0:T(8,128)} %copy-done.3, f32[8,128]{1,0:T(8,128)} %copy-done.4), custom_call_target="tpu_custom_call" | custom-call | bytes 2621440 | tf_op jit(solution)/shard_map/pallas_call | solution.py:284
  61.4 30.0 %shard_map.94 = (f32[512,512]{1,0:T(8,128)}, f32[8,128]{1,0:T(8,128)}) custom-call(f32[512,512]{1,0:T(8,128)} %get-tuple-element.69.gram_a, f32[512,512]{1,0:T(8,128)} %collective-permute-done.9.gram_b, f32[1024,512]{1,0:T(8,128)} %collective-permute-done.10.refs_0_, f32[8,128]{1,0:T(8,128)} %get-tuple-element.73.refs_1_), custom_call_target="tpu_custom_call" | custom-call | flops 30000001024 | bytes 3145728 | tf_op jit(solution)/shard_map/pallas_call | solution.py:235
  92.3 2.5 %shard_map.99 = (f32[160,2048]{1,0:T(8,128)}, f32[8,128]{1,0:T(8,128)}) custom-call(f32[32,2048]{1,0:T(8,128)} %get-tuple-element.80.refs_0_, f32[64,2048]{1,0:T(8,128)} %get-tuple-element.81.refs_1_, f32[64,2048]{1,0:T(8,128)} %get-tuple-element.82.refs_2_), custom_call_target="tpu_custom_call" | custom-call | bytes 2621440 | tf_op jit(solution)/shard_map/pallas_call | solution.py:284
  96.7 2.1 %collective-permute-start.18 = (f32[64,2048]{1,0:T(8,128)}, f32[64,2048]{1,0:T(8,128)}, u32[]{:S(2)}, u32[]{:S(2)}) collective-permute-start(f32[64,2048]{1,0:T(8,128)} %shard_map.102), channel_id=1, source_target_pairs={{0,6},{1,7},{2,4},{3,5},{4,2},{5,3},{6,0},{7,1},{8,14},{9,15},{10,... | collective-permute-start | bytes 1572872 | tf_op jit(solution)/shard_map/ppermute | solution.py:29
  99.4 15.8 %shard_map.100 = (bf16[512,2048]{1,0:T(8,128)(2,1)}, bf16[512,2048]{1,0:T(8,128)(2,1)}, f32[512,512]{1,0:T(8,128)}, bf16[512,512]{1,0:T(8,128)(2,1)}, bf16[512,512]{1,0:T(8,128)(2,1)}) custom-call(f32[512,512]{1,0:T(8,128)} %get-tuple-element.74.refs_0_, f32[2,2,4,64,512]{4,3,2,1,0:T(8,128)} %bitcast.5.refs_1_, f32[2,2,4,64,512]{4,3,2,1,0:T(8,128)} %bitcast.6.refs_2_, ...), custom_call_target="tpu_custom_call" | custom-call | flops 4294967296 | bytes 6291456 | tf_op jit(solution)/shard_map/pallas_call | solution.py:376
  115.3 7.4 %collective-permute-done.18.refs_6_ = f32[64,2048]{1,0:T(8,128)} collective-permute-done((f32[64,2048]{1,0:T(8,128)}, f32[64,2048]{1,0:T(8,128)}, u32[]{:S(2)}, u32[]{:S(2)}) %collective-permute-start.18) | collective-permute-done | bytes 524320 | tf_op jit(solution)/shard_map/ppermute | solution.py:29
  122.7 1.9 %collective-permute-done.16.refs_4_ = f32[160,2048]{1,0:T(8,128)} collective-permute-done((f32[160,2048]{1,0:T(8,128)}, f32[160,2048]{1,0:T(8,128)}, u32[]{:S(2)}, u32[]{:S(2)}) %collective-permute-start.16) | collective-permute-done | bytes 1310752 | tf_op jit(solution)/shard_map/ppermute | solution.py:31
  126.9 2.2 %collective-permute-start.24 = (f32[64,2048]{1,0:T(8,128)}, f32[64,2048]{1,0:T(8,128)S(1)}, u32[]{:S(2)}, u32[]{:S(2)}) collective-permute-start(f32[64,2048]{1,0:T(8,128)} %shard_map.105), channel_id=1, source_target_pairs={{0,7},{1,6},{2,5},{3,4},{4,3},{5,2},{6,1},{7,0},{8,15},{9,14},{10,... | collective-permute-start | bytes 1572872 | tf_op jit(solution)/shard_map/ppermute | solution.py:29
  131.8 18.5 %shard_map.104 = (f32[512,2048]{1,0:T(8,128)}, f32[512,2048]{1,0:T(8,128)}) custom-call(bf16[512,2048]{1,0:T(8,128)(2,1)} %get-tuple-element.84.q_high, bf16[512,2048]{1,0:T(8,128)(2,1)} %get-tuple-element.85.q_low, s32[1,2048]{1,0:T(1,128)} %sub.45.targets, f32[160,2048]{1,0:T(8,128)} %get-tuple-element.92.refs_0_, f32[160,2048]{1,0:T(8,128)} %get-tuple-element.93.refs_1_, ...), custom_call_target="tpu_custom_call" | custom-call | flops 6710886400 | bytes 4718592 | tf_op jit(solution)/shard_map/pallas_call | solution.py:455
  153.8 1.5 collective-permute-done.26.refs_3_
  156.9 9.0 %shard_map.107 = (f32[512,2048]{1,0:T(8,128)}, f32[512,2048]{1,0:T(8,128)}) custom-call(bf16[512,2048]{1,0:T(8,128)(2,1)} %get-tuple-element.84.q_high, bf16[512,2048]{1,0:T(8,128)(2,1)} %get-tuple-element.85.q_low, s32[1,2048]{1,0:T(1,128)} %sub.45.targets, f32[512,2048]{1,0:T(8,128)} %get-tuple-element.98.refs_5_.factor_in, ...), custom_call_target="tpu_custom_call" | custom-call | flops 1342177280 | bytes 4718592 | tf_op jit(solution)/shard_map/pallas_call | solution.py:455
  167.5 2.3 %collective-permute-done.30.refs_6_ = f32[64,2048]{1,0:T(8,128)S(1)} collective-permute-done((f32[64,2048]{1,0:T(8,128)}, f32[64,2048]{1,0:T(8,128)S(1)}, u32[]{:S(2)}, u32[]{:S(2)}) %collective-permute-start.30) | collective-permute-done | bytes 524320 | tf_op jit(solution)/shard_map/ppermute | solution.py:31
  170.6 13.9 %shard_map.109 = (f32[512,2048]{1,0:T(8,128)}, f32[512,2048]{1,0:T(8,128)}) custom-call(bf16[512,2048]{1,0:T(8,128)(2,1)} %get-tuple-element.84.q_high, bf16[512,2048]{1,0:T(8,128)(2,1)} %get-tuple-element.85.q_low, s32[1,2048]{1,0:T(1,128)} %sub.45.targets, f32[512,2048]{1,0:T(8,128)} %get-tuple-element.106.refs_2_.factor_in, ...), custom_call_target="tpu_custom_call" | custom-call | flops 4294967296 | bytes 5242880 | tf_op jit(solution)/shard_map/pallas_call | solution.py:455
  (132 shorter events, 29.5 us)
Async XLA Ops:
  2.5 11.9 %collective-permute-start.2 = (f32[64,512]{1,0:T(8,128)S(1)}, f32[64,512]{1,0:T(8,128)S(1)}, u32[]{:S(2)}, u32[]{:S(2)}) collective-permute-start(f32[64,512]{1,0:T(8,128)S(1)} %slice_select_fusion.refs_0_), channel_id=1, source_target_pairs={{0,6},{1,7},{2,4},{3,5},{4,2},{5,3},{6,0},{7,1},{8,14},{9,15},{10,... | collective-permute-start | bytes 393224 | tf_op jit(solution)/shard_map/ppermute | solution.py:29
  7.6 7.4 %collective-permute-start.1 = (f32[64,512]{1,0:T(8,128)S(1)}, f32[64,512]{1,0:T(8,128)S(1)}, u32[]{:S(2)}, u32[]{:S(2)}) collective-permute-start(f32[64,512]{1,0:T(8,128)S(1)} %slice_select_fusion.refs_0_), channel_id=1, source_target_pairs={{0,2},{1,3},{2,0},{3,1},{4,6},{5,7},{6,4},{7,5},{8,10},{9,11},{10,... | collective-permute-start | bytes 393224 | tf_op jit(solution)/shard_map/ppermute | solution.py:29
  7.6 11.1 %collective-permute-start = (f32[64,512]{1,0:T(8,128)S(1)}, f32[64,512]{1,0:T(8,128)S(1)}, u32[]{:S(2)}, u32[]{:S(2)}) collective-permute-start(f32[64,512]{1,0:T(8,128)S(1)} %slice_select_fusion.refs_0_), channel_id=1, source_target_pairs={{0,4},{1,5},{2,6},{3,7},{4,0},{5,1},{6,2},{7,3},{8,12},{9,13},{10,... | collective-permute-start | bytes 393224 | tf_op jit(solution)/shard_map/ppermute | solution.py:29
  20.1 10.3 %collective-permute-start.5 = (f32[256,256]{1,0:T(8,128)}, f32[256,256]{1,0:T(8,128)}, u32[]{:S(2)}, u32[]{:S(2)}) collective-permute-start(f32[256,256]{1,0:T(8,128)} %get-tuple-element.64.refs_0_), channel_id=1, source_target_pairs={{0,1},{1,0},{2,3},{3,2},{4,5},{5,4},{6,7},{7,6},{8,9},{9,8},{10,11... | collective-permute-start | bytes 786440 | tf_op jit(solution)/shard_map/ppermute | solution.py:29
  21.6 10.5 %collective-permute-start.3 = (f32[256,256]{1,0:T(8,128)S(1)}, f32[256,256]{1,0:T(8,128)}, u32[]{:S(2)}, u32[]{:S(2)}) collective-permute-start(f32[256,256]{1,0:T(8,128)S(1)} %get-tuple-element.60.refs_0_), channel_id=1, source_target_pairs={{0,16},{8,24},{16,0},{24,8},{1,17},{9,25},{17,1},{25,9},{2,18},{10... | collective-permute-start | bytes 786440 | tf_op jit(solution)/shard_map/ppermute | solution.py:31
  23.1 14.8 %collective-permute-start.7 = (f32[64,2048]{1,0:T(8,128)}, f32[64,2048]{1,0:T(8,128)S(1)}, u32[]{:S(2)}, u32[]{:S(2)}) collective-permute-start(f32[64,2048]{1,0:T(8,128)} %shard_map.90), channel_id=1, source_target_pairs={{0,2},{1,3},{2,0},{3,1},{4,6},{5,7},{6,4},{7,5},{8,10},{9,11},{10,... | collective-permute-start | bytes 1572872 | tf_op jit(solution)/shard_map/ppermute | solution.py:29
  31.5 16.4 %collective-permute-start.6 = (f32[512,256]{1,0:T(8,128)S(1)}, f32[512,256]{1,0:T(8,128)S(1)}, u32[]{:S(2)}, u32[]{:S(2)}) collective-permute-start(f32[512,256]{1,0:T(8,128)S(1)} %get-tuple-element.65.b_mine), channel_id=1, source_target_pairs={{0,16},{8,24},{16,0},{24,8},{1,17},{9,25},{17,1},{25,9},{2,18},{10... | collective-permute-start | bytes 1572872 | tf_op jit(solution)/shard_map/ppermute | solution.py:31
  34.3 13.6 %collective-permute-start.4 = (f32[512,256]{1,0:T(8,128)S(1)}, f32[512,256]{1,0:T(8,128)S(1)}, u32[]{:S(2)}, u32[]{:S(2)}) collective-permute-start(f32[512,256]{1,0:T(8,128)S(1)} %get-tuple-element.63.a_mine), channel_id=1, source_target_pairs={{0,1},{1,0},{2,3},{3,2},{4,5},{5,4},{6,7},{7,6},{8,9},{9,8},{10,11... | collective-permute-start | bytes 1572872 | tf_op jit(solution)/shard_map/ppermute | solution.py:29
  34.8 13.1 %collective-permute-start.8 = (f32[32,2048]{1,0:T(8,128)}, f32[32,2048]{1,0:T(8,128)S(1)}, u32[]{:S(2)}, u32[]{:S(2)}) collective-permute-start(f32[32,2048]{1,0:T(8,128)} %shard_map.91), channel_id=1, source_target_pairs={{0,4},{1,5},{2,6},{3,7},{4,0},{5,1},{6,2},{7,3},{8,12},{9,13},{10,... | collective-permute-start | bytes 786440 | tf_op jit(solution)/shard_map/ppermute | solution.py:29
  52.5 8.9 %collective-permute-start.10 = (f32[1024,512]{1,0:T(8,128)}, f32[1024,512]{1,0:T(8,128)}, u32[]{:S(2)}, u32[]{:S(2)}) collective-permute-start(f32[1024,512]{1,0:T(8,128)} %get-tuple-element.70), channel_id=1, source_target_pairs={{0,8},{8,0},{16,24},{24,16},{1,9},{9,1},{17,25},{25,17},{2,10},{10... | collective-permute-start | bytes 6291464 | tf_op jit(solution)/shard_map/ppermute | solution.py:31
  52.5 7.5 %collective-permute-start.9 = (f32[512,512]{1,0:T(8,128)}, f32[512,512]{1,0:T(8,128)}, u32[]{:S(2)}, u32[]{:S(2)}) collective-permute-start(f32[512,512]{1,0:T(8,128)} %get-tuple-element.69.gram_a), channel_id=1, source_target_pairs={{0,8},{8,0},{16,24},{24,16},{1,9},{9,1},{17,25},{25,17},{2,10},{10... | collective-permute-start | bytes 3145736 | tf_op jit(solution)/shard_map/ppermute | solution.py:31
  53.1 38.3 %collective-permute-start.13 = (f32[32,2048]{1,0:T(8,128)}, f32[32,2048]{1,0:T(8,128)S(1)}, u32[]{:S(2)}, u32[]{:S(2)}) collective-permute-start(f32[32,2048]{1,0:T(8,128)} %shard_map.96), channel_id=1, source_target_pairs={{0,4},{1,5},{2,6},{3,7},{4,0},{5,1},{6,2},{7,3},{8,12},{9,13},{10,... | collective-permute-start | bytes 786440 | tf_op jit(solution)/shard_map/ppermute | solution.py:29
  53.2 38.2 %collective-permute-start.12 = (f32[64,2048]{1,0:T(8,128)}, f32[64,2048]{1,0:T(8,128)S(1)}, u32[]{:S(2)}, u32[]{:S(2)}) collective-permute-start(f32[64,2048]{1,0:T(8,128)} %shard_map.95), channel_id=1, source_target_pairs={{0,1},{1,0},{2,3},{3,2},{4,5},{5,4},{6,7},{7,6},{8,9},{9,8},{10,11... | collective-permute-start | bytes 1572872 | tf_op jit(solution)/shard_map/ppermute | solution.py:29
  54.7 36.8 %collective-permute-start.14 = (f32[64,2048]{1,0:T(8,128)}, f32[64,2048]{1,0:T(8,128)}, u32[]{:S(2)}, u32[]{:S(2)}) collective-permute-start(f32[64,2048]{1,0:T(8,128)} %shard_map.97), channel_id=1, source_target_pairs={{0,5},{1,4},{2,7},{3,6},{4,1},{5,0},{6,3},{7,2},{8,13},{9,12},{10,... | collective-permute-start | bytes 1572872 | tf_op jit(solution)/shard_map/ppermute | solution.py:29
  60.0 31.5 %collective-permute-start.11 = (f32[160,2048]{1,0:T(8,128)}, f32[160,2048]{1,0:T(8,128)}, u32[]{:S(2)}, u32[]{:S(2)}) collective-permute-start(f32[160,2048]{1,0:T(8,128)} %get-tuple-element.75.refs_0_), channel_id=1, source_target_pairs={{0,16},{8,24},{16,0},{24,8},{1,17},{9,25},{17,1},{25,9},{2,18},{10... | collective-permute-start | bytes 3932168 | tf_op jit(solution)/shard_map/ppermute | solution.py:31
  94.8 29.9 %collective-permute-start.16 = (f32[160,2048]{1,0:T(8,128)}, f32[160,2048]{1,0:T(8,128)}, u32[]{:S(2)}, u32[]{:S(2)}) collective-permute-start(f32[160,2048]{1,0:T(8,128)} %get-tuple-element.88.refs_3_), channel_id=1, source_target_pairs={{0,16},{8,24},{16,0},{24,8},{1,17},{9,25},{17,1},{25,9},{2,18},{10... | collective-permute-start | bytes 3932168 | tf_op jit(solution)/shard_map/ppermute | solution.py:31
  95.4 29.2 %collective-permute-start.15 = (f32[160,2048]{1,0:T(8,128)}, f32[160,2048]{1,0:T(8,128)}, u32[]{:S(2)}, u32[]{:S(2)}) collective-permute-start(f32[160,2048]{1,0:T(8,128)} %get-tuple-element.86.refs_0_), channel_id=1, source_target_pairs={{0,8},{8,0},{16,24},{24,16},{1,9},{9,1},{17,25},{25,17},{2,10},{10... | collective-permute-start | bytes 3932168 | tf_op jit(solution)/shard_map/ppermute | solution.py:31
  96.3 19.0 %collective-permute-start.17 = (f32[64,2048]{1,0:T(8,128)}, f32[64,2048]{1,0:T(8,128)S(1)}, u32[]{:S(2)}, u32[]{:S(2)}) collective-permute-start(f32[64,2048]{1,0:T(8,128)} %shard_map.101), channel_id=1, source_target_pairs={{0,3},{1,2},{2,1},{3,0},{4,7},{5,6},{6,5},{7,4},{8,11},{9,10},{10,... | collective-permute-start | bytes 1572872 | tf_op jit(solution)/shard_map/ppermute | solution.py:29
  96.7 26.1 %collective-permute-start.18 = (f32[64,2048]{1,0:T(8,128)}, f32[64,2048]{1,0:T(8,128)}, u32[]{:S(2)}, u32[]{:S(2)}) collective-permute-start(f32[64,2048]{1,0:T(8,128)} %shard_map.102), channel_id=1, source_target_pairs={{0,6},{1,7},{2,4},{3,5},{4,2},{5,3},{6,0},{7,1},{8,14},{9,15},{10,... | collective-permute-start | bytes 1572872 | tf_op jit(solution)/shard_map/ppermute | solution.py:29
  125.2 6.6 %collective-permute-start.21 = (f32[160,2048]{1,0:T(8,128)}, f32[160,2048]{1,0:T(8,128)}, u32[]{:S(2)}, u32[]{:S(2)}) collective-permute-start(f32[160,2048]{1,0:T(8,128)} %get-tuple-element.96.refs_5_), channel_id=1, source_target_pairs={{0,8},{8,0},{16,24},{24,16},{1,9},{9,1},{17,25},{25,17},{2,10},{10... | collective-permute-start | bytes 3932168 | tf_op jit(solution)/shard_map/ppermute | solution.py:31
  125.9 25.8 %collective-permute-start.22 = (f32[64,2048]{1,0:T(8,128)}, f32[64,2048]{1,0:T(8,128)}, u32[]{:S(2)}, u32[]{:S(2)}) collective-permute-start(f32[64,2048]{1,0:T(8,128)} %get-tuple-element.97.refs_8_.refs_1_.refs_0_), channel_id=1, source_target_pairs={{0,16},{8,24},{16,0},{24,8},{1,17},{9,25},{17,1},{25,9},{2,18},{10... | collective-permute-start | bytes 1572872 | tf_op jit(solution)/shard_map/ppermute | solution.py:31
  126.9 23.4 %collective-permute-start.24 = (f32[64,2048]{1,0:T(8,128)}, f32[64,2048]{1,0:T(8,128)S(1)}, u32[]{:S(2)}, u32[]{:S(2)}) collective-permute-start(f32[64,2048]{1,0:T(8,128)} %shard_map.105), channel_id=1, source_target_pairs={{0,7},{1,6},{2,5},{3,4},{4,3},{5,2},{6,1},{7,0},{8,15},{9,14},{10,... | collective-permute-start | bytes 1572872 | tf_op jit(solution)/shard_map/ppermute | solution.py:29
  129.2 22.5 %collective-permute-start.23 = (f32[64,2048]{1,0:T(8,128)}, f32[64,2048]{1,0:T(8,128)}, u32[]{:S(2)}, u32[]{:S(2)}) collective-permute-start(f32[64,2048]{1,0:T(8,128)} %get-tuple-element.100.refs_2_), channel_id=1, source_target_pairs={{0,16},{8,24},{16,0},{24,8},{1,17},{9,25},{17,1},{25,9},{2,18},{10... | collective-permute-start | bytes 1572872 | tf_op jit(solution)/shard_map/ppermute | solution.py:31
  152.7 14.2 %collective-permute-start.29 = (f32[64,2048]{1,0:T(8,128)}, f32[64,2048]{1,0:T(8,128)}, u32[]{:S(2)}, u32[]{:S(2)}) collective-permute-start(f32[64,2048]{1,0:T(8,128)} %get-tuple-element.110.refs_0_), channel_id=1, source_target_pairs={{0,16},{8,24},{16,0},{24,8},{1,17},{9,25},{17,1},{25,9},{2,18},{10... | collective-permute-start | bytes 1572872 | tf_op jit(solution)/shard_map/ppermute | solution.py:31
  (29 other events, 124.9 us)

commit v6 on v5

--- a/solution.py
+++ b/solution.py
@@ -211,7 +211,8 @@
             after = after - weight * jnp.broadcast_to(top[i : i + 1], (SUB, 2 * NB))
         return after, top
 
-    lax.fori_loop(0, NB // SUB, body, (work[:SUB, :], jnp.zeros((SUB, 2 * NB), F32)))
+    start = (work[:SUB, :], jnp.zeros((SUB, 2 * NB), F32))
+    lax.fori_loop(0, NB // SUB, body, start, unroll=2)
 
 
 def factor_kernel(gram_a, gram_b, *refs):

time: 185 us -> 185 us (level)
  Pallas kernels: 110 us -> 107 us
  waiting for transfers between devices: 32.2 us -> 35 us
    pallas_call x1, Pallas kernels: 30 us -> 27.2 us  [inverse_factor(): pl.pallas_call(factor_kernel, out_shape=[jax.ShapeDtypeStruct((n, n), F32...]
    ppermute x13, waiting for transfers between devices: 21.8 us -> 24.5 us  [swap(): return lax.ppermute(x, 'ct', [(c, c ^ ct_bit) for c in range(n_ct)])]
  transfers between devices with their start and end apart: 32 -> 32, of which waited for: 13 -> 13; matrix products, arithmetic and copies ran while one was open for 3% -> 3% of each run, Pallas kernels for 48% -> 47%
where the time goes in v6:
time: 185 us; the launch traced here: 184 us
  Pallas kernels  107 us (58%)
  waiting for transfers between devices  35 us (19%)
  starting transfers between devices  30.7 us (17%)
  local copies, waits for them, and re-layouts  7.84 us (4%)
  other arithmetic  2.27 us (1%)
    pallas_call x3, Pallas kernels, mix_call(): pl.pallas_call(functools.partial(kernel, len(pieces), spots), grid=(block...  41.4 us
    pallas_call x1, Pallas kernels, inverse_factor(): pl.pallas_call(factor_kernel, out_shape=[jax.ShapeDtypeStruct((n, n), F32...  27.2 us
    ppermute x13, waiting for transfers between devices, swap(): return lax.ppermute(x, 'ct', [(c, c ^ ct_bit) for c in range(n_ct)])  24.5 us
    ppermute x13, starting transfers between devices, swap(): return lax.ppermute(x, 'ct', [(c, c ^ ct_bit) for c in range(n_ct)])  19.4 us
    pallas_call x1, Pallas kernels, basis_rows(): pl.pallas_call(functools.partial(basis_kernel, len(inverse), len(tokens))...  15.8 us
    ppermute x19, starting transfers between devices, swap(): return lax.ppermute(x, 'rt', [(r, r ^ rt_bit) for r in range(n_rt)])  11.3 us
    pallas_call x2, Pallas kernels, widen(): pl.pallas_call(functools.partial(widen_kernel, block_cols // STEP, window...  10.7 us
    ppermute x19, waiting for transfers between devices, swap(): return lax.ppermute(x, 'rt', [(r, r ^ rt_bit) for r in range(n_rt)])  10.5 us
  transfers between devices with their start and end apart: 32, of which 13 were waited for; matrix products, arithmetic and copies ran while one was open for 3% of the time, Pallas kernels for 47%

profile of v6, /device:TPU:0, one launch (start us, length us, event | category | flops | bytes accessed | tf_op | source)
XLA Modules:
  0.0 184.2 jit_solution(8817351480691953403)
XLA Ops:
  2.5 5.1 %collective-permute-start.2 = (f32[64,512]{1,0:T(8,128)S(1)}, f32[64,512]{1,0:T(8,128)S(1)}, u32[]{:S(2)}, u32[]{:S(2)}) collective-permute-start(f32[64,512]{1,0:T(8,128)S(1)} %slice_select_fusion.refs_0_), channel_id=1, source_target_pairs={{0,6},{1,7},{2,4},{3,5},{4,2},{5,3},{6,0},{7,1},{8,14},{9,15},{10,... | collective-permute-start | bytes 393224 | tf_op jit(solution)/shard_map/ppermute | solution.py:29
  10.9 3.4 %shard_map.85 = (f32[64,2048]{1,0:T(8,128)}, f32[8,128]{1,0:T(8,128)}) custom-call(s32[66]{0:T(128)} %pad_add_fusion.info, f32[64,12288]{1,0:T(8,128)} %child.3, s32[1,12288]{1,0:T(1,128)} %copy-done.17, s32[1,12288]{1,0:T(1,128)} %bitcast.19), custom_call_target="tpu_custom_call" | custom-call | flops 201326592 | bytes 3670016 | tf_op jit(solution)/shard_map/pallas_call | solution.py:113
  15.0 3.7 %collective-permute-done.refs_1_ = f32[64,512]{1,0:T(8,128)S(1)} collective-permute-done((f32[64,512]{1,0:T(8,128)S(1)}, f32[64,512]{1,0:T(8,128)S(1)}, u32[]{:S(2)}, u32[]{:S(2)}) %collective-permute-start) | collective-permute-done | bytes 131104 | tf_op jit(solution)/shard_map/ppermute | solution.py:29
  20.1 1.5 collective-permute-start.5
  23.1 7.3 %shard_map.87 = (f32[64,2048]{1,0:T(8,128)}, f32[64,2048]{1,0:T(8,128)}, f32[64,2048]{1,0:T(8,128)}, f32[64,2048]{1,0:T(8,128)}, f32[64,2048]{1,0:T(8,128)}, /*i...) custom-call(s32[66]{0:T(128)} %pad_add_fusion.info, f32[64,12288]{1,0:T(8,128)} %child.3, ...), custom_call_target="tpu_custom_call" | custom-call | flops 1409286144 | bytes 6815744 | tf_op jit(solution)/shard_map/pallas_call | solution.py:113
  34.8 3.0 %collective-permute-start.8 = (f32[32,2048]{1,0:T(8,128)}, f32[32,2048]{1,0:T(8,128)S(1)}, u32[]{:S(2)}, u32[]{:S(2)}) collective-permute-start(f32[32,2048]{1,0:T(8,128)} %shard_map.91), channel_id=1, source_target_pairs={{0,4},{1,5},{2,6},{3,7},{4,0},{5,1},{6,2},{7,3},{8,12},{9,13},{10,... | collective-permute-start | bytes 786440 | tf_op jit(solution)/shard_map/ppermute | solution.py:29
  37.9 10.0 %collective-permute-done.8.refs_1_.refs_2_ = f32[32,2048]{1,0:T(8,128)S(1)} collective-permute-done((f32[32,2048]{1,0:T(8,128)}, f32[32,2048]{1,0:T(8,128)S(1)}, u32[]{:S(2)}, u32[]{:S(2)}) %collective-permute-start.8) | collective-permute-done | bytes 262176 | tf_op jit(solution)/shard_map/ppermute | solution.py:29
  47.9 4.6 %shard_map.92 = (f32[1024,512]{1,0:T(8,128)}, f32[512,512]{1,0:T(8,128)}, f32[8,128]{1,0:T(8,128)S(1)}) custom-call(f32[512,256]{1,0:T(8,128)S(1)} %get-tuple-element.63.a_mine, f32[512,256]{1,0:T(8,128)S(1)} %collective-permute-done.4.a_other, f32[512,256]{1,0:T(8,128)S(1)} %get-tuple-element.65.b_mine, f32[512,256]{1,0:T(8,128)S(1)} %collective-permute-done.6.b_other, ...), custom_call_target="tpu_custom_call" | custom-call | flops 536870912 | bytes 524288 | tf_op jit(solution)/shard_map/pallas_call | solution.py:314
  54.7 2.9 %collective-permute-start.14 = (f32[64,2048]{1,0:T(8,128)}, f32[64,2048]{1,0:T(8,128)}, u32[]{:S(2)}, u32[]{:S(2)}) collective-permute-start(f32[64,2048]{1,0:T(8,128)} %shard_map.97), channel_id=1, source_target_pairs={{0,5},{1,4},{2,7},{3,6},{4,1},{5,0},{6,3},{7,2},{8,13},{9,12},{10,... | collective-permute-start | bytes 1572872 | tf_op jit(solution)/shard_map/ppermute | solution.py:29
  57.5 2.4 %shard_map.93 = (f32[160,2048]{1,0:T(8,128)}, f32[8,128]{1,0:T(8,128)}) custom-call(f32[64,2048]{1,0:T(8,128)} %get-tuple-element.71.refs_0_, f32[64,2048]{1,0:T(8,128)} %copy-done.2, f32[32,2048]{1,0:T(8,128)} %copy-done.3, f32[8,128]{1,0:T(8,128)} %copy-done.4), custom_call_target="tpu_custom_call" | custom-call | bytes 2621440 | tf_op jit(solution)/shard_map/pallas_call | solution.py:285
  61.4 27.2 %shard_map.94 = (f32[512,512]{1,0:T(8,128)}, f32[8,128]{1,0:T(8,128)}) custom-call(f32[512,512]{1,0:T(8,128)} %get-tuple-element.69.gram_a, f32[512,512]{1,0:T(8,128)} %collective-permute-done.9.gram_b, f32[1024,512]{1,0:T(8,128)} %collective-permute-done.10.refs_0_, f32[8,128]{1,0:T(8,128)} %get-tuple-element.73.refs_1_), custom_call_target="tpu_custom_call" | custom-call | flops 30000001024 | bytes 3145728 | tf_op jit(solution)/shard_map/pallas_call | solution.py:236
  88.6 2.0 %collective-permute-done.14.refs_4_ = f32[64,2048]{1,0:T(8,128)} collective-permute-done((f32[64,2048]{1,0:T(8,128)}, f32[64,2048]{1,0:T(8,128)}, u32[]{:S(2)}, u32[]{:S(2)}) %collective-permute-start.14) | collective-permute-done | bytes 524320 | tf_op jit(solution)/shard_map/ppermute | solution.py:29
  90.7 2.4 %shard_map.99 = (f32[160,2048]{1,0:T(8,128)}, f32[8,128]{1,0:T(8,128)}) custom-call(f32[32,2048]{1,0:T(8,128)} %get-tuple-element.80.refs_0_, f32[64,2048]{1,0:T(8,128)} %get-tuple-element.81.refs_1_, f32[64,2048]{1,0:T(8,128)} %get-tuple-element.82.refs_2_), custom_call_target="tpu_custom_call" | custom-call | bytes 2621440 | tf_op jit(solution)/shard_map/pallas_call | solution.py:285
  95.6 2.0 %collective-permute-start.18 = (f32[64,2048]{1,0:T(8,128)}, f32[64,2048]{1,0:T(8,128)}, u32[]{:S(2)}, u32[]{:S(2)}) collective-permute-start(f32[64,2048]{1,0:T(8,128)} %shard_map.102), channel_id=1, source_target_pairs={{0,6},{1,7},{2,4},{3,5},{4,2},{5,3},{6,0},{7,1},{8,14},{9,15},{10,... | collective-permute-start | bytes 1572872 | tf_op jit(solution)/shard_map/ppermute | solution.py:29
  98.4 15.8 %shard_map.100 = (bf16[512,2048]{1,0:T(8,128)(2,1)}, bf16[512,2048]{1,0:T(8,128)(2,1)}, f32[512,512]{1,0:T(8,128)}, bf16[512,512]{1,0:T(8,128)(2,1)}, bf16[512,512]{1,0:T(8,128)(2,1)}) custom-call(f32[512,512]{1,0:T(8,128)} %get-tuple-element.74.refs_0_, f32[2,2,4,64,512]{4,3,2,1,0:T(8,128)} %bitcast.5.refs_1_, f32[2,2,4,64,512]{4,3,2,1,0:T(8,128)} %bitcast.6.refs_2_, ...), custom_call_target="tpu_custom_call" | custom-call | flops 4294967296 | bytes 6291456 | tf_op jit(solution)/shard_map/pallas_call | solution.py:377
  114.2 8.0 %collective-permute-done.17.refs_5_ = f32[64,2048]{1,0:T(8,128)S(1)} collective-permute-done((f32[64,2048]{1,0:T(8,128)}, f32[64,2048]{1,0:T(8,128)S(1)}, u32[]{:S(2)}, u32[]{:S(2)}) %collective-permute-start.17) | collective-permute-done | bytes 524320 | tf_op jit(solution)/shard_map/ppermute | solution.py:29
  122.2 1.9 %collective-permute-done.16.refs_4_ = f32[160,2048]{1,0:T(8,128)} collective-permute-done((f32[160,2048]{1,0:T(8,128)}, f32[160,2048]{1,0:T(8,128)}, u32[]{:S(2)}, u32[]{:S(2)}) %collective-permute-start.16) | collective-permute-done | bytes 1310752 | tf_op jit(solution)/shard_map/ppermute | solution.py:31
  125.4 1.5 collective-permute-start.22
  126.9 2.0 %collective-permute-start.24 = (f32[64,2048]{1,0:T(8,128)}, f32[64,2048]{1,0:T(8,128)S(1)}, u32[]{:S(2)}, u32[]{:S(2)}) collective-permute-start(f32[64,2048]{1,0:T(8,128)} %shard_map.105), channel_id=1, source_target_pairs={{0,7},{1,6},{2,5},{3,4},{4,3},{5,2},{6,1},{7,0},{8,15},{9,14},{10,... | collective-permute-start | bytes 1572872 | tf_op jit(solution)/shard_map/ppermute | solution.py:29
  129.5 1.7 collective-permute-done.21.refs_7_
  131.3 18.5 %shard_map.104 = (f32[512,2048]{1,0:T(8,128)}, f32[512,2048]{1,0:T(8,128)}) custom-call(bf16[512,2048]{1,0:T(8,128)(2,1)} %get-tuple-element.84.q_high, bf16[512,2048]{1,0:T(8,128)(2,1)} %get-tuple-element.85.q_low, s32[1,2048]{1,0:T(1,128)} %sub.45.targets, f32[160,2048]{1,0:T(8,128)} %get-tuple-element.92.refs_0_, f32[160,2048]{1,0:T(8,128)} %get-tuple-element.93.refs_1_, ...), custom_call_target="tpu_custom_call" | custom-call | flops 6710886400 | bytes 4718592 | tf_op jit(solution)/shard_map/pallas_call | solution.py:456
  156.4 9.0 %shard_map.107 = (f32[512,2048]{1,0:T(8,128)}, f32[512,2048]{1,0:T(8,128)}) custom-call(bf16[512,2048]{1,0:T(8,128)(2,1)} %get-tuple-element.84.q_high, bf16[512,2048]{1,0:T(8,128)(2,1)} %get-tuple-element.85.q_low, s32[1,2048]{1,0:T(1,128)} %sub.45.targets, f32[512,2048]{1,0:T(8,128)} %get-tuple-element.98.refs_5_.factor_in, ...), custom_call_target="tpu_custom_call" | custom-call | flops 1342177280 | bytes 4718592 | tf_op jit(solution)/shard_map/pallas_call | solution.py:456
  167.0 2.3 %collective-permute-done.30.refs_6_ = f32[64,2048]{1,0:T(8,128)S(1)} collective-permute-done((f32[64,2048]{1,0:T(8,128)}, f32[64,2048]{1,0:T(8,128)S(1)}, u32[]{:S(2)}, u32[]{:S(2)}) %collective-permute-start.30) | collective-permute-done | bytes 524320 | tf_op jit(solution)/shard_map/ppermute | solution.py:31
  170.1 13.9 %shard_map.109 = (f32[512,2048]{1,0:T(8,128)}, f32[512,2048]{1,0:T(8,128)}) custom-call(bf16[512,2048]{1,0:T(8,128)(2,1)} %get-tuple-element.84.q_high, bf16[512,2048]{1,0:T(8,128)(2,1)} %get-tuple-element.85.q_low, s32[1,2048]{1,0:T(1,128)} %sub.45.targets, f32[512,2048]{1,0:T(8,128)} %get-tuple-element.106.refs_2_.factor_in, ...), custom_call_target="tpu_custom_call" | custom-call | flops 4294967296 | bytes 5242880 | tf_op jit(solution)/shard_map/pallas_call | solution.py:456
  (132 shorter events, 30.8 us)
Async XLA Ops:
  2.5 11.9 %collective-permute-start.2 = (f32[64,512]{1,0:T(8,128)S(1)}, f32[64,512]{1,0:T(8,128)S(1)}, u32[]{:S(2)}, u32[]{:S(2)}) collective-permute-start(f32[64,512]{1,0:T(8,128)S(1)} %slice_select_fusion.refs_0_), channel_id=1, source_target_pairs={{0,6},{1,7},{2,4},{3,5},{4,2},{5,3},{6,0},{7,1},{8,14},{9,15},{10,... | collective-permute-start | bytes 393224 | tf_op jit(solution)/shard_map/ppermute | solution.py:29
  7.6 7.4 %collective-permute-start.1 = (f32[64,512]{1,0:T(8,128)S(1)}, f32[64,512]{1,0:T(8,128)S(1)}, u32[]{:S(2)}, u32[]{:S(2)}) collective-permute-start(f32[64,512]{1,0:T(8,128)S(1)} %slice_select_fusion.refs_0_), channel_id=1, source_target_pairs={{0,2},{1,3},{2,0},{3,1},{4,6},{5,7},{6,4},{7,5},{8,10},{9,11},{10,... | collective-permute-start | bytes 393224 | tf_op jit(solution)/shard_map/ppermute | solution.py:29
  7.6 11.1 %collective-permute-start = (f32[64,512]{1,0:T(8,128)S(1)}, f32[64,512]{1,0:T(8,128)S(1)}, u32[]{:S(2)}, u32[]{:S(2)}) collective-permute-start(f32[64,512]{1,0:T(8,128)S(1)} %slice_select_fusion.refs_0_), channel_id=1, source_target_pairs={{0,4},{1,5},{2,6},{3,7},{4,0},{5,1},{6,2},{7,3},{8,12},{9,13},{10,... | collective-permute-start | bytes 393224 | tf_op jit(solution)/shard_map/ppermute | solution.py:29
  20.1 10.3 %collective-permute-start.5 = (f32[256,256]{1,0:T(8,128)}, f32[256,256]{1,0:T(8,128)}, u32[]{:S(2)}, u32[]{:S(2)}) collective-permute-start(f32[256,256]{1,0:T(8,128)} %get-tuple-element.64.refs_0_), channel_id=1, source_target_pairs={{0,1},{1,0},{2,3},{3,2},{4,5},{5,4},{6,7},{7,6},{8,9},{9,8},{10,11... | collective-permute-start | bytes 786440 | tf_op jit(solution)/shard_map/ppermute | solution.py:29
  21.6 10.5 %collective-permute-start.3 = (f32[256,256]{1,0:T(8,128)S(1)}, f32[256,256]{1,0:T(8,128)}, u32[]{:S(2)}, u32[]{:S(2)}) collective-permute-start(f32[256,256]{1,0:T(8,128)S(1)} %get-tuple-element.60.refs_0_), channel_id=1, source_target_pairs={{0,16},{8,24},{16,0},{24,8},{1,17},{9,25},{17,1},{25,9},{2,18},{10... | collective-permute-start | bytes 786440 | tf_op jit(solution)/shard_map/ppermute | solution.py:31
  23.1 14.8 %collective-permute-start.7 = (f32[64,2048]{1,0:T(8,128)}, f32[64,2048]{1,0:T(8,128)S(1)}, u32[]{:S(2)}, u32[]{:S(2)}) collective-permute-start(f32[64,2048]{1,0:T(8,128)} %shard_map.90), channel_id=1, source_target_pairs={{0,2},{1,3},{2,0},{3,1},{4,6},{5,7},{6,4},{7,5},{8,10},{9,11},{10,... | collective-permute-start | bytes 1572872 | tf_op jit(solution)/shard_map/ppermute | solution.py:29
  31.4 16.4 %collective-permute-start.6 = (f32[512,256]{1,0:T(8,128)S(1)}, f32[512,256]{1,0:T(8,128)S(1)}, u32[]{:S(2)}, u32[]{:S(2)}) collective-permute-start(f32[512,256]{1,0:T(8,128)S(1)} %get-tuple-element.65.b_mine), channel_id=1, source_target_pairs={{0,16},{8,24},{16,0},{24,8},{1,17},{9,25},{17,1},{25,9},{2,18},{10... | collective-permute-start | bytes 1572872 | tf_op jit(solution)/shard_map/ppermute | solution.py:31
  34.3 13.6 %collective-permute-start.4 = (f32[512,256]{1,0:T(8,128)S(1)}, f32[512,256]{1,0:T(8,128)S(1)}, u32[]{:S(2)}, u32[]{:S(2)}) collective-permute-start(f32[512,256]{1,0:T(8,128)S(1)} %get-tuple-element.63.a_mine), channel_id=1, source_target_pairs={{0,1},{1,0},{2,3},{3,2},{4,5},{5,4},{6,7},{7,6},{8,9},{9,8},{10,11... | collective-permute-start | bytes 1572872 | tf_op jit(solution)/shard_map/ppermute | solution.py:29
  34.8 13.1 %collective-permute-start.8 = (f32[32,2048]{1,0:T(8,128)}, f32[32,2048]{1,0:T(8,128)S(1)}, u32[]{:S(2)}, u32[]{:S(2)}) collective-permute-start(f32[32,2048]{1,0:T(8,128)} %shard_map.91), channel_id=1, source_target_pairs={{0,4},{1,5},{2,6},{3,7},{4,0},{5,1},{6,2},{7,3},{8,12},{9,13},{10,... | collective-permute-start | bytes 786440 | tf_op jit(solution)/shard_map/ppermute | solution.py:29
  52.5 8.9 %collective-permute-start.10 = (f32[1024,512]{1,0:T(8,128)}, f32[1024,512]{1,0:T(8,128)}, u32[]{:S(2)}, u32[]{:S(2)}) collective-permute-start(f32[1024,512]{1,0:T(8,128)} %get-tuple-element.70), channel_id=1, source_target_pairs={{0,8},{8,0},{16,24},{24,16},{1,9},{9,1},{17,25},{25,17},{2,10},{10... | collective-permute-start | bytes 6291464 | tf_op jit(solution)/shard_map/ppermute | solution.py:31
  52.5 7.5 %collective-permute-start.9 = (f32[512,512]{1,0:T(8,128)}, f32[512,512]{1,0:T(8,128)}, u32[]{:S(2)}, u32[]{:S(2)}) collective-permute-start(f32[512,512]{1,0:T(8,128)} %get-tuple-element.69.gram_a), channel_id=1, source_target_pairs={{0,8},{8,0},{16,24},{24,16},{1,9},{9,1},{17,25},{25,17},{2,10},{10... | collective-permute-start | bytes 3145736 | tf_op jit(solution)/shard_map/ppermute | solution.py:31
  53.1 35.5 %collective-permute-start.13 = (f32[32,2048]{1,0:T(8,128)}, f32[32,2048]{1,0:T(8,128)S(1)}, u32[]{:S(2)}, u32[]{:S(2)}) collective-permute-start(f32[32,2048]{1,0:T(8,128)} %shard_map.96), channel_id=1, source_target_pairs={{0,4},{1,5},{2,6},{3,7},{4,0},{5,1},{6,2},{7,3},{8,12},{9,13},{10,... | collective-permute-start | bytes 786440 | tf_op jit(solution)/shard_map/ppermute | solution.py:29
  53.2 35.4 %collective-permute-start.12 = (f32[64,2048]{1,0:T(8,128)}, f32[64,2048]{1,0:T(8,128)S(1)}, u32[]{:S(2)}, u32[]{:S(2)}) collective-permute-start(f32[64,2048]{1,0:T(8,128)} %shard_map.95), channel_id=1, source_target_pairs={{0,1},{1,0},{2,3},{3,2},{4,5},{5,4},{6,7},{7,6},{8,9},{9,8},{10,11... | collective-permute-start | bytes 1572872 | tf_op jit(solution)/shard_map/ppermute | solution.py:29
  54.7 36.0 %collective-permute-start.14 = (f32[64,2048]{1,0:T(8,128)}, f32[64,2048]{1,0:T(8,128)}, u32[]{:S(2)}, u32[]{:S(2)}) collective-permute-start(f32[64,2048]{1,0:T(8,128)} %shard_map.97), channel_id=1, source_target_pairs={{0,5},{1,4},{2,7},{3,6},{4,1},{5,0},{6,3},{7,2},{8,13},{9,12},{10,... | collective-permute-start | bytes 1572872 | tf_op jit(solution)/shard_map/ppermute | solution.py:29
  60.0 30.7 %collective-permute-start.11 = (f32[160,2048]{1,0:T(8,128)}, f32[160,2048]{1,0:T(8,128)}, u32[]{:S(2)}, u32[]{:S(2)}) collective-permute-start(f32[160,2048]{1,0:T(8,128)} %get-tuple-element.75.refs_0_), channel_id=1, source_target_pairs={{0,16},{8,24},{16,0},{24,8},{1,17},{9,25},{17,1},{25,9},{2,18},{10... | collective-permute-start | bytes 3932168 | tf_op jit(solution)/shard_map/ppermute | solution.py:31
  93.1 31.0 %collective-permute-start.16 = (f32[160,2048]{1,0:T(8,128)}, f32[160,2048]{1,0:T(8,128)}, u32[]{:S(2)}, u32[]{:S(2)}) collective-permute-start(f32[160,2048]{1,0:T(8,128)} %get-tuple-element.88.refs_3_), channel_id=1, source_target_pairs={{0,16},{8,24},{16,0},{24,8},{1,17},{9,25},{17,1},{25,9},{2,18},{10... | collective-permute-start | bytes 3932168 | tf_op jit(solution)/shard_map/ppermute | solution.py:31
  94.7 29.5 %collective-permute-start.15 = (f32[160,2048]{1,0:T(8,128)}, f32[160,2048]{1,0:T(8,128)}, u32[]{:S(2)}, u32[]{:S(2)}) collective-permute-start(f32[160,2048]{1,0:T(8,128)} %get-tuple-element.86.refs_0_), channel_id=1, source_target_pairs={{0,8},{8,0},{16,24},{24,16},{1,9},{9,1},{17,25},{25,17},{2,10},{10... | collective-permute-start | bytes 3932168 | tf_op jit(solution)/shard_map/ppermute | solution.py:31
  95.5 26.7 %collective-permute-start.17 = (f32[64,2048]{1,0:T(8,128)}, f32[64,2048]{1,0:T(8,128)S(1)}, u32[]{:S(2)}, u32[]{:S(2)}) collective-permute-start(f32[64,2048]{1,0:T(8,128)} %shard_map.101), channel_id=1, source_target_pairs={{0,3},{1,2},{2,1},{3,0},{4,7},{5,6},{6,5},{7,4},{8,11},{9,10},{10,... | collective-permute-start | bytes 1572872 | tf_op jit(solution)/shard_map/ppermute | solution.py:29
  95.6 26.6 %collective-permute-start.18 = (f32[64,2048]{1,0:T(8,128)}, f32[64,2048]{1,0:T(8,128)}, u32[]{:S(2)}, u32[]{:S(2)}) collective-permute-start(f32[64,2048]{1,0:T(8,128)} %shard_map.102), channel_id=1, source_target_pairs={{0,6},{1,7},{2,4},{3,5},{4,2},{5,3},{6,0},{7,1},{8,14},{9,15},{10,... | collective-permute-start | bytes 1572872 | tf_op jit(solution)/shard_map/ppermute | solution.py:29
  124.7 6.6 %collective-permute-start.21 = (f32[160,2048]{1,0:T(8,128)}, f32[160,2048]{1,0:T(8,128)}, u32[]{:S(2)}, u32[]{:S(2)}) collective-permute-start(f32[160,2048]{1,0:T(8,128)} %get-tuple-element.96.refs_5_), channel_id=1, source_target_pairs={{0,8},{8,0},{16,24},{24,16},{1,9},{9,1},{17,25},{25,17},{2,10},{10... | collective-permute-start | bytes 3932168 | tf_op jit(solution)/shard_map/ppermute | solution.py:31
  125.4 25.8 %collective-permute-start.22 = (f32[64,2048]{1,0:T(8,128)}, f32[64,2048]{1,0:T(8,128)}, u32[]{:S(2)}, u32[]{:S(2)}) collective-permute-start(f32[64,2048]{1,0:T(8,128)} %get-tuple-element.97.refs_8_.refs_1_.refs_0_), channel_id=1, source_target_pairs={{0,16},{8,24},{16,0},{24,8},{1,17},{9,25},{17,1},{25,9},{2,18},{10... | collective-permute-start | bytes 1572872 | tf_op jit(solution)/shard_map/ppermute | solution.py:31
  126.9 22.9 %collective-permute-start.24 = (f32[64,2048]{1,0:T(8,128)}, f32[64,2048]{1,0:T(8,128)S(1)}, u32[]{:S(2)}, u32[]{:S(2)}) collective-permute-start(f32[64,2048]{1,0:T(8,128)} %shard_map.105), channel_id=1, source_target_pairs={{0,7},{1,6},{2,5},{3,4},{4,3},{5,2},{6,1},{7,0},{8,15},{9,14},{10,... | collective-permute-start | bytes 1572872 | tf_op jit(solution)/shard_map/ppermute | solution.py:29
  128.9 22.3 %collective-permute-start.23 = (f32[64,2048]{1,0:T(8,128)}, f32[64,2048]{1,0:T(8,128)}, u32[]{:S(2)}, u32[]{:S(2)}) collective-permute-start(f32[64,2048]{1,0:T(8,128)} %get-tuple-element.100.refs_2_), channel_id=1, source_target_pairs={{0,16},{8,24},{16,0},{24,8},{1,17},{9,25},{17,1},{25,9},{2,18},{10... | collective-permute-start | bytes 1572872 | tf_op jit(solution)/shard_map/ppermute | solution.py:31
  152.3 14.2 %collective-permute-start.29 = (f32[64,2048]{1,0:T(8,128)}, f32[64,2048]{1,0:T(8,128)}, u32[]{:S(2)}, u32[]{:S(2)}) collective-permute-start(f32[64,2048]{1,0:T(8,128)} %get-tuple-element.110.refs_0_), channel_id=1, source_target_pairs={{0,16},{8,24},{16,0},{24,8},{1,17},{9,25},{17,1},{25,9},{2,18},{10... | collective-permute-start | bytes 1572872 | tf_op jit(solution)/shard_map/ppermute | solution.py:31
  (29 other events, 121.3 us)

commit v7 on v6

--- a/solution.py
+++ b/solution.py
@@ -11,7 +11,7 @@
 FRONT_COLS = 16384
 PANEL = 512
 STEP = 256
-WIDE = 512
+WIDE = 1024
 UNROLL = 8
 LANES = 128
 NB = 128

time: 185 us -> 186 us (level)
  transfers between devices with their start and end apart: 32 -> 32, of which waited for: 13 -> 13; matrix products, arithmetic and copies ran while one was open for 3% -> 3% of each run, Pallas kernels for 47% -> 46%
where the time goes in v7:
time: 186 us
  Pallas kernels  108 us (58%)
  waiting for transfers between devices  35 us (19%)
  starting transfers between devices  30.7 us (17%)
  local copies, waits for them, and re-layouts  8.29 us (4%)
  other arithmetic  2.27 us (1%)
    pallas_call x3, Pallas kernels, mix_call(): pl.pallas_call(functools.partial(kernel, len(pieces), spots), grid=(block...  42.5 us
    pallas_call x1, Pallas kernels, inverse_factor(): pl.pallas_call(factor_kernel, out_shape=[jax.ShapeDtypeStruct((n, n), F32...  27.2 us
    ppermute x13, waiting for transfers between devices, swap(): return lax.ppermute(x, 'ct', [(c, c ^ ct_bit) for c in range(n_ct)])  24.4 us
    ppermute x13, starting transfers between devices, swap(): return lax.ppermute(x, 'ct', [(c, c ^ ct_bit) for c in range(n_ct)])  19.4 us
    pallas_call x1, Pallas kernels, basis_rows(): pl.pallas_call(functools.partial(basis_kernel, len(inverse), len(tokens))...  15.8 us
    ppermute x19, starting transfers between devices, swap(): return lax.ppermute(x, 'rt', [(r, r ^ rt_bit) for r in range(n_rt)])  11.3 us
    pallas_call x2, Pallas kernels, widen(): pl.pallas_call(functools.partial(widen_kernel, block_cols // STEP, window...  10.7 us
    ppermute x19, waiting for transfers between devices, swap(): return lax.ppermute(x, 'rt', [(r, r ^ rt_bit) for r in range(n_rt)])  10.5 us
  transfers between devices with their start and end apart: 32, of which 13 were waited for; matrix products, arithmetic and copies ran while one was open for 3% of the time, Pallas kernels for 46%

profile of v7, /device:TPU:0, one launch (start us, length us, event | category | flops | bytes accessed | tf_op | source)
XLA Modules:
  0.0 185.7 jit_solution(2195268575853290459)
XLA Ops:
  2.5 5.1 %collective-permute-start.2 = (f32[64,512]{1,0:T(8,128)S(1)}, f32[64,512]{1,0:T(8,128)S(1)}, u32[]{:S(2)}, u32[]{:S(2)}) collective-permute-start(f32[64,512]{1,0:T(8,128)S(1)} %slice_select_fusion.refs_0_), channel_id=1, source_target_pairs={{0,6},{1,7},{2,4},{3,5},{4,2},{5,3},{6,0},{7,1},{8,14},{9,15},{10,... | collective-permute-start | bytes 393224 | tf_op jit(solution)/shard_map/ppermute | solution.py:29
  10.9 3.4 %shard_map.85 = (f32[64,2048]{1,0:T(8,128)}, f32[8,128]{1,0:T(8,128)}) custom-call(s32[66]{0:T(128)} %pad_add_fusion.info, f32[64,12288]{1,0:T(8,128)} %child.3, s32[1,12288]{1,0:T(1,128)} %copy-done.17, s32[1,12288]{1,0:T(1,128)} %bitcast.19), custom_call_target="tpu_custom_call" | custom-call | flops 201326592 | bytes 3670016 | tf_op jit(solution)/shard_map/pallas_call | solution.py:113
  15.0 3.7 %collective-permute-done.refs_1_ = f32[64,512]{1,0:T(8,128)S(1)} collective-permute-done((f32[64,512]{1,0:T(8,128)S(1)}, f32[64,512]{1,0:T(8,128)S(1)}, u32[]{:S(2)}, u32[]{:S(2)}) %collective-permute-start) | collective-permute-done | bytes 131104 | tf_op jit(solution)/shard_map/ppermute | solution.py:29
  20.1 1.5 collective-permute-start.5
  23.1 7.3 %shard_map.87 = (f32[64,2048]{1,0:T(8,128)}, f32[64,2048]{1,0:T(8,128)}, f32[64,2048]{1,0:T(8,128)}, f32[64,2048]{1,0:T(8,128)}, f32[64,2048]{1,0:T(8,128)}, /*i...) custom-call(s32[66]{0:T(128)} %pad_add_fusion.info, f32[64,12288]{1,0:T(8,128)} %child.3, ...), custom_call_target="tpu_custom_call" | custom-call | flops 1409286144 | bytes 6815744 | tf_op jit(solution)/shard_map/pallas_call | solution.py:113
  34.8 3.0 %collective-permute-start.8 = (f32[32,2048]{1,0:T(8,128)}, f32[32,2048]{1,0:T(8,128)S(1)}, u32[]{:S(2)}, u32[]{:S(2)}) collective-permute-start(f32[32,2048]{1,0:T(8,128)} %shard_map.91), channel_id=1, source_target_pairs={{0,4},{1,5},{2,6},{3,7},{4,0},{5,1},{6,2},{7,3},{8,12},{9,13},{10,... | collective-permute-start | bytes 786440 | tf_op jit(solution)/shard_map/ppermute | solution.py:29
  37.9 10.0 %collective-permute-done.8.refs_1_.refs_2_ = f32[32,2048]{1,0:T(8,128)S(1)} collective-permute-done((f32[32,2048]{1,0:T(8,128)}, f32[32,2048]{1,0:T(8,128)S(1)}, u32[]{:S(2)}, u32[]{:S(2)}) %collective-permute-start.8) | collective-permute-done | bytes 262176 | tf_op jit(solution)/shard_map/ppermute | solution.py:29
  47.9 4.6 %shard_map.92 = (f32[1024,512]{1,0:T(8,128)}, f32[512,512]{1,0:T(8,128)}, f32[8,128]{1,0:T(8,128)S(1)}) custom-call(f32[512,256]{1,0:T(8,128)S(1)} %get-tuple-element.63.a_mine, f32[512,256]{1,0:T(8,128)S(1)} %collective-permute-done.4.a_other, f32[512,256]{1,0:T(8,128)S(1)} %get-tuple-element.65.b_mine, f32[512,256]{1,0:T(8,128)S(1)} %collective-permute-done.6.b_other, ...), custom_call_target="tpu_custom_call" | custom-call | flops 536870912 | bytes 524288 | tf_op jit(solution)/shard_map/pallas_call | solution.py:314
  54.7 2.9 %collective-permute-start.14 = (f32[64,2048]{1,0:T(8,128)}, f32[64,2048]{1,0:T(8,128)}, u32[]{:S(2)}, u32[]{:S(2)}) collective-permute-start(f32[64,2048]{1,0:T(8,128)} %shard_map.97), channel_id=1, source_target_pairs={{0,5},{1,4},{2,7},{3,6},{4,1},{5,0},{6,3},{7,2},{8,13},{9,12},{10,... | collective-permute-start | bytes 1572872 | tf_op jit(solution)/shard_map/ppermute | solution.py:29
  57.5 2.4 %shard_map.93 = (f32[160,2048]{1,0:T(8,128)}, f32[8,128]{1,0:T(8,128)}) custom-call(f32[64,2048]{1,0:T(8,128)} %get-tuple-element.71.refs_0_, f32[64,2048]{1,0:T(8,128)} %copy-done.2, f32[32,2048]{1,0:T(8,128)} %copy-done.3, f32[8,128]{1,0:T(8,128)} %copy-done.4), custom_call_target="tpu_custom_call" | custom-call | bytes 2621440 | tf_op jit(solution)/shard_map/pallas_call | solution.py:285
  61.4 27.2 %shard_map.94 = (f32[512,512]{1,0:T(8,128)}, f32[8,128]{1,0:T(8,128)}) custom-call(f32[512,512]{1,0:T(8,128)} %get-tuple-element.69.gram_a, f32[512,512]{1,0:T(8,128)} %collective-permute-done.9.gram_b, f32[1024,512]{1,0:T(8,128)} %collective-permute-done.10.refs_0_, f32[8,128]{1,0:T(8,128)} %get-tuple-element.73.refs_1_), custom_call_target="tpu_custom_call" | custom-call | flops 30000001024 | bytes 3145728 | tf_op jit(solution)/shard_map/pallas_call | solution.py:236
  88.6 2.0 %collective-permute-done.14.refs_4_ = f32[64,2048]{1,0:T(8,128)} collective-permute-done((f32[64,2048]{1,0:T(8,128)}, f32[64,2048]{1,0:T(8,128)}, u32[]{:S(2)}, u32[]{:S(2)}) %collective-permute-start.14) | collective-permute-done | bytes 524320 | tf_op jit(solution)/shard_map/ppermute | solution.py:29
  90.7 2.4 %shard_map.99 = (f32[160,2048]{1,0:T(8,128)}, f32[8,128]{1,0:T(8,128)}) custom-call(f32[32,2048]{1,0:T(8,128)} %get-tuple-element.80.refs_0_, f32[64,2048]{1,0:T(8,128)} %get-tuple-element.81.refs_1_, f32[64,2048]{1,0:T(8,128)} %get-tuple-element.82.refs_2_), custom_call_target="tpu_custom_call" | custom-call | bytes 2621440 | tf_op jit(solution)/shard_map/pallas_call | solution.py:285
  95.6 2.1 %collective-permute-start.18 = (f32[64,2048]{1,0:T(8,128)}, f32[64,2048]{1,0:T(8,128)}, u32[]{:S(2)}, u32[]{:S(2)}) collective-permute-start(f32[64,2048]{1,0:T(8,128)} %shard_map.102), channel_id=1, source_target_pairs={{0,6},{1,7},{2,4},{3,5},{4,2},{5,3},{6,0},{7,1},{8,14},{9,15},{10,... | collective-permute-start | bytes 1572872 | tf_op jit(solution)/shard_map/ppermute | solution.py:29
  98.4 15.8 %shard_map.100 = (bf16[512,2048]{1,0:T(8,128)(2,1)}, bf16[512,2048]{1,0:T(8,128)(2,1)}, f32[512,512]{1,0:T(8,128)}, bf16[512,512]{1,0:T(8,128)(2,1)}, bf16[512,512]{1,0:T(8,128)(2,1)}) custom-call(f32[512,512]{1,0:T(8,128)} %get-tuple-element.74.refs_0_, f32[2,2,4,64,512]{4,3,2,1,0:T(8,128)} %bitcast.5.refs_1_, f32[2,2,4,64,512]{4,3,2,1,0:T(8,128)} %bitcast.6.refs_2_, ...), custom_call_target="tpu_custom_call" | custom-call | flops 4294967296 | bytes 6291456 | tf_op jit(solution)/shard_map/pallas_call | solution.py:377
  114.2 8.0 %collective-permute-done.17.refs_5_ = f32[64,2048]{1,0:T(8,128)S(1)} collective-permute-done((f32[64,2048]{1,0:T(8,128)}, f32[64,2048]{1,0:T(8,128)S(1)}, u32[]{:S(2)}, u32[]{:S(2)}) %collective-permute-start.17) | collective-permute-done | bytes 524320 | tf_op jit(solution)/shard_map/ppermute | solution.py:29
  122.2 1.9 %collective-permute-done.16.refs_4_ = f32[160,2048]{1,0:T(8,128)} collective-permute-done((f32[160,2048]{1,0:T(8,128)}, f32[160,2048]{1,0:T(8,128)}, u32[]{:S(2)}, u32[]{:S(2)}) %collective-permute-start.16) | collective-permute-done | bytes 1310752 | tf_op jit(solution)/shard_map/ppermute | solution.py:31
  126.9 2.0 %collective-permute-start.24 = (f32[64,2048]{1,0:T(8,128)}, f32[64,2048]{1,0:T(8,128)S(1)}, u32[]{:S(2)}, u32[]{:S(2)}) collective-permute-start(f32[64,2048]{1,0:T(8,128)} %shard_map.105), channel_id=1, source_target_pairs={{0,7},{1,6},{2,5},{3,4},{4,3},{5,2},{6,1},{7,0},{8,15},{9,14},{10,... | collective-permute-start | bytes 1572872 | tf_op jit(solution)/shard_map/ppermute | solution.py:29
  129.5 1.7 collective-permute-done.21.refs_7_
  131.3 19.6 %shard_map.104 = (f32[512,2048]{1,0:T(8,128)}, f32[512,2048]{1,0:T(8,128)}) custom-call(bf16[512,2048]{1,0:T(8,128)(2,1)} %get-tuple-element.84.q_high, bf16[512,2048]{1,0:T(8,128)(2,1)} %get-tuple-element.85.q_low, s32[1,2048]{1,0:T(1,128)} %sub.45.targets, f32[160,2048]{1,0:T(8,128)} %get-tuple-element.92.refs_0_, f32[160,2048]{1,0:T(8,128)} %get-tuple-element.93.refs_1_, ...), custom_call_target="tpu_custom_call" | custom-call | flops 6710886400 | bytes 4718592 | tf_op jit(solution)/shard_map/pallas_call | solution.py:456
  156.8 8.0 %shard_map.107 = (f32[512,2048]{1,0:T(8,128)}, f32[512,2048]{1,0:T(8,128)}) custom-call(bf16[512,2048]{1,0:T(8,128)(2,1)} %get-tuple-element.84.q_high, bf16[512,2048]{1,0:T(8,128)(2,1)} %get-tuple-element.85.q_low, s32[1,2048]{1,0:T(1,128)} %sub.45.targets, f32[512,2048]{1,0:T(8,128)} %get-tuple-element.98.refs_5_.factor_in, ...), custom_call_target="tpu_custom_call" | custom-call | flops 1342177280 | bytes 4718592 | tf_op jit(solution)/shard_map/pallas_call | solution.py:456
  164.8 2.2 %collective-permute-done.29.refs_1_ = f32[64,2048]{1,0:T(8,128)} collective-permute-done((f32[64,2048]{1,0:T(8,128)}, f32[64,2048]{1,0:T(8,128)}, u32[]{:S(2)}, u32[]{:S(2)}) %collective-permute-start.29) | collective-permute-done | bytes 524320 | tf_op jit(solution)/shard_map/ppermute | solution.py:31
  167.5 2.3 %collective-permute-done.30.refs_6_ = f32[64,2048]{1,0:T(8,128)S(1)} collective-permute-done((f32[64,2048]{1,0:T(8,128)}, f32[64,2048]{1,0:T(8,128)S(1)}, u32[]{:S(2)}, u32[]{:S(2)}) %collective-permute-start.30) | collective-permute-done | bytes 524320 | tf_op jit(solution)/shard_map/ppermute | solution.py:31
  170.6 14.9 %shard_map.109 = (f32[512,2048]{1,0:T(8,128)}, f32[512,2048]{1,0:T(8,128)}) custom-call(bf16[512,2048]{1,0:T(8,128)(2,1)} %get-tuple-element.84.q_high, bf16[512,2048]{1,0:T(8,128)(2,1)} %get-tuple-element.85.q_low, s32[1,2048]{1,0:T(1,128)} %sub.45.targets, f32[512,2048]{1,0:T(8,128)} %get-tuple-element.106.refs_2_.factor_in, ...), custom_call_target="tpu_custom_call" | custom-call | flops 4294967296 | bytes 5242880 | tf_op jit(solution)/shard_map/pallas_call | solution.py:456
  (132 shorter events, 30.5 us)
Async XLA Ops:
  2.5 11.9 %collective-permute-start.2 = (f32[64,512]{1,0:T(8,128)S(1)}, f32[64,512]{1,0:T(8,128)S(1)}, u32[]{:S(2)}, u32[]{:S(2)}) collective-permute-start(f32[64,512]{1,0:T(8,128)S(1)} %slice_select_fusion.refs_0_), channel_id=1, source_target_pairs={{0,6},{1,7},{2,4},{3,5},{4,2},{5,3},{6,0},{7,1},{8,14},{9,15},{10,... | collective-permute-start | bytes 393224 | tf_op jit(solution)/shard_map/ppermute | solution.py:29
  7.6 7.4 %collective-permute-start.1 = (f32[64,512]{1,0:T(8,128)S(1)}, f32[64,512]{1,0:T(8,128)S(1)}, u32[]{:S(2)}, u32[]{:S(2)}) collective-permute-start(f32[64,512]{1,0:T(8,128)S(1)} %slice_select_fusion.refs_0_), channel_id=1, source_target_pairs={{0,2},{1,3},{2,0},{3,1},{4,6},{5,7},{6,4},{7,5},{8,10},{9,11},{10,... | collective-permute-start | bytes 393224 | tf_op jit(solution)/shard_map/ppermute | solution.py:29
  7.6 11.1 %collective-permute-start = (f32[64,512]{1,0:T(8,128)S(1)}, f32[64,512]{1,0:T(8,128)S(1)}, u32[]{:S(2)}, u32[]{:S(2)}) collective-permute-start(f32[64,512]{1,0:T(8,128)S(1)} %slice_select_fusion.refs_0_), channel_id=1, source_target_pairs={{0,4},{1,5},{2,6},{3,7},{4,0},{5,1},{6,2},{7,3},{8,12},{9,13},{10,... | collective-permute-start | bytes 393224 | tf_op jit(solution)/shard_map/ppermute | solution.py:29
  20.1 10.3 %collective-permute-start.5 = (f32[256,256]{1,0:T(8,128)}, f32[256,256]{1,0:T(8,128)}, u32[]{:S(2)}, u32[]{:S(2)}) collective-permute-start(f32[256,256]{1,0:T(8,128)} %get-tuple-element.64.refs_0_), channel_id=1, source_target_pairs={{0,1},{1,0},{2,3},{3,2},{4,5},{5,4},{6,7},{7,6},{8,9},{9,8},{10,11... | collective-permute-start | bytes 786440 | tf_op jit(solution)/shard_map/ppermute | solution.py:29
  21.6 10.5 %collective-permute-start.3 = (f32[256,256]{1,0:T(8,128)S(1)}, f32[256,256]{1,0:T(8,128)}, u32[]{:S(2)}, u32[]{:S(2)}) collective-permute-start(f32[256,256]{1,0:T(8,128)S(1)} %get-tuple-element.60.refs_0_), channel_id=1, source_target_pairs={{0,16},{8,24},{16,0},{24,8},{1,17},{9,25},{17,1},{25,9},{2,18},{10... | collective-permute-start | bytes 786440 | tf_op jit(solution)/shard_map/ppermute | solution.py:31
  23.1 14.8 %collective-permute-start.7 = (f32[64,2048]{1,0:T(8,128)}, f32[64,2048]{1,0:T(8,128)S(1)}, u32[]{:S(2)}, u32[]{:S(2)}) collective-permute-start(f32[64,2048]{1,0:T(8,128)} %shard_map.90), channel_id=1, source_target_pairs={{0,2},{1,3},{2,0},{3,1},{4,6},{5,7},{6,4},{7,5},{8,10},{9,11},{10,... | collective-permute-start | bytes 1572872 | tf_op jit(solution)/shard_map/ppermute | solution.py:29
  31.4 16.4 %collective-permute-start.6 = (f32[512,256]{1,0:T(8,128)S(1)}, f32[512,256]{1,0:T(8,128)S(1)}, u32[]{:S(2)}, u32[]{:S(2)}) collective-permute-start(f32[512,256]{1,0:T(8,128)S(1)} %get-tuple-element.65.b_mine), channel_id=1, source_target_pairs={{0,16},{8,24},{16,0},{24,8},{1,17},{9,25},{17,1},{25,9},{2,18},{10... | collective-permute-start | bytes 1572872 | tf_op jit(solution)/shard_map/ppermute | solution.py:31
  34.3 13.6 %collective-permute-start.4 = (f32[512,256]{1,0:T(8,128)S(1)}, f32[512,256]{1,0:T(8,128)S(1)}, u32[]{:S(2)}, u32[]{:S(2)}) collective-permute-start(f32[512,256]{1,0:T(8,128)S(1)} %get-tuple-element.63.a_mine), channel_id=1, source_target_pairs={{0,1},{1,0},{2,3},{3,2},{4,5},{5,4},{6,7},{7,6},{8,9},{9,8},{10,11... | collective-permute-start | bytes 1572872 | tf_op jit(solution)/shard_map/ppermute | solution.py:29
  34.8 13.1 %collective-permute-start.8 = (f32[32,2048]{1,0:T(8,128)}, f32[32,2048]{1,0:T(8,128)S(1)}, u32[]{:S(2)}, u32[]{:S(2)}) collective-permute-start(f32[32,2048]{1,0:T(8,128)} %shard_map.91), channel_id=1, source_target_pairs={{0,4},{1,5},{2,6},{3,7},{4,0},{5,1},{6,2},{7,3},{8,12},{9,13},{10,... | collective-permute-start | bytes 786440 | tf_op jit(solution)/shard_map/ppermute | solution.py:29
  52.5 8.9 %collective-permute-start.10 = (f32[1024,512]{1,0:T(8,128)}, f32[1024,512]{1,0:T(8,128)}, u32[]{:S(2)}, u32[]{:S(2)}) collective-permute-start(f32[1024,512]{1,0:T(8,128)} %get-tuple-element.70), channel_id=1, source_target_pairs={{0,8},{8,0},{16,24},{24,16},{1,9},{9,1},{17,25},{25,17},{2,10},{10... | collective-permute-start | bytes 6291464 | tf_op jit(solution)/shard_map/ppermute | solution.py:31
  52.5 7.5 %collective-permute-start.9 = (f32[512,512]{1,0:T(8,128)}, f32[512,512]{1,0:T(8,128)}, u32[]{:S(2)}, u32[]{:S(2)}) collective-permute-start(f32[512,512]{1,0:T(8,128)} %get-tuple-element.69.gram_a), channel_id=1, source_target_pairs={{0,8},{8,0},{16,24},{24,16},{1,9},{9,1},{17,25},{25,17},{2,10},{10... | collective-permute-start | bytes 3145736 | tf_op jit(solution)/shard_map/ppermute | solution.py:31
  53.1 35.5 %collective-permute-start.13 = (f32[32,2048]{1,0:T(8,128)}, f32[32,2048]{1,0:T(8,128)S(1)}, u32[]{:S(2)}, u32[]{:S(2)}) collective-permute-start(f32[32,2048]{1,0:T(8,128)} %shard_map.96), channel_id=1, source_target_pairs={{0,4},{1,5},{2,6},{3,7},{4,0},{5,1},{6,2},{7,3},{8,12},{9,13},{10,... | collective-permute-start | bytes 786440 | tf_op jit(solution)/shard_map/ppermute | solution.py:29
  53.2 35.4 %collective-permute-start.12 = (f32[64,2048]{1,0:T(8,128)}, f32[64,2048]{1,0:T(8,128)S(1)}, u32[]{:S(2)}, u32[]{:S(2)}) collective-permute-start(f32[64,2048]{1,0:T(8,128)} %shard_map.95), channel_id=1, source_target_pairs={{0,1},{1,0},{2,3},{3,2},{4,5},{5,4},{6,7},{7,6},{8,9},{9,8},{10,11... | collective-permute-start | bytes 1572872 | tf_op jit(solution)/shard_map/ppermute | solution.py:29
  54.7 36.0 %collective-permute-start.14 = (f32[64,2048]{1,0:T(8,128)}, f32[64,2048]{1,0:T(8,128)}, u32[]{:S(2)}, u32[]{:S(2)}) collective-permute-start(f32[64,2048]{1,0:T(8,128)} %shard_map.97), channel_id=1, source_target_pairs={{0,5},{1,4},{2,7},{3,6},{4,1},{5,0},{6,3},{7,2},{8,13},{9,12},{10,... | collective-permute-start | bytes 1572872 | tf_op jit(solution)/shard_map/ppermute | solution.py:29
  60.0 30.7 %collective-permute-start.11 = (f32[160,2048]{1,0:T(8,128)}, f32[160,2048]{1,0:T(8,128)}, u32[]{:S(2)}, u32[]{:S(2)}) collective-permute-start(f32[160,2048]{1,0:T(8,128)} %get-tuple-element.75.refs_0_), channel_id=1, source_target_pairs={{0,16},{8,24},{16,0},{24,8},{1,17},{9,25},{17,1},{25,9},{2,18},{10... | collective-permute-start | bytes 3932168 | tf_op jit(solution)/shard_map/ppermute | solution.py:31
  93.1 31.0 %collective-permute-start.16 = (f32[160,2048]{1,0:T(8,128)}, f32[160,2048]{1,0:T(8,128)}, u32[]{:S(2)}, u32[]{:S(2)}) collective-permute-start(f32[160,2048]{1,0:T(8,128)} %get-tuple-element.88.refs_3_), channel_id=1, source_target_pairs={{0,16},{8,24},{16,0},{24,8},{1,17},{9,25},{17,1},{25,9},{2,18},{10... | collective-permute-start | bytes 3932168 | tf_op jit(solution)/shard_map/ppermute | solution.py:31
  94.6 29.5 %collective-permute-start.15 = (f32[160,2048]{1,0:T(8,128)}, f32[160,2048]{1,0:T(8,128)}, u32[]{:S(2)}, u32[]{:S(2)}) collective-permute-start(f32[160,2048]{1,0:T(8,128)} %get-tuple-element.86.refs_0_), channel_id=1, source_target_pairs={{0,8},{8,0},{16,24},{24,16},{1,9},{9,1},{17,25},{25,17},{2,10},{10... | collective-permute-start | bytes 3932168 | tf_op jit(solution)/shard_map/ppermute | solution.py:31
  95.5 26.7 %collective-permute-start.17 = (f32[64,2048]{1,0:T(8,128)}, f32[64,2048]{1,0:T(8,128)S(1)}, u32[]{:S(2)}, u32[]{:S(2)}) collective-permute-start(f32[64,2048]{1,0:T(8,128)} %shard_map.101), channel_id=1, source_target_pairs={{0,3},{1,2},{2,1},{3,0},{4,7},{5,6},{6,5},{7,4},{8,11},{9,10},{10,... | collective-permute-start | bytes 1572872 | tf_op jit(solution)/shard_map/ppermute | solution.py:29
  95.6 26.6 %collective-permute-start.18 = (f32[64,2048]{1,0:T(8,128)}, f32[64,2048]{1,0:T(8,128)}, u32[]{:S(2)}, u32[]{:S(2)}) collective-permute-start(f32[64,2048]{1,0:T(8,128)} %shard_map.102), channel_id=1, source_target_pairs={{0,6},{1,7},{2,4},{3,5},{4,2},{5,3},{6,0},{7,1},{8,14},{9,15},{10,... | collective-permute-start | bytes 1572872 | tf_op jit(solution)/shard_map/ppermute | solution.py:29
  124.7 6.6 %collective-permute-start.21 = (f32[160,2048]{1,0:T(8,128)}, f32[160,2048]{1,0:T(8,128)}, u32[]{:S(2)}, u32[]{:S(2)}) collective-permute-start(f32[160,2048]{1,0:T(8,128)} %get-tuple-element.96.refs_5_), channel_id=1, source_target_pairs={{0,8},{8,0},{16,24},{24,16},{1,9},{9,1},{17,25},{25,17},{2,10},{10... | collective-permute-start | bytes 3932168 | tf_op jit(solution)/shard_map/ppermute | solution.py:31
  125.4 25.8 %collective-permute-start.22 = (f32[64,2048]{1,0:T(8,128)}, f32[64,2048]{1,0:T(8,128)}, u32[]{:S(2)}, u32[]{:S(2)}) collective-permute-start(f32[64,2048]{1,0:T(8,128)} %get-tuple-element.97.refs_8_.refs_1_.refs_0_), channel_id=1, source_target_pairs={{0,16},{8,24},{16,0},{24,8},{1,17},{9,25},{17,1},{25,9},{2,18},{10... | collective-permute-start | bytes 1572872 | tf_op jit(solution)/shard_map/ppermute | solution.py:31
  126.9 24.0 %collective-permute-start.24 = (f32[64,2048]{1,0:T(8,128)}, f32[64,2048]{1,0:T(8,128)S(1)}, u32[]{:S(2)}, u32[]{:S(2)}) collective-permute-start(f32[64,2048]{1,0:T(8,128)} %shard_map.105), channel_id=1, source_target_pairs={{0,7},{1,6},{2,5},{3,4},{4,3},{5,2},{6,1},{7,0},{8,15},{9,14},{10,... | collective-permute-start | bytes 1572872 | tf_op jit(solution)/shard_map/ppermute | solution.py:29
  128.9 22.3 %collective-permute-start.23 = (f32[64,2048]{1,0:T(8,128)}, f32[64,2048]{1,0:T(8,128)}, u32[]{:S(2)}, u32[]{:S(2)}) collective-permute-start(f32[64,2048]{1,0:T(8,128)} %get-tuple-element.100.refs_2_), channel_id=1, source_target_pairs={{0,16},{8,24},{16,0},{24,8},{1,17},{9,25},{17,1},{25,9},{2,18},{10... | collective-permute-start | bytes 1572872 | tf_op jit(solution)/shard_map/ppermute | solution.py:31
  152.7 14.3 %collective-permute-start.29 = (f32[64,2048]{1,0:T(8,128)}, f32[64,2048]{1,0:T(8,128)}, u32[]{:S(2)}, u32[]{:S(2)}) collective-permute-start(f32[64,2048]{1,0:T(8,128)} %get-tuple-element.110.refs_0_), channel_id=1, source_target_pairs={{0,16},{8,24},{16,0},{24,8},{1,17},{9,25},{17,1},{25,9},{2,18},{10... | collective-permute-start | bytes 1572872 | tf_op jit(solution)/shard_map/ppermute | solution.py:31
  (29 other events, 121.5 us)
